TPU v7x, 512 devices: a whole 4x8x8 slice. The times are simulated.
512 devices in a mesh: blk: 256 (over y, x_lo, z, core), dp: 2 (over x_hi).
Axes of the slice: x: 4 (x_hi: 2, x_lo: 2; x = x_hi * 2 + x_lo), y: 8, z: 8, core: 2. Of those that a mesh axis runs over, the one named last changes fastest.
Arguments:
- teacher_rows: bfloat16 [8192, 256], P('blk', 'dp'), may hold values from -6 to 6
- teacher_gate: bfloat16 [26624, 8192], P('blk', 'dp'), may hold values from -0.0625 to 0.0625
- teacher_up: bfloat16 [26624, 8192], P('blk', 'dp'), may hold values from -0.0625 to 0.0625
- teacher_down: bfloat16 [26624, 8192], P('blk', 'dp'), may hold values from -0.15625 to 0.15625
- student_rows: bfloat16 [8192, 256], P('blk', 'dp'), may hold values from -6 to 6
- projector: bfloat16 [8192, 8192], P('blk'), may hold values from -0.0625 to 0.0625
Outputs:
- teacher_hidden: bfloat16 [26624, 256], P('blk', 'dp')
- residual_error: bfloat16 [8192, 256], P('blk', 'dp')
- grad_projector: bfloat16 [8192, 8192], P('blk')
All inputs are finite; a program needn't handle non-finite values.
Results may differ from a plain program's by a relative error of at most 0.012.
Values may be sent and summed in bfloat16 or wider, within the bound.
No kernel may reach another device: no remote copies, remote signals or barrier semaphores. Data moves between devices by JAX's collectives and lax.ppermute only.
A program may use at most 64 MiB of HBM per device.

v0:
```python
import jax
import jax.numpy as jnp
from jax import lax
from jax.sharding import PartitionSpec as P


def shards(teacher_rows, teacher_gate, teacher_up, teacher_down, student_rows, projector):
    gate_full, up_full, down_full = (
        lax.all_gather(teacher_gate, "dp", axis=1, tiled=True),
        lax.all_gather(teacher_up, "dp", axis=1, tiled=True),
        lax.all_gather(teacher_down, "dp", axis=1, tiled=True),
    )
    piece = lax.all_gather(teacher_rows, "blk", axis=0, tiled=True)
    preact = jnp.dot(gate_full, piece, preferred_element_type=jnp.float32)
    uppre = jnp.dot(up_full, piece, preferred_element_type=jnp.float32)
    teacher_hidden = (jax.nn.silu(preact) * uppre).astype(jnp.bfloat16)
    columns = down_full
    teacher_out = lax.psum_scatter(
        lax.dot_general(
            columns, teacher_hidden, (((0,), (0,)), ((), ())), preferred_element_type=jnp.float32
        ),
        "blk",
        scatter_dimension=0,
        tiled=True,
    )
    columns = projector
    student_out = jnp.dot(
        columns,
        lax.all_gather(student_rows, "blk", axis=0, tiled=True),
        preferred_element_type=jnp.float32,
    )
    residual_error = (student_out - teacher_out).astype(jnp.bfloat16)
    grad_local = lax.dot_general(
        residual_error,
        lax.all_gather(student_rows, "blk", axis=0, tiled=True),
        (((1,), (1,)), ((), ())),
        preferred_element_type=jnp.float32,
    )
    grad_projector = lax.psum(grad_local.astype(jnp.bfloat16), "dp")
    return (teacher_hidden, residual_error, grad_projector)


def solution(mesh):
    return jax.shard_map(
        shards,
        mesh=mesh,
        in_specs=(
            P("blk", "dp"),
            P("blk", "dp"),
            P("blk", "dp"),
            P("blk", "dp"),
            P("blk", "dp"),
            P("blk", None),
        ),
        out_specs=(P("blk", "dp"), P("blk", "dp"), P("blk", None)),
        check_vma=False,
    )
```

profile of v0, /device:TPU:1, one launch (start us, length us, event | category | flops | bytes accessed | tf_op | source)
XLA Modules:
  0.0 2139.2 jit_solution(10643168854409800376)
XLA Ops:
  7.2 0.0 copy-start
  7.2 0.0 all-gather.6.cloned.1.call-start
  7.2 0.7 all-gather.6.cloned.1.call-update
  7.9 0.0 all-gather.8.cloned.1.call-start
  8.0 0.7 all-gather.8.cloned.1.call-update
  8.7 0.0 all-gather.10.cloned.1.call-start
  8.7 0.7 all-gather.10.cloned.1.call-update
  9.4 0.0 all-gather.14.cloned.1.call-start
  9.4 0.5 all-gather.14.cloned.1.call-update
  10.0 0.0 all-gather.12.cloned.1.call-start
  10.0 0.5 all-gather.12.cloned.1.call-update
  10.6 0.0 reduce-scatter.2.cloned.1.call-start
  10.6 43.1 %all-gather.6.cloned.1.call-done = bf16[104,8192]{1,0:T(8,128)(2,1)} async-done(((bf16[104,4096]{1,0:T(8,128)(2,1)}), bf16[104,8192]{1,0:T(8,128)(2,1)}) %all-gather.6.cloned.1.call-update) | async-done | bytes 1703952 | tf_op jit(solution)/shard_map/all_gather | solution.py:9
  53.7 411.6 %all-gather.8.cloned.1.call-done = bf16[8192,128]{1,0:T(8,128)(2,1)} async-done(((bf16[32,128]{1,0:T(8,128)(2,1)}), bf16[8192,128]{1,0:T(8,128)(2,1)}) %all-gather.8.cloned.1.call-update) | async-done | bytes 2097168 | tf_op jit(solution)/shard_map/all_gather | solution.py:13
  465.3 2.9 fusion.2
  468.2 38.6 %all-gather.10.cloned.1.call-done = bf16[104,8192]{1,0:T(8,128)(2,1)} async-done(((bf16[104,4096]{1,0:T(8,128)(2,1)}), bf16[104,8192]{1,0:T(8,128)(2,1)}) %all-gather.10.cloned.1.call-update) | async-done | bytes 1703952 | tf_op jit(solution)/shard_map/all_gather | solution.py:10
  506.8 0.0 copy-done.2
  506.8 2.1 fusion
  508.9 0.0 copy-start.3
  508.9 37.5 %all-gather.14.cloned.1.call-done = bf16[104,8192]{1,0:T(8,128)(2,1)} async-done(((bf16[104,4096]{1,0:T(8,128)(2,1)}), bf16[104,8192]{1,0:T(8,128)(2,1)}) %all-gather.14.cloned.1.call-update) | async-done | bytes 1703952 | tf_op jit(solution)/shard_map/all_gather | solution.py:11
  546.3 4.4 convolution_bitcast_fusion
  550.7 0.0 reduce-scatter.2.cloned.1.call-update
  550.7 0.0 all-reduce.2.cloned.1.call-start
  550.8 407.1 %all-gather.12.cloned.1.call-done = bf16[8192,128]{1,0:T(8,128)(2,1)} async-done(((bf16[32,128]{1,0:T(8,128)(2,1)}), bf16[8192,128]{1,0:T(8,128)(2,1)}) %all-gather.12.cloned.1.call-update) | async-done | bytes 2097168 | tf_op jit(solution)/shard_map/all_gather | solution.py:29
  957.8 1122.4 %reduce-scatter.2.cloned.1.call-done = f32[32,128]{1,0:T(8,128)} async-done(((f32[8192,128]{1,0:T(8,128)}), f32[32,128]{1,0:T(8,128)}) %reduce-scatter.2.cloned.1.call-update) | async-done | bytes 16400 | tf_op jit(solution)/shard_map/reduce_scatter | solution.py:18
  2080.2 2.0 fusion.1
  2082.3 0.0 copy-done.1
  2082.3 0.0 copy-start.4
  2082.3 1.6 convolution_convert_fusion
  2083.9 0.0 all-reduce.2.cloned.1.call-update
  2083.9 46.5 %all-reduce.2.cloned.1.call-done = bf16[32,8192]{1,0:T(8,128)(2,1)} async-done(((bf16[32,8192]{1,0:T(8,128)(2,1)}), bf16[32,8192]{1,0:T(8,128)(2,1)}) %all-reduce.2.cloned.1.call-update) | async-done | bytes 524304 | tf_op jit(solution)/shard_map/psum | solution.py:39
  2130.4 1.9 copy.12
  (5 shorter events, 0.0 us)
Async XLA Ops:
  7.2 2073.1 %copy-start = (bf16[32,8192]{1,0:T(8,128)(2,1)S(1)}, bf16[32,8192]{1,0:T(8,128)(2,1)}, u32[]{:S(2)}) copy-start(bf16[32,8192]{1,0:T(8,128)(2,1)} %param.11) | copy-start | bytes 1572868
  7.2 46.5 %all-gather.6.cloned.1.call-start = ((), (), s32[]{:S(2)}) async-start(), calls=%async_computation.1 | async-start | bytes 2555904 | tf_op jit(solution)/shard_map/all_gather | solution.py:9
  7.9 457.4 %all-gather.8.cloned.1.call-start = ((), (), s32[]{:S(2)}) async-start(), calls=%async_computation.2 | async-start | bytes 2105344 | tf_op jit(solution)/shard_map/all_gather | solution.py:13
  8.7 498.1 %all-gather.10.cloned.1.call-start = ((), (), s32[]{:S(2)}) async-start(), calls=%async_computation.3 | async-start | bytes 2555904 | tf_op jit(solution)/shard_map/all_gather | solution.py:10
  9.4 536.9 %all-gather.14.cloned.1.call-start = ((), (), s32[]{:S(2)}) async-start(), calls=%async_computation.5 | async-start | bytes 2555904 | tf_op jit(solution)/shard_map/all_gather | solution.py:11
  10.0 947.8 %all-gather.12.cloned.1.call-start = ((), (), s32[]{:S(2)}) async-start(), calls=%async_computation.4 | async-start | bytes 2105344 | tf_op jit(solution)/shard_map/all_gather | solution.py:29
  10.6 2069.7 %reduce-scatter.2.cloned.1.call-start = ((), (), s32[]{:S(2)}) async-start(), calls=%async_computation.6 | async-start | bytes 4210688 | tf_op jit(solution)/shard_map/reduce_scatter | solution.py:18
  465.3 41.5 %copy-start.2 = (bf16[8192,128]{1,0:T(8,128)(2,1)S(1)}, bf16[8192,128]{1,0:T(8,128)(2,1)}, u32[]{:S(2)}) copy-start(bf16[8192,128]{1,0:T(8,128)(2,1)} %all-gather.8.cloned.1.call-done) | copy-start | bytes 6291460
  508.9 41.8 %copy-start.3 = (bf16[104,128]{1,0:T(8,128)(2,1)}, bf16[104,128]{1,0:T(8,128)(2,1)S(1)}, u32[]{:S(2)}) copy-start(bf16[104,128]{1,0:T(8,128)(2,1)S(1)} %fusion) | copy-start | bytes 79876
  550.7 1579.7 %all-reduce.2.cloned.1.call-start = ((), (), s32[]{:S(2)}) async-start(), calls=%async_computation.7 | async-start | bytes 1048576 | tf_op jit(solution)/shard_map/psum | solution.py:39
  957.8 1124.5 %copy-start.1 = (bf16[8192,128]{1,0:T(8,128)(2,1)S(1)}, bf16[8192,128]{1,0:T(8,128)(2,1)}, u32[]{:S(2)}) copy-start(bf16[8192,128]{1,0:T(8,128)(2,1)} %all-gather.12.cloned.1.call-done) | copy-start | bytes 6291460
  2082.3 50.0 %copy-start.4 = (bf16[32,128]{1,0:T(8,128)(2,1)}, bf16[32,128]{1,0:T(8,128)(2,1)S(1)}, u32[]{:S(2)}) copy-start(bf16[32,128]{1,0:T(8,128)(2,1)S(1)} %fusion.1) | copy-start | bytes 24580
Sparse Core Ops, SparseCore 0:
  10.1 43.5 all-gather.5
  55.9 409.4 all-gather.7
  467.4 39.3 all-gather.9
  508.7 37.5 all-gather.13
  548.4 409.4 all-gather.11
  960.5 1119.7 reduce-scatter.1
  2084.1 46.3 all-reduce.1
where the time goes:
time: 2140 us
  waiting for transfers between devices  2110 us (99%)
    reduce_scatter x1, waiting for transfers between devices, shards(): lax.psum_scatter(lax.dot_general(columns, teacher_hidden, (((0,), (0,)),...  1120 us
    all_gather x1, waiting for transfers between devices, shards(): piece = lax.all_gather(teacher_rows, 'blk', axis=0, tiled=True)  412 us
    all_gather x1, waiting for transfers between devices, shards(): lax.all_gather(student_rows, 'blk', axis=0, tiled=True)  407 us
    psum x1, waiting for transfers between devices, shards(): grad_projector = lax.psum(grad_local.astype(jnp.bfloat16), 'dp')  46.5 us
    all_gather x1, waiting for transfers between devices, shards(): lax.all_gather(teacher_gate, 'dp', axis=1, tiled=True)  43.1 us
  transfers between devices with their start and end apart: 7, of which 7 were waited for; matrix products, arithmetic and copies ran while one was open for 0% of the time, Pallas kernels for 0%

commit v1 on v0

v1 whole, which is shorter than its diff:
```python
import functools

import jax
import jax.numpy as jnp
from jax import lax
from jax.experimental import pallas as pl
from jax.experimental.pallas import tpu as pltpu
from jax.sharding import Mesh, PartitionSpec as P

CHIPS = ("y", "x", "z")
SWAP = [(0, 1), (1, 0)]
F32, BF16 = jnp.float32, jnp.bfloat16
PARAMS = pltpu.CompilerParams(vmem_limit_bytes=24 << 20)


def cost(flops, size):
    return pl.CostEstimate(flops=flops, bytes_accessed=size, transcendentals=0)


def zip_cores(core, own, other):
    count, rows, tokens = own.shape
    even = jnp.where(core == 0, own, other)
    odd = jnp.where(core == 0, other, own)
    return jnp.stack([even, odd], axis=1).reshape(count * 2 * rows, tokens)


def copies_kernel(rows_ref, _, out_ref):
    out_ref[...] = jnp.broadcast_to(rows_ref[...][None], out_ref.shape)


def copies(rows, after, count):
    return pl.pallas_call(
        copies_kernel,
        in_specs=[pl.BlockSpec(memory_space=pltpu.VMEM), pl.BlockSpec(memory_space=pl.ANY)],
        out_shape=jax.ShapeDtypeStruct((count, *rows.shape), rows.dtype),
        compiler_params=PARAMS,
        cost_estimate=cost(0, count * rows.size * 2),
        name="copies",
    )(rows, after)


def up_kernel(place_ref, own_ref, other_ref, gate_ref, up_ref, keep_ref, send_ref, acc_ref):
    step, last = pl.program_id(0), pl.num_programs(0) - 1
    core, half = place_ref[0], place_ref[1]

    @pl.when(step == 0)
    def _():
        acc_ref[...] = jnp.zeros_like(acc_ref)

    tokens = own_ref.shape[-1]
    rows = jnp.concatenate(
        [zip_cores(core, own_ref[t], other_ref[t]) for t in range(2)], axis=1
    )
    for i, ref in enumerate((gate_ref, up_ref)):
        acc_ref[i] += jnp.dot(ref[...], rows, preferred_element_type=F32)

    @pl.when(step == last)
    def _():
        for i in range(2):
            low, high = acc_ref[i, :, :tokens], acc_ref[i, :, tokens:]
            keep_ref[i] = jnp.where(half == 0, low, high)
            send_ref[i] = jnp.where(half == 0, high, low).astype(BF16)


def up_part(place, own, other, gate, up, steps=4):
    hidden, width = gate.shape
    rows, tokens = own.shape[-2:]
    per = width // (2 * rows * steps)
    own, other = (a.reshape(2, -1, rows, tokens) for a in (own, other))
    block = pl.BlockSpec((2, per, rows, tokens), lambda k, _: (0, k, 0, 0))
    weight = pl.BlockSpec((hidden, width // steps), lambda k, _: (0, k))
    whole = pl.BlockSpec((2, hidden, tokens), lambda k, _: (0, 0, 0))
    return pl.pallas_call(
        up_kernel,
        grid_spec=pltpu.PrefetchScalarGridSpec(
            num_scalar_prefetch=1,
            grid=(steps,),
            in_specs=[block, block, weight, weight],
            out_specs=[whole, whole],
            scratch_shapes=[pltpu.VMEM((2, hidden, 2 * tokens), F32)],
        ),
        out_shape=[
            jax.ShapeDtypeStruct((2, hidden, tokens), F32),
            jax.ShapeDtypeStruct((2, hidden, tokens), BF16),
        ],
        compiler_params=PARAMS,
        cost_estimate=cost(8 * hidden * width * tokens, 4 * hidden * width + 4 * own.size),
        name="gate_up",
    )(place, own, other, gate, up)


def down_kernel(place_ref, keep_ref, got_ref, near_ref, far_ref, hidden_ref, mine_ref, theirs_ref):
    side, step = pl.program_id(0), pl.program_id(1)
    core = place_ref[0]

    @pl.when((side == 0) & (step == 0))
    def _():
        preact, uppre = (keep_ref[i] + got_ref[i].astype(F32) for i in range(2))
        hidden_ref[...] = (preact / (1 + jnp.exp(-preact)) * uppre).astype(BF16)

    def part(ref):
        out = lax.dot_general(
            ref[...], hidden_ref[...], (((0,), (0,)), ((), ())), preferred_element_type=F32
        ).astype(BF16)
        count, rows, tokens = mine_ref.shape[1:]
        out = out.reshape(count, 2, rows, tokens)
        even, odd = out[:, 0], out[:, 1]
        mine_ref[0] = jnp.where(core == 0, even, odd)
        theirs_ref[0] = jnp.where(core == 0, odd, even)

    pl.when(side == 0)(lambda: part(near_ref))
    pl.when(side == 1)(lambda: part(far_ref))


def down_part(place, keep, got, near, far, rows, steps=4):
    hidden, width = near.shape
    tokens = keep.shape[-1]
    count = width // (2 * rows)
    whole = pl.BlockSpec((2, hidden, tokens), lambda s, k, _: (0, 0, 0))
    block = pl.BlockSpec(
        (1, count // steps, rows, tokens), lambda s, k, p: ((s + p[1]) % 2, k, 0, 0)
    )
    out = jax.ShapeDtypeStruct((2, count, rows, tokens), BF16)
    hidden_units, mine, theirs = pl.pallas_call(
        down_kernel,
        grid_spec=pltpu.PrefetchScalarGridSpec(
            num_scalar_prefetch=1,
            grid=(2, steps),
            in_specs=[
                whole,
                whole,
                pl.BlockSpec((hidden, width // steps), lambda s, k, _: (0, jnp.where(s == 0, k, steps - 1))),
                pl.BlockSpec((hidden, width // steps), lambda s, k, _: (0, jnp.where(s == 1, k, 0))),
            ],
            out_specs=[pl.BlockSpec((hidden, tokens), lambda s, k, _: (0, 0)), block, block],
        ),
        out_shape=[jax.ShapeDtypeStruct((hidden, tokens), BF16), out, out],
        compiler_params=PARAMS,
        cost_estimate=cost(4 * hidden * width * tokens, 4 * hidden * width + 8 * width * tokens),
        name="down",
    )(place, keep, got, near, far)
    return hidden_units, *(a.reshape(2 * count, rows, tokens) for a in (mine, theirs))


def student_kernel(place_ref, own_ref, other_ref, projector_ref, all_ref, out_ref):
    rows = zip_cores(place_ref[0], own_ref[...], other_ref[...])
    all_ref[...] = rows
    part = jnp.dot(projector_ref[...], rows, preferred_element_type=F32)

    @pl.when(pl.program_id(0) == 0)
    def _():
        out_ref[...] = part

    @pl.when(pl.program_id(0) != 0)
    def _():
        out_ref[...] += part


def student_part(place, own, other, projector, steps=8):
    count, rows, tokens = own.shape
    mine, width = projector.shape
    block = pl.BlockSpec((count // steps, rows, tokens), lambda k, _: (k, 0, 0))
    return pl.pallas_call(
        student_kernel,
        grid_spec=pltpu.PrefetchScalarGridSpec(
            num_scalar_prefetch=1,
            grid=(steps,),
            in_specs=[block, block, pl.BlockSpec((mine, width // steps), lambda k, _: (0, k))],
            out_specs=[
                pl.BlockSpec((width // steps, tokens), lambda k, _: (k, 0)),
                pl.BlockSpec((mine, tokens), lambda k, _: (0, 0)),
            ],
        ),
        out_shape=[
            jax.ShapeDtypeStruct((width, tokens), BF16),
            jax.ShapeDtypeStruct((mine, tokens), F32),
        ],
        compiler_params=PARAMS,
        cost_estimate=cost(2 * mine * width * tokens, 4 * width * tokens + 2 * mine * width),
        name="student",
    )(place, own, other, projector)


def grad_kernel(terms_ref, student_out_ref, student_ref, residual_ref, grad_ref):
    @pl.when(pl.program_id(0) == 0)
    def _():
        teacher_out = jnp.sum(terms_ref[...].astype(F32), axis=0)
        residual_ref[...] = (student_out_ref[...] - teacher_out).astype(BF16)

    grad_ref[...] = lax.dot_general(
        residual_ref[...], student_ref[...], (((1,), (1,)), ((), ())), preferred_element_type=F32
    ).astype(BF16)


def grad_part(terms, student_out, student_all, steps=4):
    rows, tokens = student_out.shape
    width = student_all.shape[0]
    small = pl.BlockSpec((rows, tokens), lambda k: (0, 0))
    return pl.pallas_call(
        grad_kernel,
        grid=(steps,),
        in_specs=[
            pl.BlockSpec(terms.shape, lambda k: (0, 0, 0)),
            small,
            pl.BlockSpec((width // steps, tokens), lambda k: (k, 0)),
        ],
        out_specs=[small, pl.BlockSpec((rows, width // steps), lambda k: (0, k))],
        out_shape=[
            jax.ShapeDtypeStruct((rows, tokens), BF16),
            jax.ShapeDtypeStruct((rows, width), BF16),
        ],
        compiler_params=PARAMS,
        cost_estimate=cost(2 * rows * width * tokens, 2 * (terms.size + width * tokens + rows * width)),
        name="gradient",
    )(terms, student_out, student_all)


def shards(teacher_rows, teacher_gate, teacher_up, teacher_down, student_rows, projector):
    place = jnp.stack([lax.axis_index("core"), lax.axis_index("dp")]).astype(jnp.int32)
    rows = teacher_rows.shape[0]
    chips = lax.axis_size(CHIPS)
    across = lax.axis_size("y") // 2
    spread = functools.partial(
        lax.all_to_all, axis_name=CHIPS, split_axis=0, concat_axis=0, tiled=True
    )

    trade = []
    for y in range(across):
        low, high = 2 * y, 2 * (y + across)
        trade += [(low, low), (low + 1, high), (high, low + 1), (high + 1, high + 1)]
    held = lax.ppermute(teacher_rows, ("y", "dp"), trade)
    teacher_own = spread(copies(held, held, chips))
    teacher_other = lax.ppermute(teacher_own, "core", SWAP)
    down_far = lax.ppermute(teacher_down, "dp", SWAP)

    student_own = spread(copies(student_rows, teacher_own, chips))

    keep, send = up_part(place, teacher_own, teacher_other, teacher_gate, teacher_up)
    got = lax.ppermute(send, "dp", SWAP)
    teacher_hidden, mine, theirs = down_part(place, keep, got, teacher_down, down_far, rows)
    chip_sum = (
        mine.astype(F32) + lax.ppermute(theirs, "core", SWAP).astype(F32)
    ).astype(BF16)
    terms = spread(chip_sum)

    student_other = lax.ppermute(student_own, "core", SWAP)
    student_all, student_out = student_part(place, student_own, student_other, projector)
    residual_error, grad_local = grad_part(terms, student_out, student_all)
    grad_projector = grad_local + lax.ppermute(grad_local, "dp", SWAP)
    return (teacher_hidden, residual_error, grad_projector)


def solution(mesh):
    fine = Mesh(mesh.devices.reshape(8, 2, 8, 2, 2), (*CHIPS, "core", "dp"))
    blk = (*CHIPS, "core")
    return jax.shard_map(
        shards,
        mesh=fine,
        in_specs=(P(blk, "dp"),) * 5 + (P(blk, None),),
        out_specs=(P(blk, "dp"), P(blk, "dp"), P(blk, None)),
        check_vma=False,
    )
```

time: 2140 us -> 169 us (0.08)
  the two profiles are of different devices: /device:TPU:1 before, /device:TPU:8 now
where the time goes in v1:
time: 169 us; the launch traced here: 168 us
  blocking collectives  58.6 us (35%)
  waiting for transfers between devices  57.1 us (34%)
  starting transfers between devices  30.6 us (18%)
  Pallas kernels  13.8 us (8%)
  local copies, waits for them, and re-layouts  5.24 us (3%)
  other arithmetic  2.31 us (1%)
    all_to_all x1, blocking collectives, shards(): teacher_own = spread(copies(held, held, chips))  58.6 us
    all_to_all x1, waiting for transfers between devices, shards(): terms = spread(chip_sum)  23.2 us
    ppermute x1, waiting for transfers between devices, shards(): down_far = lax.ppermute(teacher_down, 'dp', SWAP)  13.7 us
    ppermute x1, waiting for transfers between devices, shards(): grad_projector = grad_local + lax.ppermute(grad_local, 'dp', SWAP)  13.2 us
    pallas_call x1, Pallas kernels, down_part(): pl.pallas_call(down_kernel, grid_spec=pltpu.PrefetchScalarGridSpec(num_sc...  6.55 us
    all_to_all x1, starting transfers between devices, shards(): student_own = spread(copies(student_rows, teacher_own, chips))  6.27 us
    ppermute x1, starting transfers between devices, shards(): got = lax.ppermute(send, 'dp', SWAP)  5.89 us
    all_to_all x1, starting transfers between devices, shards(): terms = spread(chip_sum)  5.81 us
  transfers between devices with their start and end apart: 9, of which 6 were waited for; matrix products, arithmetic and copies ran while one was open for 1% of the time, Pallas kernels for 7%

profile of v1, /device:TPU:8, one launch (start us, length us, event | category | flops | bytes accessed | tf_op | source)
XLA Modules:
  0.0 168.4 jit_solution(7622190962632687588)
XLA Ops:
  0.6 1.4 collective-permute-start
  2.0 0.0 collective-permute-done.rows_ref._
  2.0 0.1 copies.2
  2.1 58.6 %all_to_all.15._ = bf16[128,32,128]{2,1,0:T(8,128)(2,1)S(1)} all-to-all(bf16[128,32,128]{2,1,0:T(8,128)(2,1)S(1)} %copies.2), channel_id=1, replica_groups=mesh['y'=8,'x'=2,'z'=8,'core'=2,'dp'=2] {'y','x','z'}, dimensions={0} | all-to-all | bytes 2097152 | tf_op jit(solution)/shard_map/all_to_all | solution.py:232
  60.7 1.9 %collective-permute-start.1 = (bf16[128,32,128]{2,1,0:T(8,128)(2,1)S(1)}, bf16[128,32,128]{2,1,0:T(8,128)(2,1)S(1)}, u32[]{:S(2)}, u32[]{:S(2)}) collective-permute-start(bf16[128,32,128]{2,1,0:T(8,128)(2,1)S(1)} %all_to_all.15._), channel_id=1, source_target_pairs={{0,2},{2,0},{1,3},{3,1},{4,6},{6,4},{5,7},{7,5},{8,10},{10,8},{9,1... | collective-permute-start | bytes 3145736 | tf_op jit(solution)/shard_map/ppermute | solution.py:233
  62.6 2.4 %collective-permute-start.3 = (bf16[104,4096]{1,0:T(8,128)(2,1)}, bf16[104,4096]{1,0:T(8,128)(2,1)}, u32[]{:S(2)}, u32[]{:S(2)}) collective-permute-start(bf16[104,4096]{1,0:T(8,128)(2,1)} %near_ref.1), channel_id=1, source_target_pairs={{0,1},{1,0},{2,3},{3,2},{4,5},{5,4},{6,7},{7,6},{8,9},{9,8},{10,11... | collective-permute-start | bytes 2555912 | tf_op jit(solution)/shard_map/ppermute | solution.py:234
  65.1 1.1 copies.3
  66.2 6.3 %all-to-all-start.2 = ((bf16[128,32,128]{2,1,0:T(8,128)(2,1)}), bf16[128,32,128]{2,1,0:T(8,128)(2,1)S(1)}, u32[]{:S(2)}, u32[]{:S(2)}) async-start(bf16[128,32,128]{2,1,0:T(8,128)(2,1)} %copies.3), calls=%async_computation.2 | async-start | bytes 2097152 | tf_op jit(solution)/shard_map/all_to_all | solution.py:236
  72.5 0.1 pad_add_fusion.place_ref
  72.6 0.0 collective-permute-done.1
  72.6 1.2 copy-done.2
  73.7 1.2 copy-done.3
  74.9 2.2 %gate_up.1 = (f32[2,104,128]{2,1,0:T(8,128)S(1)}, bf16[2,104,128]{2,1,0:T(8,128)(2,1)S(1)}) custom-call(s32[2]{0:T(128)S(1)} %pad_add_fusion.place_ref, bf16[2,64,32,128]{3,2,1,0:T(8,128)(2,1)S(1)} %bitcast.8, bf16[2,64,32,128]{3,2,1,0:T(8,128)(2,1)S(1)} %bitcast.9, bf16[104,4096]{1,0:T(8,128)(2,1)S(1)} %copy-done.2, bf16[104,4096]{1,0:T(8,128)(2,1)S(1)} %copy-done.3), custom_call_target="tpu_custom_call" | custom-call | flops 436207616 | bytes 3801088 | tf_op jit(solution)/shard_map/gate_up/pallas_call | solution.py:73
  77.1 5.9 %collective-permute-start.2 = (bf16[2,104,128]{2,1,0:T(8,128)(2,1)S(1)}, bf16[2,104,128]{2,1,0:T(8,128)(2,1)S(1)}, u32[]{:S(2)}, u32[]{:S(2)}) collective-permute-start(bf16[2,104,128]{2,1,0:T(8,128)(2,1)S(1)} %get-tuple-element.13), channel_id=1, source_target_pairs={{0,1},{1,0},{2,3},{3,2},{4,5},{5,4},{6,7},{7,6},{8,9},{9,8},{10,11... | collective-permute-start | bytes 159752 | tf_op jit(solution)/shard_map/ppermute | solution.py:239
  83.0 13.7 %collective-permute-done.3.far_ref = bf16[104,4096]{1,0:T(8,128)(2,1)} collective-permute-done((bf16[104,4096]{1,0:T(8,128)(2,1)}, bf16[104,4096]{1,0:T(8,128)(2,1)}, u32[]{:S(2)}, u32[]{:S(2)}) %collective-permute-start.3) | collective-permute-done | bytes 852000 | tf_op jit(solution)/shard_map/ppermute | solution.py:234
  96.7 1.8 %collective-permute-done.2.got_ref = bf16[2,104,128]{2,1,0:T(8,128)(2,1)S(1)} collective-permute-done((bf16[2,104,128]{2,1,0:T(8,128)(2,1)S(1)}, bf16[2,104,128]{2,1,0:T(8,128)(2,1)S(1)}, u32[]{:S(2)}, u32[]{:S(2)}) %collective-permute-start.2) | collective-permute-done | bytes 53280 | tf_op jit(solution)/shard_map/ppermute | solution.py:239
  98.5 6.5 %down.1 = (bf16[104,128]{1,0:T(8,128)(2,1)}, bf16[2,64,32,128]{3,2,1,0:T(8,128)(2,1)S(1)}, bf16[2,64,32,128]{3,2,1,0:T(8,128)(2,1)S(1)}) custom-call(s32[2]{0:T(128)S(1)} %pad_add_fusion.place_ref, f32[2,104,128]{2,1,0:T(8,128)S(1)} %get-tuple-element.12.keep_ref, bf16[2,104,128]{2,1,0:T(8,128)(2,1)S(1)} %collective-permute-done.2.got_ref, ...), custom_call_target="tpu_custom_call" | custom-call | flops 218103808 | bytes 5898240 | tf_op jit(solution)/shard_map/down/pallas_call | solution.py:124
  105.0 1.9 %collective-permute-start.4 = (bf16[128,32,128]{2,1,0:T(8,128)(2,1)S(1)}, bf16[128,32,128]{2,1,0:T(8,128)(2,1)S(1)}, u32[]{:S(2)}, u32[]{:S(2)}) collective-permute-start(bf16[128,32,128]{2,1,0:T(8,128)(2,1)S(1)} %bitcast.10), channel_id=1, source_target_pairs={{0,2},{2,0},{1,3},{3,1},{4,6},{6,4},{5,7},{7,5},{8,10},{10,8},{9,1... | collective-permute-start | bytes 3145736 | tf_op jit(solution)/shard_map/ppermute | solution.py:242
  106.9 2.6 %collective-permute-done.4 = bf16[128,32,128]{2,1,0:T(8,128)(2,1)S(1)} collective-permute-done((bf16[128,32,128]{2,1,0:T(8,128)(2,1)S(1)}, bf16[128,32,128]{2,1,0:T(8,128)(2,1)S(1)}, u32[]{:S(2)}, u32[]{:S(2)}) %collective-permute-start.4) | collective-permute-done | bytes 1048608 | tf_op jit(solution)/shard_map/ppermute | solution.py:242
  109.6 1.3 fusion
  110.9 0.0 all-to-all-done.2.own_ref
  110.9 5.8 %all-to-all-start.1 = ((bf16[128,32,128]{2,1,0:T(8,128)(2,1)}), bf16[128,32,128]{2,1,0:T(8,128)(2,1)S(1)}, u32[]{:S(2)}, u32[]{:S(2)}) async-start(bf16[128,32,128]{2,1,0:T(8,128)(2,1)} %fusion), calls=%async_computation.1 | async-start | bytes 2097152 | tf_op jit(solution)/shard_map/all_to_all | solution.py:244
  116.7 1.9 %collective-permute-start.5 = (bf16[128,32,128]{2,1,0:T(8,128)(2,1)S(1)}, bf16[128,32,128]{2,1,0:T(8,128)(2,1)S(1)}, u32[]{:S(2)}, u32[]{:S(2)}) collective-permute-start(bf16[128,32,128]{2,1,0:T(8,128)(2,1)S(1)} %all-to-all-done.2.own_ref), channel_id=1, source_target_pairs={{0,2},{2,0},{1,3},{3,1},{4,6},{6,4},{5,7},{7,5},{8,10},{10,8},{9,1... | collective-permute-start | bytes 3145736 | tf_op jit(solution)/shard_map/ppermute | solution.py:246
  118.6 2.6 %collective-permute-done.5.other_ref = bf16[128,32,128]{2,1,0:T(8,128)(2,1)S(1)} collective-permute-done((bf16[128,32,128]{2,1,0:T(8,128)(2,1)S(1)}, bf16[128,32,128]{2,1,0:T(8,128)(2,1)S(1)}, u32[]{:S(2)}, u32[]{:S(2)}) %collective-permute-start.5) | collective-permute-done | bytes 1048608 | tf_op jit(solution)/shard_map/ppermute | solution.py:246
  121.3 2.1 %student.1 = (bf16[8192,128]{1,0:T(8,128)(2,1)S(1)}, f32[32,128]{1,0:T(8,128)S(1)}) custom-call(s32[2]{0:T(128)S(1)} %pad_add_fusion.place_ref, bf16[128,32,128]{2,1,0:T(8,128)(2,1)S(1)} %all-to-all-done.2.own_ref, bf16[128,32,128]{2,1,0:T(8,128)(2,1)S(1)} %collective-permute-done.5.other_ref, bf16[32,8192]{1,0:T(8,128)(2,1)S(1)} %copy-done.4), custom_call_target="tpu_custom_call" | custom-call | flops 67108864 | bytes 4718592 | tf_op jit(solution)/shard_map/student/pallas_call | solution.py:163
  123.4 1.3 copy-done
  124.7 23.2 %all-to-all-done.1.terms_ref = bf16[128,32,128]{2,1,0:T(8,128)(2,1)S(1)} async-done(((bf16[128,32,128]{2,1,0:T(8,128)(2,1)}), bf16[128,32,128]{2,1,0:T(8,128)(2,1)S(1)}, u32[]{:S(2)}, u32[]{:S(2)}) %all-to-all-start.1) | async-done | bytes 1048608 | tf_op jit(solution)/shard_map/all_to_all | solution.py:244
  147.9 1.6 copy-done.1
  149.5 1.7 %gradient.1 = (bf16[32,128]{1,0:T(8,128)(2,1)}, bf16[32,8192]{1,0:T(8,128)(2,1)S(1)}) custom-call(bf16[128,32,128]{2,1,0:T(8,128)(2,1)S(1)} %all-to-all-done.1.terms_ref, f32[32,128]{1,0:T(8,128)S(1)} %get-tuple-element.17.student_out_ref, bf16[8192,128]{1,0:T(8,128)(2,1)S(1)} %copy-done.1), custom_call_target="tpu_custom_call" | custom-call | flops 67108864 | bytes 3670016 | tf_op jit(solution)/shard_map/gradient/pallas_call | solution.py:199
  151.2 3.1 %collective-permute-start.6 = (bf16[32,8192]{1,0:T(8,128)(2,1)S(1)}, bf16[32,8192]{1,0:T(8,128)(2,1)S(1)}, u32[]{:S(2)}, u32[]{:S(2)}) collective-permute-start(bf16[32,8192]{1,0:T(8,128)(2,1)S(1)} %get-tuple-element.20), channel_id=1, source_target_pairs={{0,1},{1,0},{2,3},{3,2},{4,5},{5,4},{6,7},{7,6},{8,9},{9,8},{10,11... | collective-permute-start | bytes 1572872 | tf_op jit(solution)/shard_map/ppermute | solution.py:249
  154.3 13.2 %collective-permute-done.6 = bf16[32,8192]{1,0:T(8,128)(2,1)S(1)} collective-permute-done((bf16[32,8192]{1,0:T(8,128)(2,1)S(1)}, bf16[32,8192]{1,0:T(8,128)(2,1)S(1)}, u32[]{:S(2)}, u32[]{:S(2)}) %collective-permute-start.6) | collective-permute-done | bytes 524320 | tf_op jit(solution)/shard_map/ppermute | solution.py:249
  167.5 0.9 add.7
  (8 shorter events, 0.0 us)
Async XLA Ops:
  0.6 64.4 %copy-start.5 = (bf16[32,128]{1,0:T(8,128)(2,1)S(1)}, bf16[32,128]{1,0:T(8,128)(2,1)}, u32[]{:S(2)}) copy-start(bf16[32,128]{1,0:T(8,128)(2,1)} %rows_ref.1) | copy-start | bytes 24580
  0.6 1.4 collective-permute-start
  60.7 11.8 %collective-permute-start.1 = (bf16[128,32,128]{2,1,0:T(8,128)(2,1)S(1)}, bf16[128,32,128]{2,1,0:T(8,128)(2,1)S(1)}, u32[]{:S(2)}, u32[]{:S(2)}) collective-permute-start(bf16[128,32,128]{2,1,0:T(8,128)(2,1)S(1)} %all_to_all.15._), channel_id=1, source_target_pairs={{0,2},{2,0},{1,3},{3,1},{4,6},{6,4},{5,7},{7,5},{8,10},{10,8},{9,1... | collective-permute-start | bytes 3145736 | tf_op jit(solution)/shard_map/ppermute | solution.py:233
  62.6 34.1 %collective-permute-start.3 = (bf16[104,4096]{1,0:T(8,128)(2,1)}, bf16[104,4096]{1,0:T(8,128)(2,1)}, u32[]{:S(2)}, u32[]{:S(2)}) collective-permute-start(bf16[104,4096]{1,0:T(8,128)(2,1)} %near_ref.1), channel_id=1, source_target_pairs={{0,1},{1,0},{2,3},{3,2},{4,5},{5,4},{6,7},{7,6},{8,9},{9,8},{10,11... | collective-permute-start | bytes 2555912 | tf_op jit(solution)/shard_map/ppermute | solution.py:234
  66.2 44.7 %all-to-all-start.2 = ((bf16[128,32,128]{2,1,0:T(8,128)(2,1)}), bf16[128,32,128]{2,1,0:T(8,128)(2,1)S(1)}, u32[]{:S(2)}, u32[]{:S(2)}) async-start(bf16[128,32,128]{2,1,0:T(8,128)(2,1)} %copies.3), calls=%async_computation.2 | async-start | bytes 2097152 | tf_op jit(solution)/shard_map/all_to_all | solution.py:236
  72.6 1.2 copy-start.2
  73.7 1.2 copy-start.3
  77.1 21.4 %collective-permute-start.2 = (bf16[2,104,128]{2,1,0:T(8,128)(2,1)S(1)}, bf16[2,104,128]{2,1,0:T(8,128)(2,1)S(1)}, u32[]{:S(2)}, u32[]{:S(2)}) collective-permute-start(bf16[2,104,128]{2,1,0:T(8,128)(2,1)S(1)} %get-tuple-element.13), channel_id=1, source_target_pairs={{0,1},{1,0},{2,3},{3,2},{4,5},{5,4},{6,7},{7,6},{8,9},{9,8},{10,11... | collective-permute-start | bytes 159752 | tf_op jit(solution)/shard_map/ppermute | solution.py:239
  105.0 4.5 %collective-permute-start.4 = (bf16[128,32,128]{2,1,0:T(8,128)(2,1)S(1)}, bf16[128,32,128]{2,1,0:T(8,128)(2,1)S(1)}, u32[]{:S(2)}, u32[]{:S(2)}) collective-permute-start(bf16[128,32,128]{2,1,0:T(8,128)(2,1)S(1)} %bitcast.10), channel_id=1, source_target_pairs={{0,2},{2,0},{1,3},{3,1},{4,6},{6,4},{5,7},{7,5},{8,10},{10,8},{9,1... | collective-permute-start | bytes 3145736 | tf_op jit(solution)/shard_map/ppermute | solution.py:242
  109.6 11.7 %copy-start.4 = (bf16[32,8192]{1,0:T(8,128)(2,1)S(1)}, bf16[32,8192]{1,0:T(8,128)(2,1)}, u32[]{:S(2)}) copy-start(bf16[32,8192]{1,0:T(8,128)(2,1)} %projector_ref.1) | copy-start | bytes 1572868
  110.9 37.0 %all-to-all-start.1 = ((bf16[128,32,128]{2,1,0:T(8,128)(2,1)}), bf16[128,32,128]{2,1,0:T(8,128)(2,1)S(1)}, u32[]{:S(2)}, u32[]{:S(2)}) async-start(bf16[128,32,128]{2,1,0:T(8,128)(2,1)} %fusion), calls=%async_computation.1 | async-start | bytes 2097152 | tf_op jit(solution)/shard_map/all_to_all | solution.py:244
  116.7 4.6 %collective-permute-start.5 = (bf16[128,32,128]{2,1,0:T(8,128)(2,1)S(1)}, bf16[128,32,128]{2,1,0:T(8,128)(2,1)S(1)}, u32[]{:S(2)}, u32[]{:S(2)}) collective-permute-start(bf16[128,32,128]{2,1,0:T(8,128)(2,1)S(1)} %all-to-all-done.2.own_ref), channel_id=1, source_target_pairs={{0,2},{2,0},{1,3},{3,1},{4,6},{6,4},{5,7},{7,5},{8,10},{10,8},{9,1... | collective-permute-start | bytes 3145736 | tf_op jit(solution)/shard_map/ppermute | solution.py:246
  123.4 1.3 copy-start
  147.9 1.6 copy-start.1
  151.2 16.3 %collective-permute-start.6 = (bf16[32,8192]{1,0:T(8,128)(2,1)S(1)}, bf16[32,8192]{1,0:T(8,128)(2,1)S(1)}, u32[]{:S(2)}, u32[]{:S(2)}) collective-permute-start(bf16[32,8192]{1,0:T(8,128)(2,1)S(1)} %get-tuple-element.20), channel_id=1, source_target_pairs={{0,1},{1,0},{2,3},{3,2},{4,5},{5,4},{6,7},{7,6},{8,9},{9,8},{10,11... | collective-permute-start | bytes 1572872 | tf_op jit(solution)/shard_map/ppermute | solution.py:249

commit v2 on v1

v2 whole, which is shorter than its diff:
```python
import functools

import jax
import jax.numpy as jnp
from jax import lax
from jax.experimental import pallas as pl
from jax.experimental.pallas import tpu as pltpu
from jax.sharding import Mesh, PartitionSpec as P

CHIPS = ("y", "x", "z")
SWAP = [(0, 1), (1, 0)]
F32, BF16 = jnp.float32, jnp.bfloat16
PARAMS = pltpu.CompilerParams(vmem_limit_bytes=24 << 20)


def cost(flops, size):
    return pl.CostEstimate(flops=flops, bytes_accessed=size, transcendentals=0)


def zip_cores(core, own, other):
    count, rows, tokens = own.shape
    even = jnp.where(core == 0, own, other)
    odd = jnp.where(core == 0, other, own)
    return jnp.stack([even, odd], axis=1).reshape(count * 2 * rows, tokens)


def copies_kernel(rows_ref, _, out_ref):
    out_ref[...] = jnp.broadcast_to(rows_ref[...][None], out_ref.shape)


def copies(rows, after, count):
    return pl.pallas_call(
        copies_kernel,
        in_specs=[pl.BlockSpec(memory_space=pltpu.VMEM), pl.BlockSpec(memory_space=pl.ANY)],
        out_shape=jax.ShapeDtypeStruct((count, *rows.shape), rows.dtype),
        compiler_params=PARAMS,
        cost_estimate=cost(0, count * rows.size * 2),
        name="copies",
    )(rows, after)


def up_kernel(place_ref, own_ref, other_ref, gate_ref, up_ref, keep_ref, send_ref, weight_ref, acc_ref, sem_ref):
    core, half = place_ref[0], place_ref[1]
    steps, width = weight_ref.shape[1], weight_ref.shape[3]
    per, tokens = own_ref.shape[1] // steps, own_ref.shape[3]
    arrive = []
    for k in range(steps):
        for i, ref in enumerate((gate_ref, up_ref)):
            arrive.append(
                pltpu.make_async_copy(ref.at[:, pl.ds(k * width, width)], weight_ref.at[i, k], sem_ref.at[i, k])
            )
            arrive[-1].start()
    for k in range(steps):
        part = slice(k * per, (k + 1) * per)
        rows = jnp.concatenate(
            [zip_cores(core, own_ref[t, part], other_ref[t, part]) for t in range(2)], axis=1
        )
        for i in range(2):
            arrive[2 * k + i].wait()
            term = jnp.dot(weight_ref[i, k], rows, preferred_element_type=F32)
            if k == 0:
                acc_ref[i] = term
            else:
                acc_ref[i] += term
    for i in range(2):
        low, high = acc_ref[i, :, :tokens], acc_ref[i, :, tokens:]
        keep_ref[i] = jnp.where(half == 0, low, high)
        send_ref[i] = jnp.where(half == 0, high, low).astype(BF16)


def up_part(place, own, other, gate, up, steps=4):
    hidden, width = gate.shape
    rows, tokens = own.shape[-2:]
    own, other = (a.reshape(2, -1, rows, tokens) for a in (own, other))
    vmem = pl.BlockSpec(memory_space=pltpu.VMEM)
    hbm = pl.BlockSpec(memory_space=pltpu.HBM)
    return pl.pallas_call(
        up_kernel,
        in_specs=[pl.BlockSpec(memory_space=pltpu.SMEM), vmem, vmem, hbm, hbm],
        out_specs=[vmem, vmem],
        out_shape=[
            jax.ShapeDtypeStruct((2, hidden, tokens), F32),
            jax.ShapeDtypeStruct((2, hidden, tokens), BF16),
        ],
        scratch_shapes=[
            pltpu.VMEM((2, steps, hidden, width // steps), BF16),
            pltpu.VMEM((2, hidden, 2 * tokens), F32),
            pltpu.SemaphoreType.DMA((2, steps)),
        ],
        compiler_params=PARAMS,
        cost_estimate=cost(8 * hidden * width * tokens, 4 * hidden * width + 4 * own.size),
        name="gate_up",
    )(place, own, other, gate, up)


def hidden_kernel(keep_ref, got_ref, out_ref):
    preact, uppre = (keep_ref[i] + got_ref[i].astype(F32) for i in range(2))
    out_ref[...] = (preact / (1 + jnp.exp(-preact)) * uppre).astype(BF16)


def hidden_part(keep, got):
    return pl.pallas_call(
        hidden_kernel,
        out_shape=jax.ShapeDtypeStruct(keep.shape[1:], BF16),
        compiler_params=PARAMS,
        cost_estimate=cost(0, 0),
        name="hidden",
    )(keep, got)


def down_kernel(place_ref, hidden_ref, down_ref, mine_ref, theirs_ref):
    core = place_ref[0]
    count, rows, tokens = mine_ref.shape
    out = jnp.dot(down_ref[...], hidden_ref[...], preferred_element_type=F32).astype(BF16)
    out = out.reshape(count, 2, rows, tokens)
    even, odd = out[:, 0], out[:, 1]
    mine_ref[...] = jnp.where(core == 0, even, odd)
    theirs_ref[...] = jnp.where(core == 0, odd, even)


def down_part(place, hidden_units, down, rows, steps=4):
    width, hidden = down.shape
    tokens = hidden_units.shape[-1]
    count = width // (2 * rows)
    block = pl.BlockSpec((count // steps, rows, tokens), lambda k, _: (k, 0, 0))
    out = jax.ShapeDtypeStruct((count, rows, tokens), BF16)
    return pl.pallas_call(
        down_kernel,
        grid_spec=pltpu.PrefetchScalarGridSpec(
            num_scalar_prefetch=1,
            grid=(steps,),
            in_specs=[
                pl.BlockSpec((hidden, tokens), lambda k, _: (0, 0)),
                pl.BlockSpec((width // steps, hidden), lambda k, _: (k, 0)),
            ],
            out_specs=[block, block],
        ),
        out_shape=[out, out],
        compiler_params=PARAMS,
        cost_estimate=cost(0, 0),
        name="down",
    )(place, hidden_units, down)


def student_kernel(place_ref, own_ref, own_core_ref, next_ref, next_core_ref, projector_ref, all_ref, out_ref):
    core, x = place_ref[0], place_ref[2]
    here = zip_cores(core, own_ref[0], own_core_ref[0])
    there = zip_cores(core, next_ref[0], next_core_ref[0])
    rows = jnp.concatenate([jnp.where(x == 0, here, there), jnp.where(x == 0, there, here)])
    all_ref[...] = rows
    part = jnp.dot(projector_ref[...], rows, preferred_element_type=F32)

    @pl.when(pl.program_id(0) == 0)
    def _():
        out_ref[...] = part

    @pl.when(pl.program_id(0) != 0)
    def _():
        out_ref[...] += part


def student_part(place, pieces, projector):
    steps, count, rows, tokens = pieces[0].shape
    mine, width = projector.shape
    block = pl.BlockSpec((1, count, rows, tokens), lambda k, _: (k, 0, 0, 0))
    return pl.pallas_call(
        student_kernel,
        grid_spec=pltpu.PrefetchScalarGridSpec(
            num_scalar_prefetch=1,
            grid=(steps,),
            in_specs=[block] * 4 + [pl.BlockSpec((mine, width // steps), lambda k, _: (0, k))],
            out_specs=[
                pl.BlockSpec((width // steps, tokens), lambda k, _: (k, 0)),
                pl.BlockSpec((mine, tokens), lambda k, _: (0, 0)),
            ],
        ),
        out_shape=[
            jax.ShapeDtypeStruct((width, tokens), BF16),
            jax.ShapeDtypeStruct((mine, tokens), F32),
        ],
        compiler_params=PARAMS,
        cost_estimate=cost(2 * mine * width * tokens, 4 * width * tokens + 2 * mine * width),
        name="student",
    )(place, *pieces, projector)


def grad_kernel(terms_ref, student_out_ref, student_ref, residual_ref, grad_ref, rows_ref, sem_ref):
    steps, width = rows_ref.shape[:2]
    arrive = []
    for k in range(steps):
        arrive.append(
            pltpu.make_async_copy(student_ref.at[pl.ds(k * width, width)], rows_ref.at[k], sem_ref.at[k])
        )
        arrive[-1].start()
    teacher_out = jnp.sum(terms_ref[...].astype(F32), axis=0)
    residual = (student_out_ref[...] - teacher_out).astype(BF16)
    residual_ref[...] = residual
    for k in range(steps):
        arrive[k].wait()
        grad_ref[:, k * width : (k + 1) * width] = lax.dot_general(
            residual, rows_ref[k], (((1,), (1,)), ((), ())), preferred_element_type=F32
        ).astype(BF16)


def grad_part(terms, student_out, student_all, steps=8):
    rows, tokens = student_out.shape
    width = student_all.shape[0]
    vmem = pl.BlockSpec(memory_space=pltpu.VMEM)
    return pl.pallas_call(
        grad_kernel,
        in_specs=[vmem, vmem, pl.BlockSpec(memory_space=pltpu.HBM)],
        out_specs=[vmem, vmem],
        out_shape=[
            jax.ShapeDtypeStruct((rows, tokens), BF16),
            jax.ShapeDtypeStruct((rows, width), BF16),
        ],
        scratch_shapes=[
            pltpu.VMEM((steps, width // steps, tokens), BF16),
            pltpu.SemaphoreType.DMA((steps,)),
        ],
        compiler_params=PARAMS,
        cost_estimate=cost(2 * rows * width * tokens, 2 * (terms.size + width * tokens + rows * width)),
        name="gradient",
    )(terms, student_out, student_all)


def shards(teacher_rows, teacher_gate, teacher_up, teacher_down, student_rows, projector):
    place = jnp.stack([lax.axis_index(name) for name in ("core", "dp", "x")]).astype(jnp.int32)
    rows = teacher_rows.shape[0]
    chips = lax.axis_size(CHIPS)
    across = lax.axis_size("y") // 2
    spread = functools.partial(lax.all_to_all, split_axis=0, concat_axis=0, tiled=True)

    trade = []
    for y in range(across):
        low, high = 2 * y, 2 * (y + across)
        trade += [(low, low), (low + 1, high), (high, low + 1), (high + 1, high + 1)]
    held = lax.ppermute(teacher_rows, ("y", "dp"), trade)
    down_far = lax.ppermute(teacher_down, "dp", SWAP)
    teacher_own = spread(copies(held, held, chips), CHIPS)
    teacher_own, down_far = lax.optimization_barrier((teacher_own, down_far))
    teacher_other = lax.ppermute(teacher_own, "core", SWAP)

    plane = ("y", "z")
    student_own = spread(copies(student_rows, teacher_own, lax.axis_size(plane)), plane)

    keep, send = up_part(place, teacher_own, teacher_other, teacher_gate, teacher_up)
    got = lax.ppermute(send, "dp", SWAP)
    teacher_hidden = hidden_part(keep, got)
    sums = []
    for down in (teacher_down, down_far):
        mine, theirs = down_part(place, teacher_hidden, down.T, rows)
        sums.append((mine.astype(F32) + lax.ppermute(theirs, "core", SWAP).astype(F32)).astype(BF16))
    near, far = sums
    first = place[1] == 0
    chip_sum = jnp.concatenate([jnp.where(first, near, far), jnp.where(first, far, near)])
    terms = spread(chip_sum, CHIPS)

    student_next = lax.ppermute(student_own, "x", SWAP)
    pieces = []
    for piece in (student_own, student_next):
        pieces += [piece, lax.ppermute(piece, "core", SWAP)]
    pieces = [a.reshape(lax.axis_size("y"), -1, *a.shape[1:]) for a in pieces]
    student_all, student_out = student_part(place, pieces, projector)
    residual_error, grad_local = grad_part(terms, student_out, student_all)
    grad_projector = grad_local + lax.ppermute(grad_local, "dp", SWAP)
    return (teacher_hidden, residual_error, grad_projector)


def solution(mesh):
    fine = Mesh(mesh.devices.reshape(8, 2, 8, 2, 2), (*CHIPS, "core", "dp"))
    blk = (*CHIPS, "core")
    return jax.shard_map(
        shards,
        mesh=fine,
        in_specs=(P(blk, "dp"),) * 5 + (P(blk, None),),
        out_specs=(P(blk, "dp"), P(blk, "dp"), P(blk, None)),
        check_vma=False,
    )
```

time: 169 us -> 175 us (1.036)
  the two profiles are of different devices: /device:TPU:8 before, /device:TPU:1 now
where the time goes in v2:
time: 175 us; the launch traced here: 174 us
  starting transfers between devices  82.7 us (47%)
  waiting for transfers between devices  65.3 us (37%)
  Pallas kernels  14.2 us (8%)
  local copies, waits for them, and re-layouts  7.82 us (4%)
  other arithmetic  3.45 us (2%)
    ppermute x1, waiting for transfers between devices, shards(): down_far = lax.ppermute(teacher_down, 'dp', SWAP)  30.1 us
    all_to_all x1, starting transfers between devices, shards(): teacher_own = spread(copies(held, held, chips), CHIPS)  29 us
    ppermute x1, waiting for transfers between devices, shards(): student_next = lax.ppermute(student_own, 'x', SWAP)  19.1 us
    all_to_all x1, starting transfers between devices, shards(): terms = spread(chip_sum, CHIPS)  14.7 us
    ppermute x1, waiting for transfers between devices, shards(): grad_projector = grad_local + lax.ppermute(grad_local, 'dp', SWAP)  12.5 us
    all_to_all x1, starting transfers between devices, shards(): spread(copies(student_rows, teacher_own, lax.axis_size(plane)), plane)  10.5 us
    unnamed x21, local copies, waits for them, and re-layouts  6.23 us
    ppermute x2, starting transfers between devices, shards(): pieces += [piece, lax.ppermute(piece, 'core', SWAP)]  6.03 us
  transfers between devices with their start and end apart: 13, of which 6 were waited for; matrix products, arithmetic and copies ran while one was open for 3% of the time, Pallas kernels for 6%

profile of v2, /device:TPU:1, one launch (start us, length us, event | category | flops | bytes accessed | tf_op | source)
XLA Modules:
  0.0 174.4 jit_solution(10188254317373705428)
XLA Ops:
  0.7 1.5 collective-permute-start
  2.1 1.1 copies.2
  3.3 29.0 %all-to-all-start = ((bf16[128,32,128]{2,1,0:T(8,128)(2,1)}), bf16[128,32,128]{2,1,0:T(8,128)(2,1)S(1)}, u32[]{:S(2)}, u32[]{:S(2)}) async-start(bf16[128,32,128]{2,1,0:T(8,128)(2,1)} %copies.2), calls=%async_computation | async-start | bytes 2097152 | tf_op jit(solution)/shard_map/all_to_all | solution.py:240
  32.3 2.1 %collective-permute-start.1 = (bf16[104,4096]{1,0:T(8,128)(2,1)S(1)}, bf16[104,4096]{1,0:T(8,128)(2,1)}, u32[]{:S(2)}, u32[]{:S(2)}) collective-permute-start(bf16[104,4096]{1,0:T(8,128)(2,1)S(1)} %copy-done.9), channel_id=1, source_target_pairs={{0,1},{1,0},{2,3},{3,2},{4,5},{5,4},{6,7},{7,6},{8,9},{9,8},{10,11... | collective-permute-start | bytes 2555912 | tf_op jit(solution)/shard_map/ppermute | solution.py:239
  34.4 30.1 %collective-permute-done.1 = bf16[104,4096]{1,0:T(8,128)(2,1)} collective-permute-done((bf16[104,4096]{1,0:T(8,128)(2,1)S(1)}, bf16[104,4096]{1,0:T(8,128)(2,1)}, u32[]{:S(2)}, u32[]{:S(2)}) %collective-permute-start.1) | collective-permute-done | bytes 852000 | tf_op jit(solution)/shard_map/ppermute | solution.py:239
  64.5 4.1 %collective-permute-start.2 = (bf16[128,32,128]{2,1,0:T(8,128)(2,1)S(1)}, bf16[128,32,128]{2,1,0:T(8,128)(2,1)S(1)}, u32[]{:S(2)}, u32[]{:S(2)}) collective-permute-start(bf16[128,32,128]{2,1,0:T(8,128)(2,1)S(1)} %all-to-all-done._), channel_id=1, source_target_pairs={{0,2},{2,0},{1,3},{3,1},{4,6},{6,4},{5,7},{7,5},{8,10},{10,8},{9,1... | collective-permute-start | bytes 3145736 | tf_op jit(solution)/shard_map/ppermute | solution.py:242
  69.6 10.5 %all-to-all-start.2 = ((bf16[64,32,128]{2,1,0:T(8,128)(2,1)}), bf16[64,32,128]{2,1,0:T(8,128)(2,1)S(1)}, u32[]{:S(2)}, u32[]{:S(2)}) async-start(bf16[64,32,128]{2,1,0:T(8,128)(2,1)} %copies.3), calls=%async_computation.2 | async-start | bytes 1048576 | tf_op jit(solution)/shard_map/all_to_all | solution.py:245
  80.1 1.1 copy-done.3
  81.2 2.8 %gate_up.1 = (f32[2,104,128]{2,1,0:T(8,128)S(1)}, bf16[2,104,128]{2,1,0:T(8,128)(2,1)S(1)}) custom-call(s32[3]{0:T(128)S(1)} %pad_add_fusion.place_ref, bf16[2,64,32,128]{3,2,1,0:T(8,128)(2,1)S(1)} %bitcast.11, bf16[2,64,32,128]{3,2,1,0:T(8,128)(2,1)S(1)} %bitcast.15, bf16[104,4096]{1,0:T(8,128)(2,1)S(1)} %copy-done.2, bf16[104,4096]{1,0:T(8,128)(2,1)S(1)} %copy-done.3), custom_call_target="tpu_custom_call" | custom-call | flops 436207616 | bytes 3801088 | tf_op jit(solution)/shard_map/gate_up/pallas_call | solution.py:77
  84.7 3.4 %collective-permute-start.3 = (bf16[2,104,128]{2,1,0:T(8,128)(2,1)S(1)}, bf16[2,104,128]{2,1,0:T(8,128)(2,1)S(1)}, u32[]{:S(2)}, u32[]{:S(2)}) collective-permute-start(bf16[2,104,128]{2,1,0:T(8,128)(2,1)S(1)} %get-tuple-element.17), channel_id=1, source_target_pairs={{0,1},{1,0},{2,3},{3,2},{4,5},{5,4},{6,7},{7,6},{8,9},{9,8},{10,11... | collective-permute-start | bytes 159752 | tf_op jit(solution)/shard_map/ppermute | solution.py:248
  88.2 1.6 copy.11
  89.8 1.6 copy.12
  92.9 2.5 %down.3 = (bf16[64,32,128]{2,1,0:T(8,128)(2,1)S(1)}, bf16[64,32,128]{2,1,0:T(8,128)(2,1)}) custom-call(s32[3]{0:T(128)S(1)} %pad_add_fusion.place_ref, bf16[104,128]{1,0:T(8,128)(2,1)S(1)} %copy-done.5, bf16[4096,104]{1,0:T(8,128)(2,1)S(1)} %bitcast.13), custom_call_target="tpu_custom_call" | custom-call | tf_op jit(solution)/shard_map/down/pallas_call | solution.py:127
  95.4 3.0 %collective-permute-start.5 = (bf16[64,32,128]{2,1,0:T(8,128)(2,1)}, bf16[64,32,128]{2,1,0:T(8,128)(2,1)}, u32[]{:S(2)}, u32[]{:S(2)}) collective-permute-start(bf16[64,32,128]{2,1,0:T(8,128)(2,1)} %get-tuple-element.22), channel_id=1, source_target_pairs={{0,2},{2,0},{1,3},{3,1},{4,6},{6,4},{5,7},{7,5},{8,10},{10,8},{9,1... | collective-permute-start | bytes 1572872 | tf_op jit(solution)/shard_map/ppermute | solution.py:253
  98.5 1.4 down.2
  99.9 1.9 %collective-permute-start.4 = (bf16[64,32,128]{2,1,0:T(8,128)(2,1)S(1)}, bf16[64,32,128]{2,1,0:T(8,128)(2,1)S(1)}, u32[]{:S(2)}, u32[]{:S(2)}) collective-permute-start(bf16[64,32,128]{2,1,0:T(8,128)(2,1)S(1)} %get-tuple-element.19), channel_id=1, source_target_pairs={{0,2},{2,0},{1,3},{3,1},{4,6},{6,4},{5,7},{7,5},{8,10},{10,8},{9,1... | collective-permute-start | bytes 1572872 | tf_op jit(solution)/shard_map/ppermute | solution.py:253
  101.9 1.8 %collective-permute-done.4 = bf16[64,32,128]{2,1,0:T(8,128)(2,1)S(1)} collective-permute-done((bf16[64,32,128]{2,1,0:T(8,128)(2,1)S(1)}, bf16[64,32,128]{2,1,0:T(8,128)(2,1)S(1)}, u32[]{:S(2)}, u32[]{:S(2)}) %collective-permute-start.4) | collective-permute-done | bytes 524320 | tf_op jit(solution)/shard_map/ppermute | solution.py:253
  103.7 1.4 broadcast_select_fusion.1
  105.1 1.1 pad_maximum_fusion
  106.2 14.7 %all-to-all-start.1 = ((bf16[128,32,128]{2,1,0:T(8,128)(2,1)}), bf16[128,32,128]{2,1,0:T(8,128)(2,1)S(1)}, u32[]{:S(2)}, u32[]{:S(2)}) async-start(bf16[128,32,128]{2,1,0:T(8,128)(2,1)} %pad_maximum_fusion), calls=%async_computation.1 | async-start | bytes 2097152 | tf_op jit(solution)/shard_map/all_to_all | solution.py:257
  120.9 2.5 %collective-permute-start.7 = (bf16[64,32,128]{2,1,0:T(8,128)(2,1)S(1)}, bf16[64,32,128]{2,1,0:T(8,128)(2,1)S(1)}, u32[]{:S(2)}, u32[]{:S(2)}) collective-permute-start(bf16[64,32,128]{2,1,0:T(8,128)(2,1)S(1)} %all-to-all-done.2), channel_id=1, source_target_pairs={{0,32},{32,0},{1,33},{33,1},{2,34},{34,2},{3,35},{35,3},{4,36},{36... | collective-permute-start | bytes 1572872 | tf_op jit(solution)/shard_map/ppermute | solution.py:259
  123.4 2.9 %collective-permute-start.6 = (bf16[64,32,128]{2,1,0:T(8,128)(2,1)S(1)}, bf16[64,32,128]{2,1,0:T(8,128)(2,1)S(1)}, u32[]{:S(2)}, u32[]{:S(2)}) collective-permute-start(bf16[64,32,128]{2,1,0:T(8,128)(2,1)S(1)} %all-to-all-done.2), channel_id=1, source_target_pairs={{0,2},{2,0},{1,3},{3,1},{4,6},{6,4},{5,7},{7,5},{8,10},{10,8},{9,1... | collective-permute-start | bytes 1572872 | tf_op jit(solution)/shard_map/ppermute | solution.py:262
  126.3 19.1 %collective-permute-done.7 = bf16[64,32,128]{2,1,0:T(8,128)(2,1)S(1)} collective-permute-done((bf16[64,32,128]{2,1,0:T(8,128)(2,1)S(1)}, bf16[64,32,128]{2,1,0:T(8,128)(2,1)S(1)}, u32[]{:S(2)}, u32[]{:S(2)}) %collective-permute-start.7) | collective-permute-done | bytes 524320 | tf_op jit(solution)/shard_map/ppermute | solution.py:259
  145.3 3.1 %collective-permute-start.8 = (bf16[64,32,128]{2,1,0:T(8,128)(2,1)S(1)}, bf16[64,32,128]{2,1,0:T(8,128)(2,1)S(1)}, u32[]{:S(2)}, u32[]{:S(2)}) collective-permute-start(bf16[64,32,128]{2,1,0:T(8,128)(2,1)S(1)} %collective-permute-done.7), channel_id=1, source_target_pairs={{0,2},{2,0},{1,3},{3,1},{4,6},{6,4},{5,7},{7,5},{8,10},{10,8},{9,1... | collective-permute-start | bytes 1572872 | tf_op jit(solution)/shard_map/ppermute | solution.py:262
  148.5 1.5 collective-permute-done.8
  150.0 1.0 copy-done.1
  151.0 1.0 copy-done.4
  152.1 2.4 %student.1 = (bf16[8192,128]{1,0:T(8,128)(2,1)S(1)}, f32[32,128]{1,0:T(8,128)S(1)}) custom-call(s32[3]{0:T(128)S(1)} %pad_add_fusion.place_ref, bf16[8,8,32,128]{3,2,1,0:T(8,128)(2,1)S(1)} %bitcast.14, bf16[8,8,32,128]{3,2,1,0:T(8,128)(2,1)S(1)} %bitcast.17, bf16[8,8,32,128]{3,2,1,0:T(8,128)(2,1)S(1)} %bitcast.16, bf16[8,8,32,128]{3,2,1,0:T(8,128)(2,1)S(1)} %bitcast.18, ...), custom_call_target="tpu_custom_call" | custom-call | flops 67108864 | bytes 4718592 | tf_op jit(solution)/shard_map/student/pallas_call | solution.py:166
  154.5 2.4 %gradient.1 = (bf16[32,128]{1,0:T(8,128)(2,1)}, bf16[32,8192]{1,0:T(8,128)(2,1)S(1)}) custom-call(bf16[128,32,128]{2,1,0:T(8,128)(2,1)S(1)} %all-to-all-done.1.terms_ref, f32[32,128]{1,0:T(8,128)S(1)} %get-tuple-element.23.student_out_ref, bf16[8192,128]{1,0:T(8,128)(2,1)S(1)} %get-tuple-element.24.student_ref), custom_call_target="tpu_custom_call" | custom-call | flops 67108864 | bytes 3670016 | tf_op jit(solution)/shard_map/gradient/pallas_call | solution.py:209
  156.9 4.0 %collective-permute-start.9 = (bf16[32,8192]{1,0:T(8,128)(2,1)S(1)}, bf16[32,8192]{1,0:T(8,128)(2,1)S(1)}, u32[]{:S(2)}, u32[]{:S(2)}) collective-permute-start(bf16[32,8192]{1,0:T(8,128)(2,1)S(1)} %get-tuple-element.26), channel_id=1, source_target_pairs={{0,1},{1,0},{2,3},{3,2},{4,5},{5,4},{6,7},{7,6},{8,9},{9,8},{10,11... | collective-permute-start | bytes 1572872 | tf_op jit(solution)/shard_map/ppermute | solution.py:266
  160.9 12.5 %collective-permute-done.9 = bf16[32,8192]{1,0:T(8,128)(2,1)S(1)} collective-permute-done((bf16[32,8192]{1,0:T(8,128)(2,1)S(1)}, bf16[32,8192]{1,0:T(8,128)(2,1)S(1)}, u32[]{:S(2)}, u32[]{:S(2)}) %collective-permute-start.9) | collective-permute-done | bytes 524320 | tf_op jit(solution)/shard_map/ppermute | solution.py:266
  173.5 0.9 add.11
  (28 shorter events, 3.2 us)
Async XLA Ops:
  0.6 31.6 %copy-start.9 = (bf16[104,4096]{1,0:T(8,128)(2,1)S(1)}, bf16[104,4096]{1,0:T(8,128)(2,1)}, u32[]{:S(2)}) copy-start(bf16[104,4096]{1,0:T(8,128)(2,1)} %param.9) | copy-start | bytes 2555908
  0.6 68.1 %copy-start.8 = (bf16[32,128]{1,0:T(8,128)(2,1)S(1)}, bf16[32,128]{1,0:T(8,128)(2,1)}, u32[]{:S(2)}) copy-start(bf16[32,128]{1,0:T(8,128)(2,1)} %rows_ref.1) | copy-start | bytes 24580
  0.7 1.5 collective-permute-start
  3.3 76.8 %copy-start.2 = (bf16[104,4096]{1,0:T(8,128)(2,1)S(1)}, bf16[104,4096]{1,0:T(8,128)(2,1)}, u32[]{:S(2)}) copy-start(bf16[104,4096]{1,0:T(8,128)(2,1)} %gate_ref.1) | copy-start | bytes 2555908
  3.3 61.3 %all-to-all-start = ((bf16[128,32,128]{2,1,0:T(8,128)(2,1)}), bf16[128,32,128]{2,1,0:T(8,128)(2,1)S(1)}, u32[]{:S(2)}, u32[]{:S(2)}) async-start(bf16[128,32,128]{2,1,0:T(8,128)(2,1)} %copies.2), calls=%async_computation | async-start | bytes 2097152 | tf_op jit(solution)/shard_map/all_to_all | solution.py:240
  32.3 32.3 %collective-permute-start.1 = (bf16[104,4096]{1,0:T(8,128)(2,1)S(1)}, bf16[104,4096]{1,0:T(8,128)(2,1)}, u32[]{:S(2)}, u32[]{:S(2)}) collective-permute-start(bf16[104,4096]{1,0:T(8,128)(2,1)S(1)} %copy-done.9), channel_id=1, source_target_pairs={{0,1},{1,0},{2,3},{3,2},{4,5},{5,4},{6,7},{7,6},{8,9},{9,8},{10,11... | collective-permute-start | bytes 2555912 | tf_op jit(solution)/shard_map/ppermute | solution.py:239
  64.5 15.5 %collective-permute-start.2 = (bf16[128,32,128]{2,1,0:T(8,128)(2,1)S(1)}, bf16[128,32,128]{2,1,0:T(8,128)(2,1)S(1)}, u32[]{:S(2)}, u32[]{:S(2)}) collective-permute-start(bf16[128,32,128]{2,1,0:T(8,128)(2,1)S(1)} %all-to-all-done._), channel_id=1, source_target_pairs={{0,2},{2,0},{1,3},{3,1},{4,6},{6,4},{5,7},{7,5},{8,10},{10,8},{9,1... | collective-permute-start | bytes 3145736 | tf_op jit(solution)/shard_map/ppermute | solution.py:242
  69.6 36.6 %all-to-all-start.2 = ((bf16[64,32,128]{2,1,0:T(8,128)(2,1)}), bf16[64,32,128]{2,1,0:T(8,128)(2,1)S(1)}, u32[]{:S(2)}, u32[]{:S(2)}) async-start(bf16[64,32,128]{2,1,0:T(8,128)(2,1)} %copies.3), calls=%async_computation.2 | async-start | bytes 1048576 | tf_op jit(solution)/shard_map/all_to_all | solution.py:245
  80.1 1.2 copy-start.3
  84.1 0.6 copy-start.6
  84.7 6.8 %copy-start.7 = (f32[2,104,128]{2,1,0:T(8,128)S(1)}, f32[2,104,128]{2,1,0:T(8,128)}, u32[]{:S(2)}) copy-start(f32[2,104,128]{2,1,0:T(8,128)} %copy-done.6) | copy-start | bytes 319492
  84.7 6.8 %collective-permute-start.3 = (bf16[2,104,128]{2,1,0:T(8,128)(2,1)S(1)}, bf16[2,104,128]{2,1,0:T(8,128)(2,1)S(1)}, u32[]{:S(2)}, u32[]{:S(2)}) collective-permute-start(bf16[2,104,128]{2,1,0:T(8,128)(2,1)S(1)} %get-tuple-element.17), channel_id=1, source_target_pairs={{0,1},{1,0},{2,3},{3,2},{4,5},{5,4},{6,7},{7,6},{8,9},{9,8},{10,11... | collective-permute-start | bytes 159752 | tf_op jit(solution)/shard_map/ppermute | solution.py:248
  92.2 0.7 copy-start.5
  95.4 6.4 %collective-permute-start.5 = (bf16[64,32,128]{2,1,0:T(8,128)(2,1)}, bf16[64,32,128]{2,1,0:T(8,128)(2,1)}, u32[]{:S(2)}, u32[]{:S(2)}) collective-permute-start(bf16[64,32,128]{2,1,0:T(8,128)(2,1)} %get-tuple-element.22), channel_id=1, source_target_pairs={{0,2},{2,0},{1,3},{3,1},{4,6},{6,4},{5,7},{7,5},{8,10},{10,8},{9,1... | collective-permute-start | bytes 1572872 | tf_op jit(solution)/shard_map/ppermute | solution.py:253
  99.9 3.8 %collective-permute-start.4 = (bf16[64,32,128]{2,1,0:T(8,128)(2,1)S(1)}, bf16[64,32,128]{2,1,0:T(8,128)(2,1)S(1)}, u32[]{:S(2)}, u32[]{:S(2)}) collective-permute-start(bf16[64,32,128]{2,1,0:T(8,128)(2,1)S(1)} %get-tuple-element.19), channel_id=1, source_target_pairs={{0,2},{2,0},{1,3},{3,1},{4,6},{6,4},{5,7},{7,5},{8,10},{10,8},{9,1... | collective-permute-start | bytes 1572872 | tf_op jit(solution)/shard_map/ppermute | solution.py:253
  106.2 43.8 %copy-start = (bf16[64,32,128]{2,1,0:T(8,128)(2,1)}, bf16[64,32,128]{2,1,0:T(8,128)(2,1)S(1)}, u32[]{:S(2)}) copy-start(bf16[64,32,128]{2,1,0:T(8,128)(2,1)S(1)} %all-to-all-done.2) | copy-start | bytes 1572868
  106.2 48.3 %all-to-all-start.1 = ((bf16[128,32,128]{2,1,0:T(8,128)(2,1)}), bf16[128,32,128]{2,1,0:T(8,128)(2,1)S(1)}, u32[]{:S(2)}, u32[]{:S(2)}) async-start(bf16[128,32,128]{2,1,0:T(8,128)(2,1)} %pad_maximum_fusion), calls=%async_computation.1 | async-start | bytes 2097152 | tf_op jit(solution)/shard_map/all_to_all | solution.py:257
  120.9 24.5 %collective-permute-start.7 = (bf16[64,32,128]{2,1,0:T(8,128)(2,1)S(1)}, bf16[64,32,128]{2,1,0:T(8,128)(2,1)S(1)}, u32[]{:S(2)}, u32[]{:S(2)}) collective-permute-start(bf16[64,32,128]{2,1,0:T(8,128)(2,1)S(1)} %all-to-all-done.2), channel_id=1, source_target_pairs={{0,32},{32,0},{1,33},{33,1},{2,34},{34,2},{3,35},{35,3},{4,36},{36... | collective-permute-start | bytes 1572872 | tf_op jit(solution)/shard_map/ppermute | solution.py:259
  123.4 25.1 %collective-permute-start.6 = (bf16[64,32,128]{2,1,0:T(8,128)(2,1)S(1)}, bf16[64,32,128]{2,1,0:T(8,128)(2,1)S(1)}, u32[]{:S(2)}, u32[]{:S(2)}) collective-permute-start(bf16[64,32,128]{2,1,0:T(8,128)(2,1)S(1)} %all-to-all-done.2), channel_id=1, source_target_pairs={{0,2},{2,0},{1,3},{3,1},{4,6},{6,4},{5,7},{7,5},{8,10},{10,8},{9,1... | collective-permute-start | bytes 1572872 | tf_op jit(solution)/shard_map/ppermute | solution.py:262
  145.3 4.7 %collective-permute-start.8 = (bf16[64,32,128]{2,1,0:T(8,128)(2,1)S(1)}, bf16[64,32,128]{2,1,0:T(8,128)(2,1)S(1)}, u32[]{:S(2)}, u32[]{:S(2)}) collective-permute-start(bf16[64,32,128]{2,1,0:T(8,128)(2,1)S(1)} %collective-permute-done.7), channel_id=1, source_target_pairs={{0,2},{2,0},{1,3},{3,1},{4,6},{6,4},{5,7},{7,5},{8,10},{10,8},{9,1... | collective-permute-start | bytes 1572872 | tf_op jit(solution)/shard_map/ppermute | solution.py:262
  150.0 1.0 copy-start.1
  151.0 1.0 copy-start.4
  156.9 16.5 %collective-permute-start.9 = (bf16[32,8192]{1,0:T(8,128)(2,1)S(1)}, bf16[32,8192]{1,0:T(8,128)(2,1)S(1)}, u32[]{:S(2)}, u32[]{:S(2)}) collective-permute-start(bf16[32,8192]{1,0:T(8,128)(2,1)S(1)} %get-tuple-element.26), channel_id=1, source_target_pairs={{0,1},{1,0},{2,3},{3,2},{4,5},{5,4},{6,7},{7,6},{8,9},{9,8},{10,11... | collective-permute-start | bytes 1572872 | tf_op jit(solution)/shard_map/ppermute | solution.py:266

commit v3 on v2

--- a/solution.py
+++ b/solution.py
@@ -93,60 +93,62 @@
     )(place, own, other, gate, up)
 
 
-def hidden_kernel(keep_ref, got_ref, out_ref):
-    preact, uppre = (keep_ref[i] + got_ref[i].astype(F32) for i in range(2))
-    out_ref[...] = (preact / (1 + jnp.exp(-preact)) * uppre).astype(BF16)
-
-
-def hidden_part(keep, got):
-    return pl.pallas_call(
-        hidden_kernel,
-        out_shape=jax.ShapeDtypeStruct(keep.shape[1:], BF16),
-        compiler_params=PARAMS,
-        cost_estimate=cost(0, 0),
-        name="hidden",
-    )(keep, got)
-
-
-def down_kernel(place_ref, hidden_ref, down_ref, mine_ref, theirs_ref):
+def down_kernel(place_ref, keep_ref, got_ref, near_ref, far_ref, hidden_ref, mine_ref, theirs_ref):
+    side, step = pl.program_id(0), pl.program_id(1)
     core = place_ref[0]
-    count, rows, tokens = mine_ref.shape
-    out = jnp.dot(down_ref[...], hidden_ref[...], preferred_element_type=F32).astype(BF16)
-    out = out.reshape(count, 2, rows, tokens)
-    even, odd = out[:, 0], out[:, 1]
-    mine_ref[...] = jnp.where(core == 0, even, odd)
-    theirs_ref[...] = jnp.where(core == 0, odd, even)
-
-
-def down_part(place, hidden_units, down, rows, steps=4):
-    width, hidden = down.shape
-    tokens = hidden_units.shape[-1]
+
+    @pl.when((side == 0) & (step == 0))
+    def _():
+        preact, uppre = (keep_ref[i] + got_ref[i].astype(F32) for i in range(2))
+        hidden_ref[...] = (preact / (1 + jnp.exp(-preact)) * uppre).astype(BF16)
+
+    def part(ref):
+        out = jnp.dot(ref[...], hidden_ref[...], preferred_element_type=F32).astype(BF16)
+        count, rows, tokens = mine_ref.shape[1:]
+        out = out.reshape(count, 2, rows, tokens)
+        even, odd = out[:, 0], out[:, 1]
+        mine_ref[0] = jnp.where(core == 0, even, odd)
+        theirs_ref[0] = jnp.where(core == 0, odd, even)
+
+    pl.when(side == 0)(lambda: part(near_ref))
+    pl.when(side == 1)(lambda: part(far_ref))
+
+
+def down_part(place, keep, got, near, far, rows, steps=2):
+    width, hidden = near.shape
+    tokens = keep.shape[-1]
     count = width // (2 * rows)
-    block = pl.BlockSpec((count // steps, rows, tokens), lambda k, _: (k, 0, 0))
-    out = jax.ShapeDtypeStruct((count, rows, tokens), BF16)
-    return pl.pallas_call(
+    whole = pl.BlockSpec((2, hidden, tokens), lambda s, k, _: (0, 0, 0))
+    block = pl.BlockSpec(
+        (1, count // steps, rows, tokens), lambda s, k, p: ((s + p[1]) % 2, k, 0, 0)
+    )
+    out = jax.ShapeDtypeStruct((2, count, rows, tokens), BF16)
+    hidden_units, mine, theirs = pl.pallas_call(
         down_kernel,
         grid_spec=pltpu.PrefetchScalarGridSpec(
             num_scalar_prefetch=1,
-            grid=(steps,),
+            grid=(2, steps),
             in_specs=[
-                pl.BlockSpec((hidden, tokens), lambda k, _: (0, 0)),
-                pl.BlockSpec((width // steps, hidden), lambda k, _: (k, 0)),
+                whole,
+                whole,
+                pl.BlockSpec((width // steps, hidden), lambda s, k, _: (jnp.where(s == 0, k, steps - 1), 0)),
+                pl.BlockSpec((width // steps, hidden), lambda s, k, _: (jnp.where(s == 1, k, 0), 0)),
             ],
-            out_specs=[block, block],
+            out_specs=[pl.BlockSpec((hidden, tokens), lambda s, k, _: (0, 0)), block, block],
         ),
-        out_shape=[out, out],
+        out_shape=[jax.ShapeDtypeStruct((hidden, tokens), BF16), out, out],
         compiler_params=PARAMS,
         cost_estimate=cost(0, 0),
         name="down",
-    )(place, hidden_units, down)
-
-
-def student_kernel(place_ref, own_ref, own_core_ref, next_ref, next_core_ref, projector_ref, all_ref, out_ref):
-    core, x = place_ref[0], place_ref[2]
-    here = zip_cores(core, own_ref[0], own_core_ref[0])
-    there = zip_cores(core, next_ref[0], next_core_ref[0])
-    rows = jnp.concatenate([jnp.where(x == 0, here, there), jnp.where(x == 0, there, here)])
+    )(place, keep, got, near, far)
+    return hidden_units, *(a.reshape(2 * count, rows, tokens) for a in (mine, theirs))
+
+
+def student_kernel(gathered_ref, projector_ref, all_ref, out_ref):
+    columns, count, rows, tokens = gathered_ref.shape
+    rows = jnp.concatenate(
+        [gathered_ref[:, i].reshape(columns * rows, tokens) for i in range(count)]
+    )
     all_ref[...] = rows
     part = jnp.dot(projector_ref[...], rows, preferred_element_type=F32)
 
@@ -159,21 +161,20 @@
         out_ref[...] += part
 
 
-def student_part(place, pieces, projector):
-    steps, count, rows, tokens = pieces[0].shape
+def student_part(gathered, projector, steps=8):
+    columns, count, rows, tokens = gathered.shape
     mine, width = projector.shape
-    block = pl.BlockSpec((1, count, rows, tokens), lambda k, _: (k, 0, 0, 0))
     return pl.pallas_call(
         student_kernel,
-        grid_spec=pltpu.PrefetchScalarGridSpec(
-            num_scalar_prefetch=1,
-            grid=(steps,),
-            in_specs=[block] * 4 + [pl.BlockSpec((mine, width // steps), lambda k, _: (0, k))],
-            out_specs=[
-                pl.BlockSpec((width // steps, tokens), lambda k, _: (k, 0)),
-                pl.BlockSpec((mine, tokens), lambda k, _: (0, 0)),
-            ],
-        ),
+        grid=(steps,),
+        in_specs=[
+            pl.BlockSpec((columns, count // steps, rows, tokens), lambda k: (0, k, 0, 0)),
+            pl.BlockSpec((mine, width // steps), lambda k: (0, k)),
+        ],
+        out_specs=[
+            pl.BlockSpec((width // steps, tokens), lambda k: (k, 0)),
+            pl.BlockSpec((mine, tokens), lambda k: (0, 0)),
+        ],
         out_shape=[
             jax.ShapeDtypeStruct((width, tokens), BF16),
             jax.ShapeDtypeStruct((mine, tokens), F32),
@@ -181,7 +182,7 @@
         compiler_params=PARAMS,
         cost_estimate=cost(2 * mine * width * tokens, 4 * width * tokens + 2 * mine * width),
         name="student",
-    )(place, *pieces, projector)
+    )(gathered, projector)
 
 
 def grad_kernel(terms_ref, student_out_ref, student_ref, residual_ref, grad_ref, rows_ref, sem_ref):
@@ -225,7 +226,7 @@
 
 
 def shards(teacher_rows, teacher_gate, teacher_up, teacher_down, student_rows, projector):
-    place = jnp.stack([lax.axis_index(name) for name in ("core", "dp", "x")]).astype(jnp.int32)
+    place = jnp.stack([lax.axis_index(name) for name in ("core", "dp")]).astype(jnp.int32)
     rows = teacher_rows.shape[0]
     chips = lax.axis_size(CHIPS)
     across = lax.axis_size("y") // 2
@@ -236,32 +237,28 @@
         low, high = 2 * y, 2 * (y + across)
         trade += [(low, low), (low + 1, high), (high, low + 1), (high + 1, high + 1)]
     held = lax.ppermute(teacher_rows, ("y", "dp"), trade)
-    down_far = lax.ppermute(teacher_down, "dp", SWAP)
+    quarter = teacher_down.shape[1] // 4
+    far = [lax.ppermute(teacher_down[:, :quarter], "dp", SWAP)]
+    held, far[0] = lax.optimization_barrier((held, far[0]))
+    far.append(lax.ppermute(teacher_down[:, quarter:], "dp", SWAP))
     teacher_own = spread(copies(held, held, chips), CHIPS)
-    teacher_own, down_far = lax.optimization_barrier((teacher_own, down_far))
+    student_part_rows = lax.all_gather(student_rows, ("y", "x"), axis=0)
+    teacher_own, far[1], student_part_rows = lax.optimization_barrier(
+        (teacher_own, far[1], student_part_rows)
+    )
     teacher_other = lax.ppermute(teacher_own, "core", SWAP)
-
-    plane = ("y", "z")
-    student_own = spread(copies(student_rows, teacher_own, lax.axis_size(plane)), plane)
+    student_gathered = lax.all_gather(student_part_rows, ("z", "core"), axis=0)
 
     keep, send = up_part(place, teacher_own, teacher_other, teacher_gate, teacher_up)
     got = lax.ppermute(send, "dp", SWAP)
-    teacher_hidden = hidden_part(keep, got)
-    sums = []
-    for down in (teacher_down, down_far):
-        mine, theirs = down_part(place, teacher_hidden, down.T, rows)
-        sums.append((mine.astype(F32) + lax.ppermute(theirs, "core", SWAP).astype(F32)).astype(BF16))
-    near, far = sums
-    first = place[1] == 0
-    chip_sum = jnp.concatenate([jnp.where(first, near, far), jnp.where(first, far, near)])
+    down_far = jnp.concatenate([part.T for part in far])
+    teacher_hidden, mine, theirs = down_part(place, keep, got, teacher_down.T, down_far, rows)
+    chip_sum = (
+        mine.astype(F32) + lax.ppermute(theirs, "core", SWAP).astype(F32)
+    ).astype(BF16)
     terms = spread(chip_sum, CHIPS)
 
-    student_next = lax.ppermute(student_own, "x", SWAP)
-    pieces = []
-    for piece in (student_own, student_next):
-        pieces += [piece, lax.ppermute(piece, "core", SWAP)]
-    pieces = [a.reshape(lax.axis_size("y"), -1, *a.shape[1:]) for a in pieces]
-    student_all, student_out = student_part(place, pieces, projector)
+    student_all, student_out = student_part(student_gathered, projector)
     residual_error, grad_local = grad_part(terms, student_out, student_all)
     grad_projector = grad_local + lax.ppermute(grad_local, "dp", SWAP)
     return (teacher_hidden, residual_error, grad_projector)

time: 175 us -> 196 us (1.12)
  the two profiles are of different devices: /device:TPU:1 before, /device:TPU:8 now
where the time goes in v3:
time: 196 us; the launch traced here: 195 us
  starting transfers between devices  54.8 us (28%)
  blocking collectives  52.3 us (27%)
  waiting for transfers between devices  51.5 us (26%)
  between operations  14.2 us (7%)
  Pallas kernels  10.5 us (5%)
  local copies, waits for them, and re-layouts  8.85 us (5%)
  other arithmetic  2.53 us (1%)
    all_gather x1, blocking collectives, shards(): student_part_rows = lax.all_gather(student_rows, ('y', 'x'), axis=0)  52.3 us
    all_to_all x1, starting transfers between devices, shards(): teacher_own = spread(copies(held, held, chips), CHIPS)  22.8 us
    all_gather x1, waiting for transfers between devices, shards(): student_gathered = lax.all_gather(student_part_rows, ('z', 'core'), axis=0)  15.3 us
    all_to_all x1, starting transfers between devices, shards(): terms = spread(chip_sum, CHIPS)  12.9 us
    ppermute x1, waiting for transfers between devices, shards(): grad_projector = grad_local + lax.ppermute(grad_local, 'dp', SWAP)  12.1 us
    all_to_all x1, waiting for transfers between devices, shards(): terms = spread(chip_sum, CHIPS)  11.6 us
    unnamed x17, local copies, waits for them, and re-layouts  6.55 us
    ppermute x1, waiting for transfers between devices, shards(): far = [lax.ppermute(teacher_down[:, :quarter], 'dp', SWAP)]  5.81 us
  transfers between devices with their start and end apart: 10, of which 7 were waited for; matrix products, arithmetic and copies ran while one was open for 2% of the time, Pallas kernels for 4%

profile of v3, /device:TPU:8, one launch (start us, length us, event | category | flops | bytes accessed | tf_op | source)
XLA Modules:
  0.0 194.7 jit_solution(411950868586080432)
XLA Ops:
  7.2 1.6 copy.12
  8.8 5.1 %collective-permute-start.1 = (bf16[104,1024]{0,1:T(8,128)(2,1)S(1)}, bf16[104,1024]{0,1:T(8,128)(2,1)S(1)}, u32[]{:S(2)}, u32[]{:S(2)}) collective-permute-start(bf16[104,1024]{0,1:T(8,128)(2,1)S(1)} %slice.8), channel_id=1, source_target_pairs={{0,1},{1,0},{2,3},{3,2},{4,5},{5,4},{6,7},{7,6},{8,9},{9,8},{10,11... | collective-permute-start | bytes 638984 | tf_op jit(solution)/shard_map/ppermute | solution.py:241
  13.9 0.7 collective-permute-start
  14.6 5.8 %collective-permute-done.1 = bf16[104,1024]{0,1:T(8,128)(2,1)S(1)} collective-permute-done((bf16[104,1024]{0,1:T(8,128)(2,1)S(1)}, bf16[104,1024]{0,1:T(8,128)(2,1)S(1)}, u32[]{:S(2)}, u32[]{:S(2)}) %collective-permute-start.1) | collective-permute-done | bytes 213024 | tf_op jit(solution)/shard_map/ppermute | solution.py:241
  20.4 1.1 copies.1
  21.5 22.8 %all-to-all-start = ((bf16[128,32,128]{2,1,0:T(8,128)(2,1)}), bf16[128,32,128]{2,1,0:T(8,128)(2,1)S(1)}, u32[]{:S(2)}, u32[]{:S(2)}) async-start(bf16[128,32,128]{2,1,0:T(8,128)(2,1)} %copies.1), calls=%async_computation | async-start | bytes 2097152 | tf_op jit(solution)/shard_map/all_to_all | solution.py:244
  44.4 1.9 collective-permute-start.2
  46.4 52.3 %all-gather = bf16[512,128]{1,0:T(8,128)(2,1)} all-gather(bf16[32,128]{1,0:T(8,128)(2,1)S(1)} %copy-done.6), channel_id=2, replica_groups=mesh['y'=8,'x'=2,'z'=8,'core'=2,'dp'=2] {'y','x'}, dimensions={0}, use_global_device_ids=true | all-gather | bytes 139264 | tf_op jit(solution)/shard_map/all_gather | solution.py:245
  98.7 1.9 collective-permute-start.3
  100.6 0.1 pad_add_fusion.place_ref
  100.7 2.2 %copy.14 = bf16[104,3072]{0,1:T(8,128)(2,1)} copy(bf16[104,3072]{1,0:T(8,128)(2,1)} %collective-permute-done.2) | data formatting | bytes 1277952 | tf_op jit(solution)/shard_map/optimization_barrier | solution.py:246
  103.0 0.3 collective-permute-done.3
  103.3 1.2 copy-done.1
  104.4 1.2 copy-done.2
  105.6 2.8 %gate_up.1 = (f32[2,104,128]{2,1,0:T(8,128)S(1)}, bf16[2,104,128]{2,1,0:T(8,128)(2,1)S(1)}) custom-call(s32[2]{0:T(128)S(1)} %pad_add_fusion.place_ref, bf16[2,64,32,128]{3,2,1,0:T(8,128)(2,1)S(1)} %bitcast.14, bf16[2,64,32,128]{3,2,1,0:T(8,128)(2,1)S(1)} %bitcast.16, bf16[104,4096]{1,0:T(8,128)(2,1)S(1)} %copy-done.1, bf16[104,4096]{1,0:T(8,128)(2,1)S(1)} %copy-done.2), custom_call_target="tpu_custom_call" | custom-call | flops 436207616 | bytes 3801088 | tf_op jit(solution)/shard_map/gate_up/pallas_call | solution.py:77
  108.4 3.5 %collective-permute-start.4 = (bf16[2,104,128]{2,1,0:T(8,128)(2,1)S(1)}, bf16[2,104,128]{2,1,0:T(8,128)(2,1)S(1)}, u32[]{:S(2)}, u32[]{:S(2)}) collective-permute-start(bf16[2,104,128]{2,1,0:T(8,128)(2,1)S(1)} %get-tuple-element.20), channel_id=1, source_target_pairs={{0,1},{1,0},{2,3},{3,2},{4,5},{5,4},{6,7},{7,6},{8,9},{9,8},{10,11... | collective-permute-start | bytes 159752 | tf_op jit(solution)/shard_map/ppermute | solution.py:253
  111.9 0.2 pad_maximum_fusion.far_ref
  112.1 3.8 %collective-permute-done.4.got_ref = bf16[2,104,128]{2,1,0:T(8,128)(2,1)S(1)} collective-permute-done((bf16[2,104,128]{2,1,0:T(8,128)(2,1)S(1)}, bf16[2,104,128]{2,1,0:T(8,128)(2,1)S(1)}, u32[]{:S(2)}, u32[]{:S(2)}) %collective-permute-start.4) | collective-permute-done | bytes 53280 | tf_op jit(solution)/shard_map/ppermute | solution.py:253
  115.9 2.4 %down.1 = (bf16[104,128]{1,0:T(8,128)(2,1)}, bf16[2,64,32,128]{3,2,1,0:T(8,128)(2,1)S(1)}, bf16[2,64,32,128]{3,2,1,0:T(8,128)(2,1)S(1)}) custom-call(s32[2]{0:T(128)S(1)} %pad_add_fusion.place_ref, f32[2,104,128]{2,1,0:T(8,128)S(1)} %get-tuple-element.19.keep_ref, bf16[2,104,128]{2,1,0:T(8,128)(2,1)S(1)} %collective-permute-done.4.got_ref, ...), custom_call_target="tpu_custom_call" | custom-call | tf_op jit(solution)/shard_map/down/pallas_call | solution.py:126
  118.4 1.9 collective-permute-start.5
  120.3 2.6 %collective-permute-done.5 = bf16[128,32,128]{2,1,0:T(8,128)(2,1)S(1)} collective-permute-done((bf16[128,32,128]{2,1,0:T(8,128)(2,1)S(1)}, bf16[128,32,128]{2,1,0:T(8,128)(2,1)S(1)}, u32[]{:S(2)}, u32[]{:S(2)}) %collective-permute-start.5) | collective-permute-done | bytes 1048608 | tf_op jit(solution)/shard_map/ppermute | solution.py:257
  122.9 1.3 fusion
  124.3 12.9 %all-to-all-start.1 = ((bf16[128,32,128]{2,1,0:T(8,128)(2,1)}), bf16[128,32,128]{2,1,0:T(8,128)(2,1)S(1)}, u32[]{:S(2)}, u32[]{:S(2)}) async-start(bf16[128,32,128]{2,1,0:T(8,128)(2,1)} %fusion), calls=%async_computation.1 | async-start | bytes 2097152 | tf_op jit(solution)/shard_map/all_to_all | solution.py:259
  137.1 15.3 %all-gather.4.cloned.1.call-done = bf16[256,32,128]{2,1,0:T(8,128)(2,1)} async-done(((bf16[16,32,128]{2,1,0:T(8,128)(2,1)}), bf16[256,32,128]{2,1,0:T(8,128)(2,1)}) %all-gather.4.cloned.1.call-update) | async-done | bytes 2097168 | tf_op jit(solution)/shard_map/all_gather | solution.py:250
  152.4 1.6 copy-done
  154.0 1.0 copy-done.3
  155.0 1.7 student.1
  156.7 11.6 %all-to-all-done.1.terms_ref = bf16[128,32,128]{2,1,0:T(8,128)(2,1)S(1)} async-done(((bf16[128,32,128]{2,1,0:T(8,128)(2,1)}), bf16[128,32,128]{2,1,0:T(8,128)(2,1)S(1)}, u32[]{:S(2)}, u32[]{:S(2)}) %all-to-all-start.1) | async-done | bytes 1048608 | tf_op jit(solution)/shard_map/all_to_all | solution.py:259
  168.3 2.4 %gradient.1 = (bf16[32,128]{1,0:T(8,128)(2,1)}, bf16[32,8192]{1,0:T(8,128)(2,1)S(1)}) custom-call(bf16[128,32,128]{2,1,0:T(8,128)(2,1)S(1)} %all-to-all-done.1.terms_ref, f32[32,128]{1,0:T(8,128)S(1)} %get-tuple-element.27.student_out_ref, bf16[8192,128]{1,0:T(8,128)(2,1)S(1)} %get-tuple-element.28.student_ref), custom_call_target="tpu_custom_call" | custom-call | flops 67108864 | bytes 3670016 | tf_op jit(solution)/shard_map/gradient/pallas_call | solution.py:210
  170.7 4.2 %collective-permute-start.6 = (bf16[32,8192]{1,0:T(8,128)(2,1)S(1)}, bf16[32,8192]{1,0:T(8,128)(2,1)S(1)}, u32[]{:S(2)}, u32[]{:S(2)}) collective-permute-start(bf16[32,8192]{1,0:T(8,128)(2,1)S(1)} %get-tuple-element.30), channel_id=1, source_target_pairs={{0,1},{1,0},{2,3},{3,2},{4,5},{5,4},{6,7},{7,6},{8,9},{9,8},{10,11... | collective-permute-start | bytes 1572872 | tf_op jit(solution)/shard_map/ppermute | solution.py:263
  174.9 12.1 %collective-permute-done.6 = bf16[32,8192]{1,0:T(8,128)(2,1)S(1)} collective-permute-done((bf16[32,8192]{1,0:T(8,128)(2,1)S(1)}, bf16[32,8192]{1,0:T(8,128)(2,1)S(1)}, u32[]{:S(2)}, u32[]{:S(2)}) %collective-permute-start.6) | collective-permute-done | bytes 524320 | tf_op jit(solution)/shard_map/ppermute | solution.py:263
  187.0 0.9 add.7
  (19 shorter events, 0.2 us)
Async XLA Ops:
  7.2 6.7 %copy-start.7 = (bf16[32,128]{1,0:T(8,128)(2,1)S(1)}, bf16[32,128]{1,0:T(8,128)(2,1)}, u32[]{:S(2)}) copy-start(bf16[32,128]{1,0:T(8,128)(2,1)} %param.6) | copy-start | bytes 24580
  8.8 35.6 %copy-start.5 = (bf16[104,4096]{1,0:T(8,128)(2,1)S(1)}, bf16[104,4096]{1,0:T(8,128)(2,1)}, u32[]{:S(2)}) copy-start(bf16[104,4096]{1,0:T(8,128)(2,1)} %param.9) | copy-start | bytes 2555908
  8.8 37.5 %copy-start.6 = (bf16[32,128]{1,0:T(8,128)(2,1)S(1)}, bf16[32,128]{1,0:T(8,128)(2,1)}, u32[]{:S(2)}) copy-start(bf16[32,128]{1,0:T(8,128)(2,1)} %param.10) | copy-start | bytes 24580
  8.8 11.6 %collective-permute-start.1 = (bf16[104,1024]{0,1:T(8,128)(2,1)S(1)}, bf16[104,1024]{0,1:T(8,128)(2,1)S(1)}, u32[]{:S(2)}, u32[]{:S(2)}) collective-permute-start(bf16[104,1024]{0,1:T(8,128)(2,1)S(1)} %slice.8), channel_id=1, source_target_pairs={{0,1},{1,0},{2,3},{3,2},{4,5},{5,4},{6,7},{7,6},{8,9},{9,8},{10,11... | collective-permute-start | bytes 638984 | tf_op jit(solution)/shard_map/ppermute | solution.py:241
  13.9 0.7 collective-permute-start
  21.5 77.2 %all-to-all-start = ((bf16[128,32,128]{2,1,0:T(8,128)(2,1)}), bf16[128,32,128]{2,1,0:T(8,128)(2,1)S(1)}, u32[]{:S(2)}, u32[]{:S(2)}) async-start(bf16[128,32,128]{2,1,0:T(8,128)(2,1)} %copies.1), calls=%async_computation | async-start | bytes 2097152 | tf_op jit(solution)/shard_map/all_to_all | solution.py:244
  44.3 108.1 %all-gather.4.cloned.1.call-start = ((), (), s32[]{:S(2)}) async-start(), calls=%async_computation.2 | async-start | bytes 2228224 | tf_op jit(solution)/shard_map/all_gather | solution.py:250
  44.4 54.3 %collective-permute-start.2 = (bf16[104,3072]{1,0:T(8,128)(2,1)S(1)}, bf16[104,3072]{1,0:T(8,128)(2,1)}, u32[]{:S(2)}, u32[]{:S(2)}) collective-permute-start(bf16[104,3072]{1,0:T(8,128)(2,1)S(1)} %slice.7), channel_id=1, source_target_pairs={{0,1},{1,0},{2,3},{3,2},{4,5},{5,4},{6,7},{7,6},{8,9},{9,8},{10,11... | collective-permute-start | bytes 1916936 | tf_op jit(solution)/shard_map/ppermute | solution.py:243
  98.7 4.5 %collective-permute-start.3 = (bf16[128,32,128]{2,1,0:T(8,128)(2,1)S(1)}, bf16[128,32,128]{2,1,0:T(8,128)(2,1)S(1)}, u32[]{:S(2)}, u32[]{:S(2)}) collective-permute-start(bf16[128,32,128]{2,1,0:T(8,128)(2,1)S(1)} %all-to-all-done), channel_id=1, source_target_pairs={{0,2},{2,0},{1,3},{3,1},{4,6},{6,4},{5,7},{7,5},{8,10},{10,8},{9,1... | collective-permute-start | bytes 3145736 | tf_op jit(solution)/shard_map/ppermute | solution.py:249
  103.3 1.2 copy-start.1
  104.4 1.2 copy-start.2
  105.6 6.3 %copy-start.4 = (bf16[104,3072]{0,1:T(8,128)(2,1)S(1)}, bf16[104,3072]{0,1:T(8,128)(2,1)}, u32[]{:S(2)}) copy-start(bf16[104,3072]{0,1:T(8,128)(2,1)} %copy.14) | copy-start | bytes 1916932
  108.4 7.5 %collective-permute-start.4 = (bf16[2,104,128]{2,1,0:T(8,128)(2,1)S(1)}, bf16[2,104,128]{2,1,0:T(8,128)(2,1)S(1)}, u32[]{:S(2)}, u32[]{:S(2)}) collective-permute-start(bf16[2,104,128]{2,1,0:T(8,128)(2,1)S(1)} %get-tuple-element.20), channel_id=1, source_target_pairs={{0,1},{1,0},{2,3},{3,2},{4,5},{5,4},{6,7},{7,6},{8,9},{9,8},{10,11... | collective-permute-start | bytes 159752 | tf_op jit(solution)/shard_map/ppermute | solution.py:253
  118.4 4.5 %collective-permute-start.5 = (bf16[128,32,128]{2,1,0:T(8,128)(2,1)S(1)}, bf16[128,32,128]{2,1,0:T(8,128)(2,1)S(1)}, u32[]{:S(2)}, u32[]{:S(2)}) collective-permute-start(bf16[128,32,128]{2,1,0:T(8,128)(2,1)S(1)} %bitcast.17), channel_id=1, source_target_pairs={{0,2},{2,0},{1,3},{3,1},{4,6},{6,4},{5,7},{7,5},{8,10},{10,8},{9,1... | collective-permute-start | bytes 3145736 | tf_op jit(solution)/shard_map/ppermute | solution.py:257
  124.3 44.0 %all-to-all-start.1 = ((bf16[128,32,128]{2,1,0:T(8,128)(2,1)}), bf16[128,32,128]{2,1,0:T(8,128)(2,1)S(1)}, u32[]{:S(2)}, u32[]{:S(2)}) async-start(bf16[128,32,128]{2,1,0:T(8,128)(2,1)} %fusion), calls=%async_computation.1 | async-start | bytes 2097152 | tf_op jit(solution)/shard_map/all_to_all | solution.py:259
  152.4 1.6 copy-start
  154.0 1.0 copy-start.3
  170.7 16.3 %collective-permute-start.6 = (bf16[32,8192]{1,0:T(8,128)(2,1)S(1)}, bf16[32,8192]{1,0:T(8,128)(2,1)S(1)}, u32[]{:S(2)}, u32[]{:S(2)}) collective-permute-start(bf16[32,8192]{1,0:T(8,128)(2,1)S(1)} %get-tuple-element.30), channel_id=1, source_target_pairs={{0,1},{1,0},{2,3},{3,2},{4,5},{5,4},{6,7},{7,6},{8,9},{9,8},{10,11... | collective-permute-start | bytes 1572872 | tf_op jit(solution)/shard_map/ppermute | solution.py:263
Sparse Core Ops, SparseCore 0:
  103.1 49.2 all-gather.3

commit v4 on v3

--- a/solution.py
+++ b/solution.py
@@ -144,11 +144,11 @@
     return hidden_units, *(a.reshape(2 * count, rows, tokens) for a in (mine, theirs))
 
 
-def student_kernel(gathered_ref, projector_ref, all_ref, out_ref):
-    columns, count, rows, tokens = gathered_ref.shape
-    rows = jnp.concatenate(
-        [gathered_ref[:, i].reshape(columns * rows, tokens) for i in range(count)]
-    )
+def student_kernel(place_ref, gathered_ref, projector_ref, all_ref, out_ref):
+    columns, _, rows, tokens = gathered_ref.shape
+    low, high = (gathered_ref[:, i].reshape(columns * rows, tokens) for i in range(2))
+    even = place_ref[2] == 0
+    rows = jnp.concatenate([jnp.where(even, low, high), jnp.where(even, high, low)])
     all_ref[...] = rows
     part = jnp.dot(projector_ref[...], rows, preferred_element_type=F32)
 
@@ -161,20 +161,24 @@
         out_ref[...] += part
 
 
-def student_part(gathered, projector, steps=8):
+def student_part(place, gathered, projector):
     columns, count, rows, tokens = gathered.shape
     mine, width = projector.shape
+    steps = count // 2
     return pl.pallas_call(
         student_kernel,
-        grid=(steps,),
-        in_specs=[
-            pl.BlockSpec((columns, count // steps, rows, tokens), lambda k: (0, k, 0, 0)),
-            pl.BlockSpec((mine, width // steps), lambda k: (0, k)),
-        ],
-        out_specs=[
-            pl.BlockSpec((width // steps, tokens), lambda k: (k, 0)),
-            pl.BlockSpec((mine, tokens), lambda k: (0, 0)),
-        ],
+        grid_spec=pltpu.PrefetchScalarGridSpec(
+            num_scalar_prefetch=1,
+            grid=(steps,),
+            in_specs=[
+                pl.BlockSpec((columns, 2, rows, tokens), lambda k, p: (0, k ^ p[3], 0, 0)),
+                pl.BlockSpec((mine, width // steps), lambda k, _: (0, k)),
+            ],
+            out_specs=[
+                pl.BlockSpec((width // steps, tokens), lambda k, _: (k, 0)),
+                pl.BlockSpec((mine, tokens), lambda k, _: (0, 0)),
+            ],
+        ),
         out_shape=[
             jax.ShapeDtypeStruct((width, tokens), BF16),
             jax.ShapeDtypeStruct((mine, tokens), F32),
@@ -182,7 +186,7 @@
         compiler_params=PARAMS,
         cost_estimate=cost(2 * mine * width * tokens, 4 * width * tokens + 2 * mine * width),
         name="student",
-    )(gathered, projector)
+    )(place, gathered, projector)
 
 
 def grad_kernel(terms_ref, student_out_ref, student_ref, residual_ref, grad_ref, rows_ref, sem_ref):
@@ -226,7 +230,7 @@
 
 
 def shards(teacher_rows, teacher_gate, teacher_up, teacher_down, student_rows, projector):
-    place = jnp.stack([lax.axis_index(name) for name in ("core", "dp")]).astype(jnp.int32)
+    place = jnp.stack([lax.axis_index(name) for name in ("core", "dp", "x", "y")]).astype(jnp.int32)
     rows = teacher_rows.shape[0]
     chips = lax.axis_size(CHIPS)
     across = lax.axis_size("y") // 2
@@ -237,28 +241,30 @@
         low, high = 2 * y, 2 * (y + across)
         trade += [(low, low), (low + 1, high), (high, low + 1), (high + 1, high + 1)]
     held = lax.ppermute(teacher_rows, ("y", "dp"), trade)
-    quarter = teacher_down.shape[1] // 4
-    far = [lax.ppermute(teacher_down[:, :quarter], "dp", SWAP)]
-    held, far[0] = lax.optimization_barrier((held, far[0]))
-    far.append(lax.ppermute(teacher_down[:, quarter:], "dp", SWAP))
+    down_far = lax.ppermute(teacher_down, "dp", SWAP)
     teacher_own = spread(copies(held, held, chips), CHIPS)
-    student_part_rows = lax.all_gather(student_rows, ("y", "x"), axis=0)
-    teacher_own, far[1], student_part_rows = lax.optimization_barrier(
-        (teacher_own, far[1], student_part_rows)
+    column = student_rows[None]
+    for name in ("x", "y"):
+        bit, size = 1, lax.axis_size(name)
+        while bit < size:
+            moved = lax.ppermute(column, name, [(i, i ^ bit) for i in range(size)])
+            column = jnp.concatenate([column, moved])
+            bit *= 2
+    teacher_own, down_far, column = lax.optimization_barrier(
+        (teacher_own, down_far, column)
     )
     teacher_other = lax.ppermute(teacher_own, "core", SWAP)
-    student_gathered = lax.all_gather(student_part_rows, ("z", "core"), axis=0)
+    student_gathered = lax.all_gather(column, ("z", "core"), axis=0)
 
     keep, send = up_part(place, teacher_own, teacher_other, teacher_gate, teacher_up)
     got = lax.ppermute(send, "dp", SWAP)
-    down_far = jnp.concatenate([part.T for part in far])
-    teacher_hidden, mine, theirs = down_part(place, keep, got, teacher_down.T, down_far, rows)
+    teacher_hidden, mine, theirs = down_part(place, keep, got, teacher_down.T, down_far.T, rows)
     chip_sum = (
         mine.astype(F32) + lax.ppermute(theirs, "core", SWAP).astype(F32)
     ).astype(BF16)
     terms = spread(chip_sum, CHIPS)
 
-    student_all, student_out = student_part(student_gathered, projector)
+    student_all, student_out = student_part(place, student_gathered, projector)
     residual_error, grad_local = grad_part(terms, student_out, student_all)
     grad_projector = grad_local + lax.ppermute(grad_local, "dp", SWAP)
     return (teacher_hidden, residual_error, grad_projector)

time: 196 us -> 189 us (0.964)
  the two profiles are of different devices: /device:TPU:8 before, /device:TPU:42 now
where the time goes in v4:
time: 189 us
  waiting for transfers between devices  92 us (49%)
  starting transfers between devices  61.6 us (33%)
  between operations  14.3 us (8%)
  Pallas kernels  11.3 us (6%)
  local copies, waits for them, and re-layouts  7.03 us (4%)
  other arithmetic  2.34 us (1%)
    ppermute x4, waiting for transfers between devices, shards(): moved = lax.ppermute(column, name, [(i, i ^ bit) for i in range(size)])  39.1 us
    all_gather x1, waiting for transfers between devices, shards(): student_gathered = lax.all_gather(column, ('z', 'core'), axis=0)  25.5 us
    all_to_all x1, starting transfers between devices, shards(): teacher_own = spread(copies(held, held, chips), CHIPS)  18.3 us
    all_to_all x1, starting transfers between devices, shards(): terms = spread(chip_sum, CHIPS)  13.7 us
    ppermute x1, waiting for transfers between devices, shards(): grad_projector = grad_local + lax.ppermute(grad_local, 'dp', SWAP)  13.7 us
    ppermute x4, starting transfers between devices, shards(): moved = lax.ppermute(column, name, [(i, i ^ bit) for i in range(size)])  12 us
    ppermute x1, waiting for transfers between devices, shards(): held = lax.ppermute(teacher_rows, ('y', 'dp'), trade)  7.58 us
    unnamed x19, local copies, waits for them, and re-layouts  5.43 us
  transfers between devices with their start and end apart: 13, of which 10 were waited for; matrix products, arithmetic and copies ran while one was open for 2% of the time, Pallas kernels for 4%

profile of v4, /device:TPU:42, one launch (start us, length us, event | category | flops | bytes accessed | tf_op | source)
XLA Modules:
  0.0 188.5 jit_solution(217645824739535976)
XLA Ops:
  7.2 4.6 %collective-permute-start = (bf16[32,128]{1,0:T(8,128)(2,1)}, bf16[32,128]{1,0:T(8,128)(2,1)S(1)}, u32[]{:S(2)}, u32[]{:S(2)}) collective-permute-start(bf16[32,128]{1,0:T(8,128)(2,1)} %param.6), channel_id=1, source_target_pairs={{0,0},{1,256},{256,1},{257,257},{64,64},{65,320},{320,65},{321,321... | collective-permute-start | bytes 24584 | tf_op jit(solution)/shard_map/ppermute | solution.py:243
  11.8 7.6 %collective-permute-done.rows_ref._ = bf16[32,128]{1,0:T(8,128)(2,1)S(1)} collective-permute-done((bf16[32,128]{1,0:T(8,128)(2,1)}, bf16[32,128]{1,0:T(8,128)(2,1)S(1)}, u32[]{:S(2)}, u32[]{:S(2)}) %collective-permute-start) | collective-permute-done | bytes 8224 | tf_op jit(solution)/shard_map/ppermute | solution.py:243
  19.4 1.1 copies.1
  20.5 18.3 %all-to-all-start = ((bf16[128,32,128]{2,1,0:T(8,128)(2,1)}), bf16[128,32,128]{2,1,0:T(8,128)(2,1)S(1)}, u32[]{:S(2)}, u32[]{:S(2)}) async-start(bf16[128,32,128]{2,1,0:T(8,128)(2,1)} %copies.1), calls=%async_computation | async-start | bytes 2097152 | tf_op jit(solution)/shard_map/all_to_all | solution.py:245
  38.9 1.9 %collective-permute-start.1 = (bf16[104,4096]{1,0:T(8,128)(2,1)S(1)}, bf16[104,4096]{1,0:T(8,128)(2,1)}, u32[]{:S(2)}, u32[]{:S(2)}) collective-permute-start(bf16[104,4096]{1,0:T(8,128)(2,1)S(1)} %copy-done.4), channel_id=1, source_target_pairs={{0,1},{1,0},{2,3},{3,2},{4,5},{5,4},{6,7},{7,6},{8,9},{9,8},{10,11... | collective-permute-start | bytes 2555912 | tf_op jit(solution)/shard_map/ppermute | solution.py:244
  40.8 2.9 %collective-permute-start.2 = (bf16[1,32,128]{2,1,0:T(8,128)(2,1)S(1)}, bf16[1,32,128]{2,1,0:T(8,128)(2,1)S(1)}, u32[]{:S(2)}, u32[]{:S(2)}) collective-permute-start(bf16[1,32,128]{2,1,0:T(8,128)(2,1)S(1)} %bitcast.21), channel_id=1, source_target_pairs={{0,32},{32,0},{1,33},{33,1},{2,34},{34,2},{3,35},{35,3},{4,36},{36... | collective-permute-start | bytes 24584 | tf_op jit(solution)/shard_map/ppermute | solution.py:250
  43.8 25.6 %collective-permute-done.2 = bf16[1,32,128]{2,1,0:T(8,128)(2,1)S(1)} collective-permute-done((bf16[1,32,128]{2,1,0:T(8,128)(2,1)S(1)}, bf16[1,32,128]{2,1,0:T(8,128)(2,1)S(1)}, u32[]{:S(2)}, u32[]{:S(2)}) %collective-permute-start.2) | collective-permute-done | bytes 8224 | tf_op jit(solution)/shard_map/ppermute | solution.py:250
  69.4 3.1 %collective-permute-start.3 = (bf16[2,32,128]{2,1,0:T(8,128)(2,1)S(1)}, bf16[2,32,128]{2,1,0:T(8,128)(2,1)S(1)}, u32[]{:S(2)}, u32[]{:S(2)}) collective-permute-start(bf16[2,32,128]{2,1,0:T(8,128)(2,1)S(1)} %pad_maximum_fusion.2), channel_id=1, source_target_pairs={{0,64},{64,0},{128,192},{192,128},{256,320},{320,256},{384,448},{4... | collective-permute-start | bytes 49160 | tf_op jit(solution)/shard_map/ppermute | solution.py:250
  72.4 2.5 %collective-permute-done.3 = bf16[2,32,128]{2,1,0:T(8,128)(2,1)S(1)} collective-permute-done((bf16[2,32,128]{2,1,0:T(8,128)(2,1)S(1)}, bf16[2,32,128]{2,1,0:T(8,128)(2,1)S(1)}, u32[]{:S(2)}, u32[]{:S(2)}) %collective-permute-start.3) | collective-permute-done | bytes 16416 | tf_op jit(solution)/shard_map/ppermute | solution.py:250
  75.0 2.9 %collective-permute-start.4 = (bf16[4,32,128]{2,1,0:T(8,128)(2,1)S(1)}, bf16[4,32,128]{2,1,0:T(8,128)(2,1)S(1)}, u32[]{:S(2)}, u32[]{:S(2)}) collective-permute-start(bf16[4,32,128]{2,1,0:T(8,128)(2,1)S(1)} %pad_maximum_fusion.1), channel_id=1, source_target_pairs={{0,128},{64,192},{128,0},{192,64},{256,384},{320,448},{384,256},{4... | collective-permute-start | bytes 98312 | tf_op jit(solution)/shard_map/ppermute | solution.py:250
  78.0 3.8 %collective-permute-done.4 = bf16[4,32,128]{2,1,0:T(8,128)(2,1)S(1)} collective-permute-done((bf16[4,32,128]{2,1,0:T(8,128)(2,1)S(1)}, bf16[4,32,128]{2,1,0:T(8,128)(2,1)S(1)}, u32[]{:S(2)}, u32[]{:S(2)}) %collective-permute-start.4) | collective-permute-done | bytes 32800 | tf_op jit(solution)/shard_map/ppermute | solution.py:250
  81.7 3.1 %collective-permute-start.5 = (bf16[8,32,128]{2,1,0:T(8,128)(2,1)S(1)}, bf16[8,32,128]{2,1,0:T(8,128)(2,1)S(1)}, u32[]{:S(2)}, u32[]{:S(2)}) collective-permute-start(bf16[8,32,128]{2,1,0:T(8,128)(2,1)S(1)} %pad_maximum_fusion), channel_id=1, source_target_pairs={{0,256},{64,320},{128,384},{192,448},{256,0},{320,64},{384,128},{4... | collective-permute-start | bytes 196616 | tf_op jit(solution)/shard_map/ppermute | solution.py:250
  84.8 7.2 %collective-permute-done.5 = bf16[8,32,128]{2,1,0:T(8,128)(2,1)S(1)} collective-permute-done((bf16[8,32,128]{2,1,0:T(8,128)(2,1)S(1)}, bf16[8,32,128]{2,1,0:T(8,128)(2,1)S(1)}, u32[]{:S(2)}, u32[]{:S(2)}) %collective-permute-start.5) | collective-permute-done | bytes 65568 | tf_op jit(solution)/shard_map/ppermute | solution.py:250
  92.1 1.9 %collective-permute-start.6 = (bf16[128,32,128]{2,1,0:T(8,128)(2,1)S(1)}, bf16[128,32,128]{2,1,0:T(8,128)(2,1)S(1)}, u32[]{:S(2)}, u32[]{:S(2)}) collective-permute-start(bf16[128,32,128]{2,1,0:T(8,128)(2,1)S(1)} %all-to-all-done), channel_id=1, source_target_pairs={{0,2},{2,0},{1,3},{3,1},{4,6},{6,4},{5,7},{7,5},{8,10},{10,8},{9,1... | collective-permute-start | bytes 3145736 | tf_op jit(solution)/shard_map/ppermute | solution.py:256
  94.2 2.5 %collective-permute-done.6 = bf16[128,32,128]{2,1,0:T(8,128)(2,1)S(1)} collective-permute-done((bf16[128,32,128]{2,1,0:T(8,128)(2,1)S(1)}, bf16[128,32,128]{2,1,0:T(8,128)(2,1)S(1)}, u32[]{:S(2)}, u32[]{:S(2)}) %collective-permute-start.6) | collective-permute-done | bytes 1048608 | tf_op jit(solution)/shard_map/ppermute | solution.py:256
  96.7 1.2 copy-done.2
  97.8 2.8 %gate_up.1 = (f32[2,104,128]{2,1,0:T(8,128)S(1)}, bf16[2,104,128]{2,1,0:T(8,128)(2,1)S(1)}) custom-call(s32[4]{0:T(128)S(1)} %pad_add_fusion.place_ref, bf16[2,64,32,128]{3,2,1,0:T(8,128)(2,1)S(1)} %bitcast.17, bf16[2,64,32,128]{3,2,1,0:T(8,128)(2,1)S(1)} %bitcast.19, bf16[104,4096]{1,0:T(8,128)(2,1)S(1)} %copy-done.1, bf16[104,4096]{1,0:T(8,128)(2,1)S(1)} %copy-done.2), custom_call_target="tpu_custom_call" | custom-call | flops 436207616 | bytes 3801088 | tf_op jit(solution)/shard_map/gate_up/pallas_call | solution.py:77
  100.7 3.5 %collective-permute-start.7 = (bf16[2,104,128]{2,1,0:T(8,128)(2,1)S(1)}, bf16[2,104,128]{2,1,0:T(8,128)(2,1)S(1)}, u32[]{:S(2)}, u32[]{:S(2)}) collective-permute-start(bf16[2,104,128]{2,1,0:T(8,128)(2,1)S(1)} %get-tuple-element.17), channel_id=1, source_target_pairs={{0,1},{1,0},{2,3},{3,2},{4,5},{5,4},{6,7},{7,6},{8,9},{9,8},{10,11... | collective-permute-start | bytes 159752 | tf_op jit(solution)/shard_map/ppermute | solution.py:260
  104.2 1.6 copy.11
  105.8 1.6 copy.12
  108.2 2.4 %down.1 = (bf16[104,128]{1,0:T(8,128)(2,1)}, bf16[2,64,32,128]{3,2,1,0:T(8,128)(2,1)S(1)}, bf16[2,64,32,128]{3,2,1,0:T(8,128)(2,1)S(1)}) custom-call(s32[4]{0:T(128)S(1)} %pad_add_fusion.place_ref, f32[2,104,128]{2,1,0:T(8,128)S(1)} %get-tuple-element.16.keep_ref, bf16[2,104,128]{2,1,0:T(8,128)(2,1)S(1)} %collective-permute-done.7.got_ref, ...), custom_call_target="tpu_custom_call" | custom-call | tf_op jit(solution)/shard_map/down/pallas_call | solution.py:126
  110.6 1.9 %collective-permute-start.8 = (bf16[128,32,128]{2,1,0:T(8,128)(2,1)S(1)}, bf16[128,32,128]{2,1,0:T(8,128)(2,1)S(1)}, u32[]{:S(2)}, u32[]{:S(2)}) collective-permute-start(bf16[128,32,128]{2,1,0:T(8,128)(2,1)S(1)} %bitcast.20), channel_id=1, source_target_pairs={{0,2},{2,0},{1,3},{3,1},{4,6},{6,4},{5,7},{7,5},{8,10},{10,8},{9,1... | collective-permute-start | bytes 3145736 | tf_op jit(solution)/shard_map/ppermute | solution.py:263
  112.6 2.7 %collective-permute-done.8 = bf16[128,32,128]{2,1,0:T(8,128)(2,1)S(1)} collective-permute-done((bf16[128,32,128]{2,1,0:T(8,128)(2,1)S(1)}, bf16[128,32,128]{2,1,0:T(8,128)(2,1)S(1)}, u32[]{:S(2)}, u32[]{:S(2)}) %collective-permute-start.8) | collective-permute-done | bytes 1048608 | tf_op jit(solution)/shard_map/ppermute | solution.py:263
  115.2 1.3 fusion
  116.5 13.7 %all-to-all-start.1 = ((bf16[128,32,128]{2,1,0:T(8,128)(2,1)}), bf16[128,32,128]{2,1,0:T(8,128)(2,1)S(1)}, u32[]{:S(2)}, u32[]{:S(2)}) async-start(bf16[128,32,128]{2,1,0:T(8,128)(2,1)} %fusion), calls=%async_computation.1 | async-start | bytes 2097152 | tf_op jit(solution)/shard_map/all_to_all | solution.py:265
  130.3 25.5 %all-gather.3.cloned.1.call-done = bf16[256,32,128]{2,1,0:T(8,128)(2,1)} async-done(((bf16[16,32,128]{2,1,0:T(8,128)(2,1)}), bf16[256,32,128]{2,1,0:T(8,128)(2,1)}) %all-gather.3.cloned.1.call-update) | async-done | bytes 2097168 | tf_op jit(solution)/shard_map/all_gather | solution.py:257
  155.8 1.6 copy-done
  157.4 1.0 copy-done.3
  158.4 2.5 %student.1 = (bf16[8192,128]{1,0:T(8,128)(2,1)S(1)}, f32[32,128]{1,0:T(8,128)S(1)}) custom-call(s32[4]{0:T(128)S(1)} %pad_add_fusion.place_ref, bf16[16,16,32,128]{3,2,1,0:T(8,128)(2,1)S(1)} %bitcast.18, bf16[32,8192]{1,0:T(8,128)(2,1)S(1)} %copy-done.3), custom_call_target="tpu_custom_call" | custom-call | flops 67108864 | bytes 4718592 | tf_op jit(solution)/shard_map/student/pallas_call | solution.py:168
  160.9 2.4 %gradient.1 = (bf16[32,128]{1,0:T(8,128)(2,1)}, bf16[32,8192]{1,0:T(8,128)(2,1)S(1)}) custom-call(bf16[128,32,128]{2,1,0:T(8,128)(2,1)S(1)} %all-to-all-done.1.terms_ref, f32[32,128]{1,0:T(8,128)S(1)} %get-tuple-element.23.student_out_ref, bf16[8192,128]{1,0:T(8,128)(2,1)S(1)} %get-tuple-element.24.student_ref), custom_call_target="tpu_custom_call" | custom-call | flops 67108864 | bytes 3670016 | tf_op jit(solution)/shard_map/gradient/pallas_call | solution.py:214
  163.3 3.7 %collective-permute-start.9 = (bf16[32,8192]{1,0:T(8,128)(2,1)S(1)}, bf16[32,8192]{1,0:T(8,128)(2,1)S(1)}, u32[]{:S(2)}, u32[]{:S(2)}) collective-permute-start(bf16[32,8192]{1,0:T(8,128)(2,1)S(1)} %get-tuple-element.26), channel_id=1, source_target_pairs={{0,1},{1,0},{2,3},{3,2},{4,5},{5,4},{6,7},{7,6},{8,9},{9,8},{10,11... | collective-permute-start | bytes 1572872 | tf_op jit(solution)/shard_map/ppermute | solution.py:269
  167.1 13.7 %collective-permute-done.9 = bf16[32,8192]{1,0:T(8,128)(2,1)S(1)} collective-permute-done((bf16[32,8192]{1,0:T(8,128)(2,1)S(1)}, bf16[32,8192]{1,0:T(8,128)(2,1)S(1)}, u32[]{:S(2)}, u32[]{:S(2)}) %collective-permute-start.9) | collective-permute-done | bytes 524320 | tf_op jit(solution)/shard_map/ppermute | solution.py:269
  (27 shorter events, 2.0 us)
Async XLA Ops:
  7.2 31.7 %copy-start.4 = (bf16[104,4096]{1,0:T(8,128)(2,1)S(1)}, bf16[104,4096]{1,0:T(8,128)(2,1)}, u32[]{:S(2)}) copy-start(bf16[104,4096]{1,0:T(8,128)(2,1)} %param.9) | copy-start | bytes 2555908
  7.2 33.7 %copy-start.6 = (bf16[32,128]{1,0:T(8,128)(2,1)S(1)}, bf16[32,128]{1,0:T(8,128)(2,1)}, u32[]{:S(2)}) copy-start(bf16[32,128]{1,0:T(8,128)(2,1)} %param.10) | copy-start | bytes 24580
  7.2 89.5 %copy-start.1 = (bf16[104,4096]{1,0:T(8,128)(2,1)S(1)}, bf16[104,4096]{1,0:T(8,128)(2,1)}, u32[]{:S(2)}) copy-start(bf16[104,4096]{1,0:T(8,128)(2,1)} %gate_ref.1) | copy-start | bytes 2555908
  7.2 12.2 %collective-permute-start = (bf16[32,128]{1,0:T(8,128)(2,1)}, bf16[32,128]{1,0:T(8,128)(2,1)S(1)}, u32[]{:S(2)}, u32[]{:S(2)}) collective-permute-start(bf16[32,128]{1,0:T(8,128)(2,1)} %param.6), channel_id=1, source_target_pairs={{0,0},{1,256},{256,1},{257,257},{64,64},{65,320},{320,65},{321,321... | collective-permute-start | bytes 24584 | tf_op jit(solution)/shard_map/ppermute | solution.py:243
  20.5 71.6 %all-to-all-start = ((bf16[128,32,128]{2,1,0:T(8,128)(2,1)}), bf16[128,32,128]{2,1,0:T(8,128)(2,1)S(1)}, u32[]{:S(2)}, u32[]{:S(2)}) async-start(bf16[128,32,128]{2,1,0:T(8,128)(2,1)} %copies.1), calls=%async_computation | async-start | bytes 2097152 | tf_op jit(solution)/shard_map/all_to_all | solution.py:245
  38.8 117.0 %all-gather.3.cloned.1.call-start = ((), (), s32[]{:S(2)}) async-start(), calls=%async_computation.2 | async-start | bytes 2228224 | tf_op jit(solution)/shard_map/all_gather | solution.py:257
  38.9 53.2 %collective-permute-start.1 = (bf16[104,4096]{1,0:T(8,128)(2,1)S(1)}, bf16[104,4096]{1,0:T(8,128)(2,1)}, u32[]{:S(2)}, u32[]{:S(2)}) collective-permute-start(bf16[104,4096]{1,0:T(8,128)(2,1)S(1)} %copy-done.4), channel_id=1, source_target_pairs={{0,1},{1,0},{2,3},{3,2},{4,5},{5,4},{6,7},{7,6},{8,9},{9,8},{10,11... | collective-permute-start | bytes 2555912 | tf_op jit(solution)/shard_map/ppermute | solution.py:244
  40.8 28.5 %collective-permute-start.2 = (bf16[1,32,128]{2,1,0:T(8,128)(2,1)S(1)}, bf16[1,32,128]{2,1,0:T(8,128)(2,1)S(1)}, u32[]{:S(2)}, u32[]{:S(2)}) collective-permute-start(bf16[1,32,128]{2,1,0:T(8,128)(2,1)S(1)} %bitcast.21), channel_id=1, source_target_pairs={{0,32},{32,0},{1,33},{33,1},{2,34},{34,2},{3,35},{35,3},{4,36},{36... | collective-permute-start | bytes 24584 | tf_op jit(solution)/shard_map/ppermute | solution.py:250
  69.4 5.6 %collective-permute-start.3 = (bf16[2,32,128]{2,1,0:T(8,128)(2,1)S(1)}, bf16[2,32,128]{2,1,0:T(8,128)(2,1)S(1)}, u32[]{:S(2)}, u32[]{:S(2)}) collective-permute-start(bf16[2,32,128]{2,1,0:T(8,128)(2,1)S(1)} %pad_maximum_fusion.2), channel_id=1, source_target_pairs={{0,64},{64,0},{128,192},{192,128},{256,320},{320,256},{384,448},{4... | collective-permute-start | bytes 49160 | tf_op jit(solution)/shard_map/ppermute | solution.py:250
  75.0 6.7 %collective-permute-start.4 = (bf16[4,32,128]{2,1,0:T(8,128)(2,1)S(1)}, bf16[4,32,128]{2,1,0:T(8,128)(2,1)S(1)}, u32[]{:S(2)}, u32[]{:S(2)}) collective-permute-start(bf16[4,32,128]{2,1,0:T(8,128)(2,1)S(1)} %pad_maximum_fusion.1), channel_id=1, source_target_pairs={{0,128},{64,192},{128,0},{192,64},{256,384},{320,448},{384,256},{4... | collective-permute-start | bytes 98312 | tf_op jit(solution)/shard_map/ppermute | solution.py:250
  81.7 10.3 %collective-permute-start.5 = (bf16[8,32,128]{2,1,0:T(8,128)(2,1)S(1)}, bf16[8,32,128]{2,1,0:T(8,128)(2,1)S(1)}, u32[]{:S(2)}, u32[]{:S(2)}) collective-permute-start(bf16[8,32,128]{2,1,0:T(8,128)(2,1)S(1)} %pad_maximum_fusion), channel_id=1, source_target_pairs={{0,256},{64,320},{128,384},{192,448},{256,0},{320,64},{384,128},{4... | collective-permute-start | bytes 196616 | tf_op jit(solution)/shard_map/ppermute | solution.py:250
  92.1 2.0 %copy-start.5 = (bf16[16,32,128]{2,1,0:T(8,128)(2,1)}, bf16[16,32,128]{2,1,0:T(8,128)(2,1)S(1)}, u32[]{:S(2)}) copy-start(bf16[16,32,128]{2,1,0:T(8,128)(2,1)S(1)} %constant_dynamic-update-slice_fusion) | copy-start | bytes 393220
  92.1 4.6 %collective-permute-start.6 = (bf16[128,32,128]{2,1,0:T(8,128)(2,1)S(1)}, bf16[128,32,128]{2,1,0:T(8,128)(2,1)S(1)}, u32[]{:S(2)}, u32[]{:S(2)}) collective-permute-start(bf16[128,32,128]{2,1,0:T(8,128)(2,1)S(1)} %all-to-all-done), channel_id=1, source_target_pairs={{0,2},{2,0},{1,3},{3,1},{4,6},{6,4},{5,7},{7,5},{8,10},{10,8},{9,1... | collective-permute-start | bytes 3145736 | tf_op jit(solution)/shard_map/ppermute | solution.py:256
  96.7 1.2 copy-start.2
  100.7 7.5 %collective-permute-start.7 = (bf16[2,104,128]{2,1,0:T(8,128)(2,1)S(1)}, bf16[2,104,128]{2,1,0:T(8,128)(2,1)S(1)}, u32[]{:S(2)}, u32[]{:S(2)}) collective-permute-start(bf16[2,104,128]{2,1,0:T(8,128)(2,1)S(1)} %get-tuple-element.17), channel_id=1, source_target_pairs={{0,1},{1,0},{2,3},{3,2},{4,5},{5,4},{6,7},{7,6},{8,9},{9,8},{10,11... | collective-permute-start | bytes 159752 | tf_op jit(solution)/shard_map/ppermute | solution.py:260
  110.6 4.6 %collective-permute-start.8 = (bf16[128,32,128]{2,1,0:T(8,128)(2,1)S(1)}, bf16[128,32,128]{2,1,0:T(8,128)(2,1)S(1)}, u32[]{:S(2)}, u32[]{:S(2)}) collective-permute-start(bf16[128,32,128]{2,1,0:T(8,128)(2,1)S(1)} %bitcast.20), channel_id=1, source_target_pairs={{0,2},{2,0},{1,3},{3,1},{4,6},{6,4},{5,7},{7,5},{8,10},{10,8},{9,1... | collective-permute-start | bytes 3145736 | tf_op jit(solution)/shard_map/ppermute | solution.py:263
  116.5 44.4 %all-to-all-start.1 = ((bf16[128,32,128]{2,1,0:T(8,128)(2,1)}), bf16[128,32,128]{2,1,0:T(8,128)(2,1)S(1)}, u32[]{:S(2)}, u32[]{:S(2)}) async-start(bf16[128,32,128]{2,1,0:T(8,128)(2,1)} %fusion), calls=%async_computation.1 | async-start | bytes 2097152 | tf_op jit(solution)/shard_map/all_to_all | solution.py:265
  155.8 1.6 copy-start
  157.4 1.0 copy-start.3
  163.3 17.5 %collective-permute-start.9 = (bf16[32,8192]{1,0:T(8,128)(2,1)S(1)}, bf16[32,8192]{1,0:T(8,128)(2,1)S(1)}, u32[]{:S(2)}, u32[]{:S(2)}) collective-permute-start(bf16[32,8192]{1,0:T(8,128)(2,1)S(1)} %get-tuple-element.26), channel_id=1, source_target_pairs={{0,1},{1,0},{2,3},{3,2},{4,5},{5,4},{6,7},{7,6},{8,9},{9,8},{10,11... | collective-permute-start | bytes 1572872 | tf_op jit(solution)/shard_map/ppermute | solution.py:269
Sparse Core Ops, SparseCore 0:
  94.2 61.5 all-gather.2

commit v5 on v1

v5 whole, which is shorter than its diff:
```python
import functools

import jax
import jax.numpy as jnp
from jax import lax
from jax.experimental import pallas as pl
from jax.experimental.pallas import tpu as pltpu
from jax.sharding import Mesh, PartitionSpec as P

CHIPS = ("y", "x", "z")
SWAP = [(0, 1), (1, 0)]
F32, BF16 = jnp.float32, jnp.bfloat16
PARAMS = pltpu.CompilerParams(vmem_limit_bytes=24 << 20)


def cost(flops, size):
    return pl.CostEstimate(flops=flops, bytes_accessed=size, transcendentals=0)


def zip_cores(core, own, other):
    count, rows, tokens = own.shape
    even = jnp.where(core == 0, own, other)
    odd = jnp.where(core == 0, other, own)
    return jnp.stack([even, odd], axis=1).reshape(count * 2 * rows, tokens)


def copies_kernel(rows_ref, _, out_ref):
    out_ref[...] = jnp.broadcast_to(rows_ref[...][None], out_ref.shape)


def copies(rows, after, count):
    return pl.pallas_call(
        copies_kernel,
        in_specs=[pl.BlockSpec(memory_space=pltpu.VMEM), pl.BlockSpec(memory_space=pl.ANY)],
        out_shape=jax.ShapeDtypeStruct((count, *rows.shape), rows.dtype),
        compiler_params=PARAMS,
        cost_estimate=cost(0, count * rows.size * 2),
        name="copies",
    )(rows, after)


def pack_kernel(gate_ref, up_ref, out_ref):
    out_ref[0] = gate_ref[...]
    out_ref[1] = up_ref[...]


def pack(gate, up, steps=4):
    hidden, width = gate.shape
    block = pl.BlockSpec((hidden, width // steps), lambda k: (0, k))
    return pl.pallas_call(
        pack_kernel,
        grid=(steps,),
        in_specs=[block, block],
        out_specs=pl.BlockSpec((2, hidden, width // steps), lambda k: (0, 0, k)),
        out_shape=jax.ShapeDtypeStruct((2, hidden, width), BF16),
        compiler_params=PARAMS,
        cost_estimate=cost(0, 8 * hidden * width),
        name="pack",
    )(gate, up)


def up_kernel(place_ref, own_ref, other_ref, weight_ref, keep_ref, send_ref, acc_ref):
    step, last = pl.program_id(0), pl.num_programs(0) - 1
    core, half = place_ref[0], place_ref[1]
    tokens = own_ref.shape[-1]
    rows = jnp.concatenate(
        [zip_cores(core, own_ref[t], other_ref[t]) for t in range(2)], axis=1
    )
    for i in range(2):
        term = jnp.dot(weight_ref[i], rows, preferred_element_type=F32)

        @pl.when(step == 0)
        def _():
            acc_ref[i] = term

        @pl.when(step != 0)
        def _():
            acc_ref[i] += term

    @pl.when(step == last)
    def _():
        for i in range(2):
            low, high = acc_ref[i, :, :tokens], acc_ref[i, :, tokens:]
            keep_ref[i] = jnp.where(half == 0, low, high)
            send_ref[i] = jnp.where(half == 0, high, low).astype(BF16)


def up_part(place, own, other, weights, steps=4):
    hidden, width = weights.shape[1:]
    rows, tokens = own.shape[-2:]
    per = width // (2 * rows * steps)
    own, other = (a.reshape(2, -1, rows, tokens) for a in (own, other))
    block = pl.BlockSpec((2, per, rows, tokens), lambda k, _: (0, k, 0, 0))
    whole = pl.BlockSpec((2, hidden, tokens), lambda k, _: (0, 0, 0))
    return pl.pallas_call(
        up_kernel,
        grid_spec=pltpu.PrefetchScalarGridSpec(
            num_scalar_prefetch=1,
            grid=(steps,),
            in_specs=[
                block,
                block,
                pl.BlockSpec((2, hidden, width // steps), lambda k, _: (0, 0, k)),
            ],
            out_specs=[whole, whole],
            scratch_shapes=[pltpu.VMEM((2, hidden, 2 * tokens), F32)],
        ),
        out_shape=[
            jax.ShapeDtypeStruct((2, hidden, tokens), F32),
            jax.ShapeDtypeStruct((2, hidden, tokens), BF16),
        ],
        compiler_params=PARAMS,
        cost_estimate=cost(8 * hidden * width * tokens, 4 * hidden * width + 4 * own.size),
        name="gate_up",
    )(place, own, other, weights)


def down_kernel(place_ref, keep_ref, got_ref, near_ref, far_ref, hidden_ref, mine_ref, theirs_ref):
    side, step = pl.program_id(0), pl.program_id(1)
    core = place_ref[0]

    @pl.when((side == 0) & (step == 0))
    def _():
        preact, uppre = (keep_ref[i] + got_ref[i].astype(F32) for i in range(2))
        hidden_ref[...] = (preact / (1 + jnp.exp(-preact)) * uppre).astype(BF16)

    def part(ref):
        out = jnp.dot(ref[...], hidden_ref[...], preferred_element_type=F32).astype(BF16)
        count, rows, tokens = mine_ref.shape[1:]
        out = out.reshape(count, 2, rows, tokens)
        even, odd = out[:, 0], out[:, 1]
        mine_ref[0] = jnp.where(core == 0, even, odd)
        theirs_ref[0] = jnp.where(core == 0, odd, even)

    pl.when(side == 0)(lambda: part(near_ref))
    pl.when(side == 1)(lambda: part(far_ref))


def down_part(place, keep, got, near, far, rows, steps=2):
    width, hidden = near.shape
    tokens = keep.shape[-1]
    count = width // (2 * rows)
    whole = pl.BlockSpec((2, hidden, tokens), lambda s, k, _: (0, 0, 0))
    block = pl.BlockSpec(
        (1, count // steps, rows, tokens), lambda s, k, p: ((s + p[1]) % 2, k, 0, 0)
    )
    out = jax.ShapeDtypeStruct((2, count, rows, tokens), BF16)
    hidden_units, mine, theirs = pl.pallas_call(
        down_kernel,
        grid_spec=pltpu.PrefetchScalarGridSpec(
            num_scalar_prefetch=1,
            grid=(2, steps),
            in_specs=[
                whole,
                whole,
                pl.BlockSpec((width // steps, hidden), lambda s, k, _: (jnp.where(s == 0, k, steps - 1), 0)),
                pl.BlockSpec((width // steps, hidden), lambda s, k, _: (jnp.where(s == 1, k, 0), 0)),
            ],
            out_specs=[pl.BlockSpec((hidden, tokens), lambda s, k, _: (0, 0)), block, block],
        ),
        out_shape=[jax.ShapeDtypeStruct((hidden, tokens), BF16), out, out],
        compiler_params=PARAMS,
        cost_estimate=cost(0, 0),
        name="down",
    )(place, keep, got, near, far)
    return hidden_units, *(a.reshape(2 * count, rows, tokens) for a in (mine, theirs))


def student_kernel(place_ref, own_ref, other_ref, projector_ref, out_ref):
    rows = zip_cores(place_ref[0], own_ref[...], other_ref[...])
    part = jnp.dot(projector_ref[...], rows, preferred_element_type=F32)

    @pl.when(pl.program_id(0) == 0)
    def _():
        out_ref[...] = part

    @pl.when(pl.program_id(0) != 0)
    def _():
        out_ref[...] += part


def student_part(place, own, other, projector, steps=4):
    count, rows, tokens = own.shape
    mine, width = projector.shape
    block = pl.BlockSpec((count // steps, rows, tokens), lambda k, _: (k, 0, 0))
    return pl.pallas_call(
        student_kernel,
        grid_spec=pltpu.PrefetchScalarGridSpec(
            num_scalar_prefetch=1,
            grid=(steps,),
            in_specs=[block, block, pl.BlockSpec((mine, width // steps), lambda k, _: (0, k))],
            out_specs=pl.BlockSpec((mine, tokens), lambda k, _: (0, 0)),
        ),
        out_shape=jax.ShapeDtypeStruct((mine, tokens), F32),
        compiler_params=PARAMS,
        cost_estimate=cost(2 * mine * width * tokens, 2 * width * tokens + 2 * mine * width),
        name="student",
    )(place, own, other, projector)


def grad_kernel(place_ref, terms_ref, student_out_ref, own_ref, other_ref, residual_ref, grad_ref):
    @pl.when(pl.program_id(0) == 0)
    def _():
        teacher_out = jnp.sum(terms_ref[...].astype(F32), axis=0)
        residual_ref[...] = (student_out_ref[...] - teacher_out).astype(BF16)

    rows = zip_cores(place_ref[0], own_ref[...], other_ref[...])
    grad_ref[...] = lax.dot_general(
        residual_ref[...], rows, (((1,), (1,)), ((), ())), preferred_element_type=F32
    ).astype(BF16)


def grad_part(place, terms, student_out, own, other, steps=4):
    mine, tokens = student_out.shape
    count, rows = own.shape[:2]
    width = 2 * count * rows
    small = pl.BlockSpec((mine, tokens), lambda k, _: (0, 0))
    block = pl.BlockSpec((count // steps, rows, tokens), lambda k, _: (k, 0, 0))
    return pl.pallas_call(
        grad_kernel,
        grid_spec=pltpu.PrefetchScalarGridSpec(
            num_scalar_prefetch=1,
            grid=(steps,),
            in_specs=[pl.BlockSpec(terms.shape, lambda k, _: (0, 0, 0)), small, block, block],
            out_specs=[small, pl.BlockSpec((mine, width // steps), lambda k, _: (0, k))],
        ),
        out_shape=[
            jax.ShapeDtypeStruct((mine, tokens), BF16),
            jax.ShapeDtypeStruct((mine, width), BF16),
        ],
        compiler_params=PARAMS,
        cost_estimate=cost(2 * mine * width * tokens, 2 * (terms.size + width * tokens + mine * width)),
        name="gradient",
    )(place, terms, student_out, own, other)


def shards(teacher_rows, teacher_gate, teacher_up, teacher_down, student_rows, projector):
    place = jnp.stack([lax.axis_index(name) for name in ("core", "dp")]).astype(jnp.int32)
    rows = teacher_rows.shape[0]
    chips = lax.axis_size(CHIPS)
    across = lax.axis_size("y") // 2
    spread = functools.partial(lax.all_to_all, split_axis=0, concat_axis=0, tiled=True)

    trade = []
    for y in range(across):
        low, high = 2 * y, 2 * (y + across)
        trade += [(low, low), (low + 1, high), (high, low + 1), (high + 1, high + 1)]
    held = lax.ppermute(teacher_rows, ("y", "dp"), trade)
    down_far = lax.ppermute(teacher_down, "dp", SWAP)
    teacher_own = spread(copies(held, held, chips), CHIPS)
    teacher_own, down_far, down_near, student_copies, gate_and_up = lax.optimization_barrier(
        (
            teacher_own,
            down_far,
            teacher_down.T,
            copies(student_rows, held, chips),
            pack(teacher_gate, teacher_up),
        )
    )
    teacher_other = lax.ppermute(teacher_own, "core", SWAP)
    student_own = spread(student_copies, CHIPS)

    keep, send = up_part(place, teacher_own, teacher_other, gate_and_up)
    send, down_far = lax.optimization_barrier((send, down_far))
    got = lax.ppermute(send, "dp", SWAP)
    teacher_hidden, mine, theirs = down_part(place, keep, got, down_near, down_far.T, rows)
    chip_sum = (
        mine.astype(F32) + lax.ppermute(theirs, "core", SWAP).astype(F32)
    ).astype(BF16)
    terms = spread(chip_sum, CHIPS)

    student_other = lax.ppermute(student_own, "core", SWAP)
    student_out = student_part(place, student_own, student_other, projector)
    residual_error, grad_local = grad_part(place, terms, student_out, student_own, student_other)
    grad_projector = grad_local + lax.ppermute(grad_local, "dp", SWAP)
    return (teacher_hidden, residual_error, grad_projector)


def solution(mesh):
    fine = Mesh(mesh.devices.reshape(8, 2, 8, 2, 2), (*CHIPS, "core", "dp"))
    blk = (*CHIPS, "core")
    return jax.shard_map(
        shards,
        mesh=fine,
        in_specs=(P(blk, "dp"),) * 5 + (P(blk, None),),
        out_specs=(P(blk, "dp"), P(blk, "dp"), P(blk, None)),
        check_vma=False,
    )
```

time: 169 us -> 167 us (0.988)
  blocking collectives: 58.6 us -> 0 us
  starting transfers between devices: 30.6 us -> 67.2 us
  waiting for transfers between devices: 57.1 us -> 76.6 us
  local copies, waits for them, and re-layouts: 5.24 us -> 7.29 us
    all_to_all x1 -> x0, blocking collectives: 58.6 us -> none  [shards(): teacher_own = spread(copies(held, held, chips))]
    all_to_all x2 -> x3, starting transfers between devices: 12.1 us -> 49.5 us  [the longest x1 29.6 us: shards(): teacher_own = spread(copies(held, held, chips), CHIPS)]
    ppermute x1, waiting for transfers between devices: 13.7 us -> 24.3 us  [shards(): down_far = lax.ppermute(teacher_down, 'dp', SWAP)]
    all_to_all x2 -> x3, waiting for transfers between devices: 23.2 us -> 33.1 us  [the longest x1 23.2 us: shards(): terms = spread(chip_sum, CHIPS)]
    pallas_call x1, Pallas kernels: 6.55 us -> 2.42 us  [down_part(): pl.pallas_call(down_kernel, grid_spec=pltpu.PrefetchScalarGridSpec(num_sc...]
    pallas_call x1, Pallas kernels: 2.18 us -> 4.49 us  [up_part(): pl.pallas_call(up_kernel, grid_spec=pltpu.PrefetchScalarGridSpec(num_scal...]
    ppermute x1, waiting for transfers between devices: 13.2 us -> 11 us  [shards(): grad_projector = grad_local + lax.ppermute(grad_local, 'dp', SWAP)]
    ppermute x1, starting transfers between devices: 5.89 us -> 4.16 us  [shards(): got = lax.ppermute(send, 'dp', SWAP)]
  transfers between devices with their start and end apart: 9 -> 10, of which waited for: 6 -> 7; matrix products, arithmetic and copies ran while one was open for 1% -> 3% of each run, Pallas kernels for 7% -> 5%
where the time goes in v5:
time: 167 us
  waiting for transfers between devices  76.6 us (46%)
  starting transfers between devices  67.2 us (40%)
  Pallas kernels  12.5 us (7%)
  local copies, waits for them, and re-layouts  7.29 us (4%)
  other arithmetic  2.31 us (1%)
    all_to_all x1, starting transfers between devices, shards(): teacher_own = spread(copies(held, held, chips), CHIPS)  29.6 us
    ppermute x1, waiting for transfers between devices, shards(): down_far = lax.ppermute(teacher_down, 'dp', SWAP)  24.3 us
    all_to_all x1, waiting for transfers between devices, shards(): terms = spread(chip_sum, CHIPS)  23.2 us
    all_to_all x1, starting transfers between devices, shards(): student_own = spread(student_copies, CHIPS)  13.2 us
    ppermute x1, waiting for transfers between devices, shards(): grad_projector = grad_local + lax.ppermute(grad_local, 'dp', SWAP)  11 us
    all_to_all x1, waiting for transfers between devices, shards(): student_own = spread(student_copies, CHIPS)  9.85 us
    all_to_all x1, starting transfers between devices, shards(): terms = spread(chip_sum, CHIPS)  6.64 us
    unnamed x13, local copies, waits for them, and re-layouts  5.7 us
  transfers between devices with their start and end apart: 10, of which 7 were waited for; matrix products, arithmetic and copies ran while one was open for 3% of the time, Pallas kernels for 5%

profile of v5, /device:TPU:8, one launch (start us, length us, event | category | flops | bytes accessed | tf_op | source)
XLA Modules:
  0.0 166.6 jit_solution(7089207109408908721)
XLA Ops:
  0.6 1.4 collective-permute-start
  2.0 1.1 copies.2
  3.1 29.6 %all-to-all-start = ((bf16[128,32,128]{2,1,0:T(8,128)(2,1)}), bf16[128,32,128]{2,1,0:T(8,128)(2,1)}, u32[]{:S(2)}, u32[]{:S(2)}) async-start(bf16[128,32,128]{2,1,0:T(8,128)(2,1)} %copies.2), calls=%async_computation | async-start | bytes 2097152 | tf_op jit(solution)/shard_map/all_to_all | solution.py:250
  32.7 2.4 %collective-permute-start.1 = (bf16[104,4096]{1,0:T(8,128)(2,1)}, bf16[104,4096]{1,0:T(8,128)(2,1)}, u32[]{:S(2)}, u32[]{:S(2)}) collective-permute-start(bf16[104,4096]{1,0:T(8,128)(2,1)} %param.9), channel_id=1, source_target_pairs={{0,1},{1,0},{2,3},{3,2},{4,5},{5,4},{6,7},{7,6},{8,9},{9,8},{10,11... | collective-permute-start | bytes 2555912 | tf_op jit(solution)/shard_map/ppermute | solution.py:249
  35.1 2.3 %copy.11 = bf16[104,4096]{0,1:T(8,128)(2,1)} copy(bf16[104,4096]{1,0:T(8,128)(2,1)} %param.9) | data formatting | bytes 1703936 | tf_op args[3]
  37.4 1.2 copy-done.3
  38.6 0.4 pack.1.weight_ref
  39.0 0.2 copy-done.5
  39.3 0.1 copies.3
  39.4 1.0 copy-done.1
  40.4 24.3 %collective-permute-done.1 = bf16[104,4096]{1,0:T(8,128)(2,1)} collective-permute-done((bf16[104,4096]{1,0:T(8,128)(2,1)}, bf16[104,4096]{1,0:T(8,128)(2,1)}, u32[]{:S(2)}, u32[]{:S(2)}) %collective-permute-start.1) | collective-permute-done | bytes 852000 | tf_op jit(solution)/shard_map/ppermute | solution.py:249
  64.7 1.9 %collective-permute-start.2 = (bf16[128,32,128]{2,1,0:T(8,128)(2,1)}, bf16[128,32,128]{2,1,0:T(8,128)(2,1)}, u32[]{:S(2)}, u32[]{:S(2)}) collective-permute-start(bf16[128,32,128]{2,1,0:T(8,128)(2,1)} %all-to-all-done), channel_id=1, source_target_pairs={{0,2},{2,0},{1,3},{3,1},{4,6},{6,4},{5,7},{7,5},{8,10},{10,8},{9,1... | collective-permute-start | bytes 3145736 | tf_op jit(solution)/shard_map/ppermute | solution.py:260
  66.7 13.2 %all-to-all-start.2 = ((bf16[128,32,128]{2,1,0:T(8,128)(2,1)}), bf16[128,32,128]{2,1,0:T(8,128)(2,1)S(1)}, u32[]{:S(2)}, u32[]{:S(2)}) async-start(bf16[128,32,128]{2,1,0:T(8,128)(2,1)} %copy-done.1), calls=%async_computation.2 | async-start | bytes 2097152 | tf_op jit(solution)/shard_map/all_to_all | solution.py:261
  80.0 4.5 %gate_up.1 = (f32[2,104,128]{2,1,0:T(8,128)S(1)}, bf16[2,104,128]{2,1,0:T(8,128)(2,1)S(1)}) custom-call(s32[2]{0:T(128)S(1)} %pad_add_fusion.place_ref, bf16[2,64,32,128]{3,2,1,0:T(8,128)(2,1)} %bitcast.3.own_ref, bf16[2,64,32,128]{3,2,1,0:T(8,128)(2,1)} %bitcast.4.other_ref, bf16[2,104,4096]{2,1,0:T(8,128)(2,1)S(1)} %pack.1.weight_ref), custom_call_target="tpu_custom_call" | custom-call | flops 436207616 | bytes 3801088 | tf_op jit(solution)/shard_map/gate_up/pallas_call | solution.py:95
  84.5 4.2 %collective-permute-start.3 = (bf16[2,104,128]{2,1,0:T(8,128)(2,1)S(1)}, bf16[2,104,128]{2,1,0:T(8,128)(2,1)S(1)}, u32[]{:S(2)}, u32[]{:S(2)}) collective-permute-start(bf16[2,104,128]{2,1,0:T(8,128)(2,1)S(1)} %get-tuple-element.22), channel_id=1, source_target_pairs={{0,1},{1,0},{2,3},{3,2},{4,5},{5,4},{6,7},{7,6},{8,9},{9,8},{10,11... | collective-permute-start | bytes 159752 | tf_op jit(solution)/shard_map/ppermute | solution.py:265
  88.7 1.6 copy.12
  90.3 2.9 %collective-permute-done.3.got_ref = bf16[2,104,128]{2,1,0:T(8,128)(2,1)S(1)} collective-permute-done((bf16[2,104,128]{2,1,0:T(8,128)(2,1)S(1)}, bf16[2,104,128]{2,1,0:T(8,128)(2,1)S(1)}, u32[]{:S(2)}, u32[]{:S(2)}) %collective-permute-start.3) | collective-permute-done | bytes 53280 | tf_op jit(solution)/shard_map/ppermute | solution.py:265
  93.2 2.4 %down.1 = (bf16[104,128]{1,0:T(8,128)(2,1)}, bf16[2,64,32,128]{3,2,1,0:T(8,128)(2,1)S(1)}, bf16[2,64,32,128]{3,2,1,0:T(8,128)(2,1)S(1)}) custom-call(s32[2]{0:T(128)S(1)} %pad_add_fusion.place_ref, f32[2,104,128]{2,1,0:T(8,128)S(1)} %get-tuple-element.19.keep_ref, bf16[2,104,128]{2,1,0:T(8,128)(2,1)S(1)} %collective-permute-done.3.got_ref, ...), custom_call_target="tpu_custom_call" | custom-call | tf_op jit(solution)/shard_map/down/pallas_call | solution.py:148
  95.6 1.9 %collective-permute-start.4 = (bf16[128,32,128]{2,1,0:T(8,128)(2,1)S(1)}, bf16[128,32,128]{2,1,0:T(8,128)(2,1)S(1)}, u32[]{:S(2)}, u32[]{:S(2)}) collective-permute-start(bf16[128,32,128]{2,1,0:T(8,128)(2,1)S(1)} %bitcast.12), channel_id=1, source_target_pairs={{0,2},{2,0},{1,3},{3,1},{4,6},{6,4},{5,7},{7,5},{8,10},{10,8},{9,1... | collective-permute-start | bytes 3145736 | tf_op jit(solution)/shard_map/ppermute | solution.py:268
  97.5 2.6 %collective-permute-done.4 = bf16[128,32,128]{2,1,0:T(8,128)(2,1)S(1)} collective-permute-done((bf16[128,32,128]{2,1,0:T(8,128)(2,1)S(1)}, bf16[128,32,128]{2,1,0:T(8,128)(2,1)S(1)}, u32[]{:S(2)}, u32[]{:S(2)}) %collective-permute-start.4) | collective-permute-done | bytes 1048608 | tf_op jit(solution)/shard_map/ppermute | solution.py:268
  100.2 1.3 fusion
  101.5 9.9 %all-to-all-done.2.own_ref = bf16[128,32,128]{2,1,0:T(8,128)(2,1)S(1)} async-done(((bf16[128,32,128]{2,1,0:T(8,128)(2,1)}), bf16[128,32,128]{2,1,0:T(8,128)(2,1)S(1)}, u32[]{:S(2)}, u32[]{:S(2)}) %all-to-all-start.2) | async-done | bytes 1048608 | tf_op jit(solution)/shard_map/all_to_all | solution.py:261
  111.3 6.6 %all-to-all-start.1 = ((bf16[128,32,128]{2,1,0:T(8,128)(2,1)}), bf16[128,32,128]{2,1,0:T(8,128)(2,1)S(1)}, u32[]{:S(2)}, u32[]{:S(2)}) async-start(bf16[128,32,128]{2,1,0:T(8,128)(2,1)} %fusion), calls=%async_computation.1 | async-start | bytes 2097152 | tf_op jit(solution)/shard_map/all_to_all | solution.py:270
  118.0 1.9 %collective-permute-start.5 = (bf16[128,32,128]{2,1,0:T(8,128)(2,1)S(1)}, bf16[128,32,128]{2,1,0:T(8,128)(2,1)S(1)}, u32[]{:S(2)}, u32[]{:S(2)}) collective-permute-start(bf16[128,32,128]{2,1,0:T(8,128)(2,1)S(1)} %all-to-all-done.2.own_ref), channel_id=1, source_target_pairs={{0,2},{2,0},{1,3},{3,1},{4,6},{6,4},{5,7},{7,5},{8,10},{10,8},{9,1... | collective-permute-start | bytes 3145736 | tf_op jit(solution)/shard_map/ppermute | solution.py:272
  119.9 2.6 %collective-permute-done.5.other_ref = bf16[128,32,128]{2,1,0:T(8,128)(2,1)S(1)} collective-permute-done((bf16[128,32,128]{2,1,0:T(8,128)(2,1)S(1)}, bf16[128,32,128]{2,1,0:T(8,128)(2,1)S(1)}, u32[]{:S(2)}, u32[]{:S(2)}) %collective-permute-start.5) | collective-permute-done | bytes 1048608 | tf_op jit(solution)/shard_map/ppermute | solution.py:272
  122.5 1.0 copy-done.4
  123.6 1.5 student.1.student_out_ref
  125.1 23.2 %all-to-all-done.1.terms_ref = bf16[128,32,128]{2,1,0:T(8,128)(2,1)S(1)} async-done(((bf16[128,32,128]{2,1,0:T(8,128)(2,1)}), bf16[128,32,128]{2,1,0:T(8,128)(2,1)S(1)}, u32[]{:S(2)}, u32[]{:S(2)}) %all-to-all-start.1) | async-done | bytes 1048608 | tf_op jit(solution)/shard_map/all_to_all | solution.py:270
  148.3 2.4 %gradient.1 = (bf16[32,128]{1,0:T(8,128)(2,1)}, bf16[32,8192]{1,0:T(8,128)(2,1)S(1)}) custom-call(s32[2]{0:T(128)S(1)} %pad_add_fusion.place_ref, bf16[128,32,128]{2,1,0:T(8,128)(2,1)S(1)} %all-to-all-done.1.terms_ref, f32[32,128]{1,0:T(8,128)S(1)} %student.1.student_out_ref, bf16[128,32,128]{2,1,0:T(8,128)(2,1)S(1)} %all-to-all-done.2.own_ref, ...), custom_call_target="tpu_custom_call" | custom-call | flops 67108864 | bytes 3670016 | tf_op jit(solution)/shard_map/gradient/pallas_call | solution.py:219
  150.7 4.0 %collective-permute-start.6 = (bf16[32,8192]{1,0:T(8,128)(2,1)S(1)}, bf16[32,8192]{1,0:T(8,128)(2,1)S(1)}, u32[]{:S(2)}, u32[]{:S(2)}) collective-permute-start(bf16[32,8192]{1,0:T(8,128)(2,1)S(1)} %get-tuple-element.30), channel_id=1, source_target_pairs={{0,1},{1,0},{2,3},{3,2},{4,5},{5,4},{6,7},{7,6},{8,9},{9,8},{10,11... | collective-permute-start | bytes 1572872 | tf_op jit(solution)/shard_map/ppermute | solution.py:275
  154.7 11.0 %collective-permute-done.6 = bf16[32,8192]{1,0:T(8,128)(2,1)S(1)} collective-permute-done((bf16[32,8192]{1,0:T(8,128)(2,1)S(1)}, bf16[32,8192]{1,0:T(8,128)(2,1)S(1)}, u32[]{:S(2)}, u32[]{:S(2)}) %collective-permute-start.6) | collective-permute-done | bytes 524320 | tf_op jit(solution)/shard_map/ppermute | solution.py:275
  165.7 0.9 add.7
  (12 shorter events, 0.1 us)
Async XLA Ops:
  0.6 1.4 collective-permute-start
  3.1 34.3 %copy-start.2 = (bf16[104,4096]{1,0:T(8,128)(2,1)S(1)}, bf16[104,4096]{1,0:T(8,128)(2,1)}, u32[]{:S(2)}) copy-start(bf16[104,4096]{1,0:T(8,128)(2,1)} %gate_ref.1) | copy-start | bytes 2555908
  3.1 61.6 %all-to-all-start = ((bf16[128,32,128]{2,1,0:T(8,128)(2,1)}), bf16[128,32,128]{2,1,0:T(8,128)(2,1)}, u32[]{:S(2)}, u32[]{:S(2)}) async-start(bf16[128,32,128]{2,1,0:T(8,128)(2,1)} %copies.2), calls=%async_computation | async-start | bytes 2097152 | tf_op jit(solution)/shard_map/all_to_all | solution.py:250
  32.7 32.0 %collective-permute-start.1 = (bf16[104,4096]{1,0:T(8,128)(2,1)}, bf16[104,4096]{1,0:T(8,128)(2,1)}, u32[]{:S(2)}, u32[]{:S(2)}) collective-permute-start(bf16[104,4096]{1,0:T(8,128)(2,1)} %param.9), channel_id=1, source_target_pairs={{0,1},{1,0},{2,3},{3,2},{4,5},{5,4},{6,7},{7,6},{8,9},{9,8},{10,11... | collective-permute-start | bytes 2555912 | tf_op jit(solution)/shard_map/ppermute | solution.py:249
  37.4 1.2 copy-start.3
  38.6 0.7 copy-start.5
  39.4 1.0 copy-start.1
  64.7 15.3 %collective-permute-start.2 = (bf16[128,32,128]{2,1,0:T(8,128)(2,1)}, bf16[128,32,128]{2,1,0:T(8,128)(2,1)}, u32[]{:S(2)}, u32[]{:S(2)}) collective-permute-start(bf16[128,32,128]{2,1,0:T(8,128)(2,1)} %all-to-all-done), channel_id=1, source_target_pairs={{0,2},{2,0},{1,3},{3,1},{4,6},{6,4},{5,7},{7,5},{8,10},{10,8},{9,1... | collective-permute-start | bytes 3145736 | tf_op jit(solution)/shard_map/ppermute | solution.py:260
  66.7 44.7 %all-to-all-start.2 = ((bf16[128,32,128]{2,1,0:T(8,128)(2,1)}), bf16[128,32,128]{2,1,0:T(8,128)(2,1)S(1)}, u32[]{:S(2)}, u32[]{:S(2)}) async-start(bf16[128,32,128]{2,1,0:T(8,128)(2,1)} %copy-done.1), calls=%async_computation.2 | async-start | bytes 2097152 | tf_op jit(solution)/shard_map/all_to_all | solution.py:261
  84.5 8.7 %copy-start = (bf16[104,4096]{0,1:T(8,128)(2,1)S(1)}, bf16[104,4096]{0,1:T(8,128)(2,1)}, u32[]{:S(2)}) copy-start(bf16[104,4096]{0,1:T(8,128)(2,1)} %copy.11) | copy-start | bytes 2555908
  84.5 8.7 %collective-permute-start.3 = (bf16[2,104,128]{2,1,0:T(8,128)(2,1)S(1)}, bf16[2,104,128]{2,1,0:T(8,128)(2,1)S(1)}, u32[]{:S(2)}, u32[]{:S(2)}) collective-permute-start(bf16[2,104,128]{2,1,0:T(8,128)(2,1)S(1)} %get-tuple-element.22), channel_id=1, source_target_pairs={{0,1},{1,0},{2,3},{3,2},{4,5},{5,4},{6,7},{7,6},{8,9},{9,8},{10,11... | collective-permute-start | bytes 159752 | tf_op jit(solution)/shard_map/ppermute | solution.py:265
  95.6 4.5 %collective-permute-start.4 = (bf16[128,32,128]{2,1,0:T(8,128)(2,1)S(1)}, bf16[128,32,128]{2,1,0:T(8,128)(2,1)S(1)}, u32[]{:S(2)}, u32[]{:S(2)}) collective-permute-start(bf16[128,32,128]{2,1,0:T(8,128)(2,1)S(1)} %bitcast.12), channel_id=1, source_target_pairs={{0,2},{2,0},{1,3},{3,1},{4,6},{6,4},{5,7},{7,5},{8,10},{10,8},{9,1... | collective-permute-start | bytes 3145736 | tf_op jit(solution)/shard_map/ppermute | solution.py:268
  111.3 37.0 %all-to-all-start.1 = ((bf16[128,32,128]{2,1,0:T(8,128)(2,1)}), bf16[128,32,128]{2,1,0:T(8,128)(2,1)S(1)}, u32[]{:S(2)}, u32[]{:S(2)}) async-start(bf16[128,32,128]{2,1,0:T(8,128)(2,1)} %fusion), calls=%async_computation.1 | async-start | bytes 2097152 | tf_op jit(solution)/shard_map/all_to_all | solution.py:270
  118.0 4.6 %collective-permute-start.5 = (bf16[128,32,128]{2,1,0:T(8,128)(2,1)S(1)}, bf16[128,32,128]{2,1,0:T(8,128)(2,1)S(1)}, u32[]{:S(2)}, u32[]{:S(2)}) collective-permute-start(bf16[128,32,128]{2,1,0:T(8,128)(2,1)S(1)} %all-to-all-done.2.own_ref), channel_id=1, source_target_pairs={{0,2},{2,0},{1,3},{3,1},{4,6},{6,4},{5,7},{7,5},{8,10},{10,8},{9,1... | collective-permute-start | bytes 3145736 | tf_op jit(solution)/shard_map/ppermute | solution.py:272
  122.5 1.0 copy-start.4
  150.7 15.0 %collective-permute-start.6 = (bf16[32,8192]{1,0:T(8,128)(2,1)S(1)}, bf16[32,8192]{1,0:T(8,128)(2,1)S(1)}, u32[]{:S(2)}, u32[]{:S(2)}) collective-permute-start(bf16[32,8192]{1,0:T(8,128)(2,1)S(1)} %get-tuple-element.30), channel_id=1, source_target_pairs={{0,1},{1,0},{2,3},{3,2},{4,5},{5,4},{6,7},{7,6},{8,9},{9,8},{10,11... | collective-permute-start | bytes 1572872 | tf_op jit(solution)/shard_map/ppermute | solution.py:275

commit v6 on v5

--- a/solution.py
+++ b/solution.py
@@ -24,19 +24,22 @@
     return jnp.stack([even, odd], axis=1).reshape(count * 2 * rows, tokens)
 
 
-def copies_kernel(rows_ref, _, out_ref):
-    out_ref[...] = jnp.broadcast_to(rows_ref[...][None], out_ref.shape)
-
-
-def copies(rows, after, count):
+def copies_kernel(teacher_ref, student_ref, out_ref):
+    rows = teacher_ref.shape[0]
+    shape = (out_ref.shape[0], *teacher_ref.shape)
+    out_ref[:, :rows] = jnp.broadcast_to(teacher_ref[...][None], shape)
+    out_ref[:, rows:] = jnp.broadcast_to(student_ref[...][None], shape)
+
+
+def copies(teacher, student, count):
+    rows, tokens = teacher.shape
     return pl.pallas_call(
         copies_kernel,
-        in_specs=[pl.BlockSpec(memory_space=pltpu.VMEM), pl.BlockSpec(memory_space=pl.ANY)],
-        out_shape=jax.ShapeDtypeStruct((count, *rows.shape), rows.dtype),
-        compiler_params=PARAMS,
-        cost_estimate=cost(0, count * rows.size * 2),
+        out_shape=jax.ShapeDtypeStruct((count, 2 * rows, tokens), BF16),
+        compiler_params=PARAMS,
+        cost_estimate=cost(0, 4 * count * rows * tokens),
         name="copies",
-    )(rows, after)
+    )(teacher, student)
 
 
 def pack_kernel(gate_ref, up_ref, out_ref):
@@ -59,56 +62,43 @@
     )(gate, up)
 
 
-def up_kernel(place_ref, own_ref, other_ref, weight_ref, keep_ref, send_ref, acc_ref):
-    step, last = pl.program_id(0), pl.num_programs(0) - 1
+def up_kernel(steps, place_ref, own_ref, other_ref, weight_ref, keep_ref, send_ref, acc_ref):
     core, half = place_ref[0], place_ref[1]
-    tokens = own_ref.shape[-1]
-    rows = jnp.concatenate(
-        [zip_cores(core, own_ref[t], other_ref[t]) for t in range(2)], axis=1
-    )
+    count, tokens = own_ref.shape[1], own_ref.shape[3]
+    rows, width = own_ref.shape[2] // 2, weight_ref.shape[2]
+    for k in range(steps):
+        part = slice(k * count // steps, (k + 1) * count // steps)
+        columns = slice(k * width // steps, (k + 1) * width // steps)
+        block = jnp.concatenate(
+            [zip_cores(core, own_ref[t, part, :rows], other_ref[t, part, :rows]) for t in range(2)],
+            axis=1,
+        )
+        for i in range(2):
+            term = jnp.dot(weight_ref[i, :, columns], block, preferred_element_type=F32)
+            if k == 0:
+                acc_ref[i] = term
+            else:
+                acc_ref[i] += term
     for i in range(2):
-        term = jnp.dot(weight_ref[i], rows, preferred_element_type=F32)
-
-        @pl.when(step == 0)
-        def _():
-            acc_ref[i] = term
-
-        @pl.when(step != 0)
-        def _():
-            acc_ref[i] += term
-
-    @pl.when(step == last)
-    def _():
-        for i in range(2):
-            low, high = acc_ref[i, :, :tokens], acc_ref[i, :, tokens:]
-            keep_ref[i] = jnp.where(half == 0, low, high)
-            send_ref[i] = jnp.where(half == 0, high, low).astype(BF16)
+        low, high = acc_ref[i, :, :tokens], acc_ref[i, :, tokens:]
+        keep_ref[i] = jnp.where(half == 0, low, high)
+        send_ref[i] = jnp.where(half == 0, high, low).astype(BF16)
 
 
 def up_part(place, own, other, weights, steps=4):
     hidden, width = weights.shape[1:]
-    rows, tokens = own.shape[-2:]
-    per = width // (2 * rows * steps)
-    own, other = (a.reshape(2, -1, rows, tokens) for a in (own, other))
-    block = pl.BlockSpec((2, per, rows, tokens), lambda k, _: (0, k, 0, 0))
-    whole = pl.BlockSpec((2, hidden, tokens), lambda k, _: (0, 0, 0))
-    return pl.pallas_call(
-        up_kernel,
-        grid_spec=pltpu.PrefetchScalarGridSpec(
-            num_scalar_prefetch=1,
-            grid=(steps,),
-            in_specs=[
-                block,
-                block,
-                pl.BlockSpec((2, hidden, width // steps), lambda k, _: (0, 0, k)),
-            ],
-            out_specs=[whole, whole],
-            scratch_shapes=[pltpu.VMEM((2, hidden, 2 * tokens), F32)],
-        ),
+    tokens = own.shape[-1]
+    own, other = (a.reshape(2, -1, *a.shape[1:]) for a in (own, other))
+    vmem = pl.BlockSpec(memory_space=pltpu.VMEM)
+    return pl.pallas_call(
+        functools.partial(up_kernel, steps),
+        in_specs=[pl.BlockSpec(memory_space=pltpu.SMEM), vmem, vmem, vmem],
+        out_specs=[vmem, vmem],
         out_shape=[
             jax.ShapeDtypeStruct((2, hidden, tokens), F32),
             jax.ShapeDtypeStruct((2, hidden, tokens), BF16),
         ],
+        scratch_shapes=[pltpu.VMEM((2, hidden, 2 * tokens), F32)],
         compiler_params=PARAMS,
         cost_estimate=cost(8 * hidden * width * tokens, 4 * hidden * width + 4 * own.size),
         name="gate_up",
@@ -182,7 +172,7 @@
 def student_part(place, own, other, projector, steps=4):
     count, rows, tokens = own.shape
     mine, width = projector.shape
-    block = pl.BlockSpec((count // steps, rows, tokens), lambda k, _: (k, 0, 0))
+    block = pl.BlockSpec((count // steps, rows // 2, tokens), lambda k, _: (k, 1, 0))
     return pl.pallas_call(
         student_kernel,
         grid_spec=pltpu.PrefetchScalarGridSpec(
@@ -213,9 +203,9 @@
 def grad_part(place, terms, student_out, own, other, steps=4):
     mine, tokens = student_out.shape
     count, rows = own.shape[:2]
-    width = 2 * count * rows
+    width = count * rows
     small = pl.BlockSpec((mine, tokens), lambda k, _: (0, 0))
-    block = pl.BlockSpec((count // steps, rows, tokens), lambda k, _: (k, 0, 0))
+    block = pl.BlockSpec((count // steps, rows // 2, tokens), lambda k, _: (k, 1, 0))
     return pl.pallas_call(
         grad_kernel,
         grid_spec=pltpu.PrefetchScalarGridSpec(
@@ -247,20 +237,13 @@
         trade += [(low, low), (low + 1, high), (high, low + 1), (high + 1, high + 1)]
     held = lax.ppermute(teacher_rows, ("y", "dp"), trade)
     down_far = lax.ppermute(teacher_down, "dp", SWAP)
-    teacher_own = spread(copies(held, held, chips), CHIPS)
-    teacher_own, down_far, down_near, student_copies, gate_and_up = lax.optimization_barrier(
-        (
-            teacher_own,
-            down_far,
-            teacher_down.T,
-            copies(student_rows, held, chips),
-            pack(teacher_gate, teacher_up),
-        )
+    own = spread(copies(held, student_rows, chips), CHIPS)
+    own, down_far, down_near, gate_and_up = lax.optimization_barrier(
+        (own, down_far, teacher_down.T, pack(teacher_gate, teacher_up))
     )
-    teacher_other = lax.ppermute(teacher_own, "core", SWAP)
-    student_own = spread(student_copies, CHIPS)
-
-    keep, send = up_part(place, teacher_own, teacher_other, gate_and_up)
+    other = lax.ppermute(own, "core", SWAP)
+
+    keep, send = up_part(place, own, other, gate_and_up)
     send, down_far = lax.optimization_barrier((send, down_far))
     got = lax.ppermute(send, "dp", SWAP)
     teacher_hidden, mine, theirs = down_part(place, keep, got, down_near, down_far.T, rows)
@@ -269,9 +252,8 @@
     ).astype(BF16)
     terms = spread(chip_sum, CHIPS)
 
-    student_other = lax.ppermute(student_own, "core", SWAP)
-    student_out = student_part(place, student_own, student_other, projector)
-    residual_error, grad_local = grad_part(place, terms, student_out, student_own, student_other)
+    student_out = student_part(place, own, other, projector)
+    residual_error, grad_local = grad_part(place, terms, student_out, own, other)
     grad_projector = grad_local + lax.ppermute(grad_local, "dp", SWAP)
     return (teacher_hidden, residual_error, grad_projector)
 

time: 167 us -> 173 us (1.036)
  starting transfers between devices: 67.2 us -> 48.3 us
  waiting for transfers between devices: 76.6 us -> 94.4 us
  local copies, waits for them, and re-layouts: 7.29 us -> 13.1 us
    all_to_all x2 -> x1, starting transfers between devices: 42.8 us -> 29 us  [shards(): own = spread(copies(held, student_rows, chips), CHIPS)]
    ppermute x1, waiting for transfers between devices: 24.3 us -> 31.4 us  [shards(): down_far = lax.ppermute(teacher_down, 'dp', SWAP)]
    unnamed x13 -> x17, local copies, waits for them, and re-layouts: 5.7 us -> 10.8 us
    all_to_all x1, waiting for transfers between devices: 23.2 us -> 26.9 us  [shards(): terms = spread(chip_sum, CHIPS)]
    pallas_call x3 -> x2, Pallas kernels: 5.74 us -> 2.87 us  [the longest x1 2.36 us: up_part(): pl.pallas_call(functools.partial(up_kernel, steps), in_specs=[pl.BlockSpe...]
    all_to_all x2 -> x1, waiting for transfers between devices: 9.86 us -> 12.7 us  [shards(): own = spread(copies(held, student_rows, chips), CHIPS)]
    ppermute x1, waiting for transfers between devices: 11 us -> 13.7 us  [shards(): grad_projector = grad_local + lax.ppermute(grad_local, 'dp', SWAP)]
    ppermute x2 -> x1, starting transfers between devices: 3.83 us -> 1.91 us  [shards(): other = lax.ppermute(own, 'core', SWAP)]
  transfers between devices with their start and end apart: 10 -> 8, of which waited for: 7 -> 7; matrix products, arithmetic and copies ran while one was open for 3% -> 2% of each run, Pallas kernels for 5% -> 2%
where the time goes in v6:
time: 173 us; the launch traced here: 172 us
  waiting for transfers between devices  94.4 us (55%)
  starting transfers between devices  48.3 us (28%)
  local copies, waits for them, and re-layouts  13.1 us (8%)
  Pallas kernels  13 us (8%)
  other arithmetic  2.31 us (1%)
    ppermute x1, waiting for transfers between devices, shards(): down_far = lax.ppermute(teacher_down, 'dp', SWAP)  31.4 us
    all_to_all x1, starting transfers between devices, shards(): own = spread(copies(held, student_rows, chips), CHIPS)  29 us
    all_to_all x1, waiting for transfers between devices, shards(): terms = spread(chip_sum, CHIPS)  26.9 us
    ppermute x1, waiting for transfers between devices, shards(): grad_projector = grad_local + lax.ppermute(grad_local, 'dp', SWAP)  13.7 us
    all_to_all x1, waiting for transfers between devices, shards(): own = spread(copies(held, student_rows, chips), CHIPS)  12.7 us
    unnamed x17, local copies, waits for them, and re-layouts  10.8 us
    all_to_all x1, starting transfers between devices, shards(): terms = spread(chip_sum, CHIPS)  6.7 us
    ppermute x1, waiting for transfers between devices, shards(): other = lax.ppermute(own, 'core', SWAP)  4.18 us
  transfers between devices with their start and end apart: 8, of which 7 were waited for; matrix products, arithmetic and copies ran while one was open for 2% of the time, Pallas kernels for 2%

profile of v6, /device:TPU:8, one launch (start us, length us, event | category | flops | bytes accessed | tf_op | source)
XLA Modules:
  0.0 171.9 jit_solution(5543200803152915404)
XLA Ops:
  0.6 1.4 collective-permute-start
  2.0 0.7 copy-done.7
  2.7 0.5 copies.1
  3.2 1.3 copy-done
  4.5 29.0 %all-to-all-start = ((bf16[128,64,128]{2,1,0:T(8,128)(2,1)}), bf16[128,64,128]{2,1,0:T(8,128)(2,1)S(1)}, u32[]{:S(2)}, u32[]{:S(2)}) async-start(bf16[128,64,128]{2,1,0:T(8,128)(2,1)} %copy-done), calls=%async_computation | async-start | bytes 4194304 | tf_op jit(solution)/shard_map/all_to_all | solution.py:240
  33.6 2.4 %collective-permute-start.1 = (bf16[104,4096]{1,0:T(8,128)(2,1)}, bf16[104,4096]{1,0:T(8,128)(2,1)}, u32[]{:S(2)}, u32[]{:S(2)}) collective-permute-start(bf16[104,4096]{1,0:T(8,128)(2,1)} %param.9), channel_id=1, source_target_pairs={{0,1},{1,0},{2,3},{3,2},{4,5},{5,4},{6,7},{7,6},{8,9},{9,8},{10,11... | collective-permute-start | bytes 2555912 | tf_op jit(solution)/shard_map/ppermute | solution.py:239
  36.0 1.6 copy.11
  37.6 1.1 copy-done.4
  38.8 1.2 copy-done.5
  40.4 1.2 copy-done.1
  41.5 31.4 %collective-permute-done.1 = bf16[104,4096]{1,0:T(8,128)(2,1)} collective-permute-done((bf16[104,4096]{1,0:T(8,128)(2,1)}, bf16[104,4096]{1,0:T(8,128)(2,1)}, u32[]{:S(2)}, u32[]{:S(2)}) %collective-permute-start.1) | collective-permute-done | bytes 852000 | tf_op jit(solution)/shard_map/ppermute | solution.py:239
  73.0 12.7 %all-to-all-done.own_ref = bf16[128,64,128]{2,1,0:T(8,128)(2,1)S(1)} async-done(((bf16[128,64,128]{2,1,0:T(8,128)(2,1)}), bf16[128,64,128]{2,1,0:T(8,128)(2,1)S(1)}, u32[]{:S(2)}, u32[]{:S(2)}) %all-to-all-start) | async-done | bytes 2097184 | tf_op jit(solution)/shard_map/all_to_all | solution.py:240
  85.7 1.9 %collective-permute-start.2 = (bf16[128,64,128]{2,1,0:T(8,128)(2,1)S(1)}, bf16[128,64,128]{2,1,0:T(8,128)(2,1)}, u32[]{:S(2)}, u32[]{:S(2)}) collective-permute-start(bf16[128,64,128]{2,1,0:T(8,128)(2,1)S(1)} %all-to-all-done.own_ref), channel_id=1, source_target_pairs={{0,2},{2,0},{1,3},{3,1},{4,6},{6,4},{5,7},{7,5},{8,10},{10,8},{9,1... | collective-permute-start | bytes 6291464 | tf_op jit(solution)/shard_map/ppermute | solution.py:244
  87.7 4.2 %collective-permute-done.2.other_ref = bf16[128,64,128]{2,1,0:T(8,128)(2,1)} collective-permute-done((bf16[128,64,128]{2,1,0:T(8,128)(2,1)S(1)}, bf16[128,64,128]{2,1,0:T(8,128)(2,1)}, u32[]{:S(2)}, u32[]{:S(2)}) %collective-permute-start.2) | collective-permute-done | bytes 2097184 | tf_op jit(solution)/shard_map/ppermute | solution.py:244
  91.8 1.5 copy-done.2
  93.3 2.4 %gate_up.1 = (f32[2,104,128]{2,1,0:T(8,128)S(1)}, bf16[2,104,128]{2,1,0:T(8,128)(2,1)S(1)}) custom-call(s32[2]{0:T(128)S(1)} %pad_add_fusion.place_ref, bf16[2,64,64,128]{3,2,1,0:T(8,128)(2,1)S(1)} %bitcast.10, bf16[2,64,64,128]{3,2,1,0:T(8,128)(2,1)} %bitcast.4.other_ref, bf16[2,104,4096]{2,1,0:T(8,128)(2,1)S(1)} %copy-done.2), custom_call_target="tpu_custom_call" | custom-call | flops 436207616 | bytes 5898240 | tf_op jit(solution)/shard_map/gate_up/pallas_call | solution.py:93
  95.7 2.4 %collective-permute-start.3 = (bf16[2,104,128]{2,1,0:T(8,128)(2,1)S(1)}, bf16[2,104,128]{2,1,0:T(8,128)(2,1)S(1)}, u32[]{:S(2)}, u32[]{:S(2)}) collective-permute-start(bf16[2,104,128]{2,1,0:T(8,128)(2,1)S(1)} %get-tuple-element.21), channel_id=1, source_target_pairs={{0,1},{1,0},{2,3},{3,2},{4,5},{5,4},{6,7},{7,6},{8,9},{9,8},{10,11... | collective-permute-start | bytes 159752 | tf_op jit(solution)/shard_map/ppermute | solution.py:248
  98.1 2.2 %copy.12 = bf16[104,4096]{0,1:T(8,128)(2,1)} copy(bf16[104,4096]{1,0:T(8,128)(2,1)} %collective-permute-done.1) | data formatting | bytes 1703936 | tf_op jit(solution)/shard_map/optimization_barrier | solution.py:247
  100.3 2.9 %collective-permute-done.3.got_ref = bf16[2,104,128]{2,1,0:T(8,128)(2,1)S(1)} collective-permute-done((bf16[2,104,128]{2,1,0:T(8,128)(2,1)S(1)}, bf16[2,104,128]{2,1,0:T(8,128)(2,1)S(1)}, u32[]{:S(2)}, u32[]{:S(2)}) %collective-permute-start.3) | collective-permute-done | bytes 53280 | tf_op jit(solution)/shard_map/ppermute | solution.py:248
  103.2 1.2 copy-done.3
  104.4 2.4 %down.1 = (bf16[104,128]{1,0:T(8,128)(2,1)}, bf16[2,64,32,128]{3,2,1,0:T(8,128)(2,1)S(1)}, bf16[2,64,32,128]{3,2,1,0:T(8,128)(2,1)S(1)}) custom-call(s32[2]{0:T(128)S(1)} %pad_add_fusion.place_ref, f32[2,104,128]{2,1,0:T(8,128)S(1)} %get-tuple-element.18.keep_ref, bf16[2,104,128]{2,1,0:T(8,128)(2,1)S(1)} %collective-permute-done.3.got_ref, ...), custom_call_target="tpu_custom_call" | custom-call | tf_op jit(solution)/shard_map/down/pallas_call | solution.py:138
  106.8 1.9 %collective-permute-start.4 = (bf16[128,32,128]{2,1,0:T(8,128)(2,1)S(1)}, bf16[128,32,128]{2,1,0:T(8,128)(2,1)S(1)}, u32[]{:S(2)}, u32[]{:S(2)}) collective-permute-start(bf16[128,32,128]{2,1,0:T(8,128)(2,1)S(1)} %bitcast.13), channel_id=1, source_target_pairs={{0,2},{2,0},{1,3},{3,1},{4,6},{6,4},{5,7},{7,5},{8,10},{10,8},{9,1... | collective-permute-start | bytes 3145736 | tf_op jit(solution)/shard_map/ppermute | solution.py:251
  108.8 2.6 %collective-permute-done.4 = bf16[128,32,128]{2,1,0:T(8,128)(2,1)S(1)} collective-permute-done((bf16[128,32,128]{2,1,0:T(8,128)(2,1)S(1)}, bf16[128,32,128]{2,1,0:T(8,128)(2,1)S(1)}, u32[]{:S(2)}, u32[]{:S(2)}) %collective-permute-start.4) | collective-permute-done | bytes 1048608 | tf_op jit(solution)/shard_map/ppermute | solution.py:251
  111.4 1.3 fusion
  112.7 6.7 %all-to-all-start.1 = ((bf16[128,32,128]{2,1,0:T(8,128)(2,1)}), bf16[128,32,128]{2,1,0:T(8,128)(2,1)S(1)}, u32[]{:S(2)}, u32[]{:S(2)}) async-start(bf16[128,32,128]{2,1,0:T(8,128)(2,1)} %fusion), calls=%async_computation.1 | async-start | bytes 2097152 | tf_op jit(solution)/shard_map/all_to_all | solution.py:253
  119.4 1.0 copy-done.6
  120.5 3.2 %student.1.student_out_ref = f32[32,128]{1,0:T(8,128)S(1)} custom-call(s32[2]{0:T(128)S(1)} %pad_add_fusion.place_ref, bf16[128,64,128]{2,1,0:T(8,128)(2,1)S(1)} %all-to-all-done.own_ref, bf16[128,64,128]{2,1,0:T(8,128)(2,1)} %collective-permute-done.2.other_ref, bf16[32,8192]{1,0:T(8,128)(2,1)S(1)} %copy-done.6), custom_call_target="tpu_custom_call" | custom-call | flops 67108864 | bytes 2621440 | tf_op jit(solution)/shard_map/student/pallas_call | solution.py:176
  123.7 26.9 %all-to-all-done.1.terms_ref = bf16[128,32,128]{2,1,0:T(8,128)(2,1)S(1)} async-done(((bf16[128,32,128]{2,1,0:T(8,128)(2,1)}), bf16[128,32,128]{2,1,0:T(8,128)(2,1)S(1)}, u32[]{:S(2)}, u32[]{:S(2)}) %all-to-all-start.1) | async-done | bytes 1048608 | tf_op jit(solution)/shard_map/all_to_all | solution.py:253
  150.6 4.1 %gradient.1 = (bf16[32,128]{1,0:T(8,128)(2,1)}, bf16[32,8192]{1,0:T(8,128)(2,1)S(1)}) custom-call(s32[2]{0:T(128)S(1)} %pad_add_fusion.place_ref, bf16[128,32,128]{2,1,0:T(8,128)(2,1)S(1)} %all-to-all-done.1.terms_ref, f32[32,128]{1,0:T(8,128)S(1)} %student.1.student_out_ref, bf16[128,64,128]{2,1,0:T(8,128)(2,1)S(1)} %all-to-all-done.own_ref, ...), custom_call_target="tpu_custom_call" | custom-call | flops 67108864 | bytes 3670016 | tf_op jit(solution)/shard_map/gradient/pallas_call | solution.py:209
  154.7 2.6 %collective-permute-start.5 = (bf16[32,8192]{1,0:T(8,128)(2,1)S(1)}, bf16[32,8192]{1,0:T(8,128)(2,1)S(1)}, u32[]{:S(2)}, u32[]{:S(2)}) collective-permute-start(bf16[32,8192]{1,0:T(8,128)(2,1)S(1)} %get-tuple-element.28), channel_id=1, source_target_pairs={{0,1},{1,0},{2,3},{3,2},{4,5},{5,4},{6,7},{7,6},{8,9},{9,8},{10,11... | collective-permute-start | bytes 1572872 | tf_op jit(solution)/shard_map/ppermute | solution.py:257
  157.3 13.7 %collective-permute-done.5 = bf16[32,8192]{1,0:T(8,128)(2,1)S(1)} collective-permute-done((bf16[32,8192]{1,0:T(8,128)(2,1)S(1)}, bf16[32,8192]{1,0:T(8,128)(2,1)S(1)}, u32[]{:S(2)}, u32[]{:S(2)}) %collective-permute-start.5) | collective-permute-done | bytes 524320 | tf_op jit(solution)/shard_map/ppermute | solution.py:257
  170.9 0.9 add.7
  (11 shorter events, 0.5 us)
Async XLA Ops:
  0.6 1.4 collective-permute-start
  2.0 0.7 copy-start.7
  3.2 1.3 copy-start
  4.5 81.1 %all-to-all-start = ((bf16[128,64,128]{2,1,0:T(8,128)(2,1)}), bf16[128,64,128]{2,1,0:T(8,128)(2,1)S(1)}, u32[]{:S(2)}, u32[]{:S(2)}) async-start(bf16[128,64,128]{2,1,0:T(8,128)(2,1)} %copy-done), calls=%async_computation | async-start | bytes 4194304 | tf_op jit(solution)/shard_map/all_to_all | solution.py:240
  33.6 39.4 %collective-permute-start.1 = (bf16[104,4096]{1,0:T(8,128)(2,1)}, bf16[104,4096]{1,0:T(8,128)(2,1)}, u32[]{:S(2)}, u32[]{:S(2)}) collective-permute-start(bf16[104,4096]{1,0:T(8,128)(2,1)} %param.9), channel_id=1, source_target_pairs={{0,1},{1,0},{2,3},{3,2},{4,5},{5,4},{6,7},{7,6},{8,9},{9,8},{10,11... | collective-permute-start | bytes 2555912 | tf_op jit(solution)/shard_map/ppermute | solution.py:239
  37.6 1.2 copy-start.4
  38.8 1.2 copy-start.5
  40.4 1.2 copy-start.1
  85.7 6.2 %collective-permute-start.2 = (bf16[128,64,128]{2,1,0:T(8,128)(2,1)S(1)}, bf16[128,64,128]{2,1,0:T(8,128)(2,1)}, u32[]{:S(2)}, u32[]{:S(2)}) collective-permute-start(bf16[128,64,128]{2,1,0:T(8,128)(2,1)S(1)} %all-to-all-done.own_ref), channel_id=1, source_target_pairs={{0,2},{2,0},{1,3},{3,1},{4,6},{6,4},{5,7},{7,5},{8,10},{10,8},{9,1... | collective-permute-start | bytes 6291464 | tf_op jit(solution)/shard_map/ppermute | solution.py:244
  91.8 1.5 copy-start.2
  95.7 7.5 %collective-permute-start.3 = (bf16[2,104,128]{2,1,0:T(8,128)(2,1)S(1)}, bf16[2,104,128]{2,1,0:T(8,128)(2,1)S(1)}, u32[]{:S(2)}, u32[]{:S(2)}) collective-permute-start(bf16[2,104,128]{2,1,0:T(8,128)(2,1)S(1)} %get-tuple-element.21), channel_id=1, source_target_pairs={{0,1},{1,0},{2,3},{3,2},{4,5},{5,4},{6,7},{7,6},{8,9},{9,8},{10,11... | collective-permute-start | bytes 159752 | tf_op jit(solution)/shard_map/ppermute | solution.py:248
  103.2 1.2 copy-start.3
  106.8 4.5 %collective-permute-start.4 = (bf16[128,32,128]{2,1,0:T(8,128)(2,1)S(1)}, bf16[128,32,128]{2,1,0:T(8,128)(2,1)S(1)}, u32[]{:S(2)}, u32[]{:S(2)}) collective-permute-start(bf16[128,32,128]{2,1,0:T(8,128)(2,1)S(1)} %bitcast.13), channel_id=1, source_target_pairs={{0,2},{2,0},{1,3},{3,1},{4,6},{6,4},{5,7},{7,5},{8,10},{10,8},{9,1... | collective-permute-start | bytes 3145736 | tf_op jit(solution)/shard_map/ppermute | solution.py:251
  112.7 37.9 %all-to-all-start.1 = ((bf16[128,32,128]{2,1,0:T(8,128)(2,1)}), bf16[128,32,128]{2,1,0:T(8,128)(2,1)S(1)}, u32[]{:S(2)}, u32[]{:S(2)}) async-start(bf16[128,32,128]{2,1,0:T(8,128)(2,1)} %fusion), calls=%async_computation.1 | async-start | bytes 2097152 | tf_op jit(solution)/shard_map/all_to_all | solution.py:253
  119.4 1.0 copy-start.6
  154.7 16.3 %collective-permute-start.5 = (bf16[32,8192]{1,0:T(8,128)(2,1)S(1)}, bf16[32,8192]{1,0:T(8,128)(2,1)S(1)}, u32[]{:S(2)}, u32[]{:S(2)}) collective-permute-start(bf16[32,8192]{1,0:T(8,128)(2,1)S(1)} %get-tuple-element.28), channel_id=1, source_target_pairs={{0,1},{1,0},{2,3},{3,2},{4,5},{5,4},{6,7},{7,6},{8,9},{9,8},{10,11... | collective-permute-start | bytes 1572872 | tf_op jit(solution)/shard_map/ppermute | solution.py:257

commit v7 on v6

--- a/solution.py
+++ b/solution.py
@@ -24,22 +24,19 @@
     return jnp.stack([even, odd], axis=1).reshape(count * 2 * rows, tokens)
 
 
-def copies_kernel(teacher_ref, student_ref, out_ref):
-    rows = teacher_ref.shape[0]
-    shape = (out_ref.shape[0], *teacher_ref.shape)
-    out_ref[:, :rows] = jnp.broadcast_to(teacher_ref[...][None], shape)
-    out_ref[:, rows:] = jnp.broadcast_to(student_ref[...][None], shape)
-
-
-def copies(teacher, student, count):
-    rows, tokens = teacher.shape
+def copies_kernel(rows_ref, _, out_ref):
+    out_ref[...] = jnp.broadcast_to(rows_ref[...][None], out_ref.shape)
+
+
+def copies(rows, after, count):
     return pl.pallas_call(
         copies_kernel,
-        out_shape=jax.ShapeDtypeStruct((count, 2 * rows, tokens), BF16),
-        compiler_params=PARAMS,
-        cost_estimate=cost(0, 4 * count * rows * tokens),
+        in_specs=[pl.BlockSpec(memory_space=pltpu.VMEM), pl.BlockSpec(memory_space=pl.ANY)],
+        out_shape=jax.ShapeDtypeStruct((count, *rows.shape), rows.dtype),
+        compiler_params=PARAMS,
+        cost_estimate=cost(0, count * rows.size * 2),
         name="copies",
-    )(teacher, student)
+    )(rows, after)
 
 
 def pack_kernel(gate_ref, up_ref, out_ref):
@@ -65,12 +62,12 @@
 def up_kernel(steps, place_ref, own_ref, other_ref, weight_ref, keep_ref, send_ref, acc_ref):
     core, half = place_ref[0], place_ref[1]
     count, tokens = own_ref.shape[1], own_ref.shape[3]
-    rows, width = own_ref.shape[2] // 2, weight_ref.shape[2]
+    width = weight_ref.shape[2]
     for k in range(steps):
         part = slice(k * count // steps, (k + 1) * count // steps)
         columns = slice(k * width // steps, (k + 1) * width // steps)
         block = jnp.concatenate(
-            [zip_cores(core, own_ref[t, part, :rows], other_ref[t, part, :rows]) for t in range(2)],
+            [zip_cores(core, own_ref[t, part], other_ref[t, part]) for t in range(2)],
             axis=1,
         )
         for i in range(2):
@@ -156,8 +153,19 @@
     return hidden_units, *(a.reshape(2 * count, rows, tokens) for a in (mine, theirs))
 
 
+def in_order(core, own_ref, other_ref):
+    rows = own_ref.shape[2] // 2
+    return jnp.concatenate(
+        [
+            zip_cores(core, own_ref[y, :, part], other_ref[y, :, part])
+            for y in range(own_ref.shape[0])
+            for part in (slice(0, rows), slice(rows, 2 * rows))
+        ]
+    )
+
+
 def student_kernel(place_ref, own_ref, other_ref, projector_ref, out_ref):
-    rows = zip_cores(place_ref[0], own_ref[...], other_ref[...])
+    rows = in_order(place_ref[0], own_ref, other_ref)
     part = jnp.dot(projector_ref[...], rows, preferred_element_type=F32)
 
     @pl.when(pl.program_id(0) == 0)
@@ -170,9 +178,9 @@
 
 
 def student_part(place, own, other, projector, steps=4):
-    count, rows, tokens = own.shape
+    across, count, rows, tokens = own.shape
     mine, width = projector.shape
-    block = pl.BlockSpec((count // steps, rows // 2, tokens), lambda k, _: (k, 1, 0))
+    block = pl.BlockSpec((across // steps, count, rows, tokens), lambda k, _: (k, 0, 0, 0))
     return pl.pallas_call(
         student_kernel,
         grid_spec=pltpu.PrefetchScalarGridSpec(
@@ -194,7 +202,7 @@
         teacher_out = jnp.sum(terms_ref[...].astype(F32), axis=0)
         residual_ref[...] = (student_out_ref[...] - teacher_out).astype(BF16)
 
-    rows = zip_cores(place_ref[0], own_ref[...], other_ref[...])
+    rows = in_order(place_ref[0], own_ref, other_ref)
     grad_ref[...] = lax.dot_general(
         residual_ref[...], rows, (((1,), (1,)), ((), ())), preferred_element_type=F32
     ).astype(BF16)
@@ -202,10 +210,10 @@
 
 def grad_part(place, terms, student_out, own, other, steps=4):
     mine, tokens = student_out.shape
-    count, rows = own.shape[:2]
-    width = count * rows
+    across, count, rows = own.shape[:3]
+    width = 2 * across * count * rows
     small = pl.BlockSpec((mine, tokens), lambda k, _: (0, 0))
-    block = pl.BlockSpec((count // steps, rows // 2, tokens), lambda k, _: (k, 1, 0))
+    block = pl.BlockSpec((across // steps, count, rows, tokens), lambda k, _: (k, 0, 0, 0))
     return pl.pallas_call(
         grad_kernel,
         grid_spec=pltpu.PrefetchScalarGridSpec(
@@ -236,14 +244,28 @@
         low, high = 2 * y, 2 * (y + across)
         trade += [(low, low), (low + 1, high), (high, low + 1), (high + 1, high + 1)]
     held = lax.ppermute(teacher_rows, ("y", "dp"), trade)
+    near_x = lax.ppermute(student_rows, "x", SWAP)
+    held, near_x = lax.optimization_barrier((held, near_x))
+    first = lax.axis_index("x") == 0
+    pair = jnp.concatenate(
+        [jnp.where(first, student_rows, near_x), jnp.where(first, near_x, student_rows)]
+    )
     down_far = lax.ppermute(teacher_down, "dp", SWAP)
-    own = spread(copies(held, student_rows, chips), CHIPS)
-    own, down_far, down_near, gate_and_up = lax.optimization_barrier(
-        (own, down_far, teacher_down.T, pack(teacher_gate, teacher_up))
-    )
-    other = lax.ppermute(own, "core", SWAP)
-
-    keep, send = up_part(place, own, other, gate_and_up)
+    plane = ("y", "z")
+    teacher_own = spread(copies(held, held, chips), CHIPS)
+    teacher_own, down_far, down_near, student_copies, gate_and_up = lax.optimization_barrier(
+        (
+            teacher_own,
+            down_far,
+            teacher_down.T,
+            copies(pair, held, lax.axis_size(plane)),
+            pack(teacher_gate, teacher_up),
+        )
+    )
+    teacher_other = lax.ppermute(teacher_own, "core", SWAP)
+    student_own = spread(student_copies, plane)
+
+    keep, send = up_part(place, teacher_own, teacher_other, gate_and_up)
     send, down_far = lax.optimization_barrier((send, down_far))
     got = lax.ppermute(send, "dp", SWAP)
     teacher_hidden, mine, theirs = down_part(place, keep, got, down_near, down_far.T, rows)
@@ -252,8 +274,12 @@
     ).astype(BF16)
     terms = spread(chip_sum, CHIPS)
 
-    student_out = student_part(place, own, other, projector)
-    residual_error, grad_local = grad_part(place, terms, student_out, own, other)
+    student_other = lax.ppermute(student_own, "core", SWAP)
+    student_own, student_other = (
+        a.reshape(lax.axis_size("y"), -1, *a.shape[1:]) for a in (student_own, student_other)
+    )
+    student_out = student_part(place, student_own, student_other, projector)
+    residual_error, grad_local = grad_part(place, terms, student_out, student_own, student_other)
     grad_projector = grad_local + lax.ppermute(grad_local, "dp", SWAP)
     return (teacher_hidden, residual_error, grad_projector)
 

time: 173 us -> 167 us (0.965)
  starting transfers between devices: 48.3 us -> 64.6 us
  waiting for transfers between devices: 94.4 us -> 80.8 us
  local copies, waits for them, and re-layouts: 13.1 us -> 7.3 us
  Pallas kernels: 13 us -> 10.4 us
    ppermute x1, waiting for transfers between devices: 31.4 us -> 24.2 us  [shards(): down_far = lax.ppermute(teacher_down, 'dp', SWAP)]
    all_to_all x1 -> x2, starting transfers between devices: 29 us -> 35.4 us  [the longest x1 23.9 us: shards(): teacher_own = spread(copies(held, held, chips), CHIPS)]
    ppermute x1 -> x3, starting transfers between devices: 1.91 us -> 7.22 us  [the longest x1 3.39 us: shards(): near_x = lax.ppermute(student_rows, 'x', SWAP)]
    unnamed x17 -> x13, local copies, waits for them, and re-layouts: 10.8 us -> 5.71 us
    all_to_all x1, waiting for transfers between devices: 26.9 us -> 23.6 us  [shards(): terms = spread(chip_sum, CHIPS)]
    ppermute x1, waiting for transfers between devices: 13.7 us -> 11.6 us  [shards(): grad_projector = grad_local + lax.ppermute(grad_local, 'dp', SWAP)]
    all_to_all x1, starting transfers between devices: 6.7 us -> 8.57 us  [shards(): terms = spread(chip_sum, CHIPS)]
    all_to_all x1 -> x2, waiting for transfers between devices: 12.7 us -> 11.5 us  [the longest x1 11.5 us: shards(): student_own = spread(student_copies, plane)]
  transfers between devices with their start and end apart: 8 -> 11, of which waited for: 7 -> 8; matrix products, arithmetic and copies ran while one was open for 2% -> 3% of each run, Pallas kernels for 2% -> 4%
where the time goes in v7:
time: 167 us; the launch traced here: 166 us
  waiting for transfers between devices  80.8 us (48%)
  starting transfers between devices  64.6 us (39%)
  Pallas kernels  10.4 us (6%)
  local copies, waits for them, and re-layouts  7.3 us (4%)
  other arithmetic  2.31 us (1%)
    ppermute x1, waiting for transfers between devices, shards(): down_far = lax.ppermute(teacher_down, 'dp', SWAP)  24.2 us
    all_to_all x1, starting transfers between devices, shards(): teacher_own = spread(copies(held, held, chips), CHIPS)  23.9 us
    all_to_all x1, waiting for transfers between devices, shards(): terms = spread(chip_sum, CHIPS)  23.6 us
    ppermute x1, waiting for transfers between devices, shards(): grad_projector = grad_local + lax.ppermute(grad_local, 'dp', SWAP)  11.6 us
    all_to_all x1, starting transfers between devices, shards(): student_own = spread(student_copies, plane)  11.6 us
    all_to_all x1, waiting for transfers between devices, shards(): student_own = spread(student_copies, plane)  11.5 us
    all_to_all x1, starting transfers between devices, shards(): terms = spread(chip_sum, CHIPS)  8.57 us
    unnamed x13, local copies, waits for them, and re-layouts  5.71 us
  transfers between devices with their start and end apart: 11, of which 8 were waited for; matrix products, arithmetic and copies ran while one was open for 3% of the time, Pallas kernels for 4%

profile of v7, /device:TPU:8, one launch (start us, length us, event | category | flops | bytes accessed | tf_op | source)
XLA Modules:
  0.0 166.2 jit_solution(14554133581055397002)
XLA Ops:
  0.6 1.4 collective-permute-start
  2.0 3.4 %collective-permute-start.1 = (bf16[32,128]{1,0:T(8,128)(2,1)}, bf16[32,128]{1,0:T(8,128)(2,1)S(1)}, u32[]{:S(2)}, u32[]{:S(2)}) collective-permute-start(bf16[32,128]{1,0:T(8,128)(2,1)} %param.10), channel_id=1, source_target_pairs={{0,32},{32,0},{1,33},{33,1},{2,34},{34,2},{3,35},{35,3},{4,36},{36... | collective-permute-start | bytes 24584 | tf_op jit(solution)/shard_map/ppermute | solution.py:247
  5.4 2.3 %collective-permute-done.1 = bf16[32,128]{1,0:T(8,128)(2,1)S(1)} collective-permute-done((bf16[32,128]{1,0:T(8,128)(2,1)}, bf16[32,128]{1,0:T(8,128)(2,1)S(1)}, u32[]{:S(2)}, u32[]{:S(2)}) %collective-permute-start.1) | collective-permute-done | bytes 8224 | tf_op jit(solution)/shard_map/ppermute | solution.py:247
  7.7 1.1 copies.2
  8.8 23.9 %all-to-all-start = ((bf16[128,32,128]{2,1,0:T(8,128)(2,1)}), bf16[128,32,128]{2,1,0:T(8,128)(2,1)}, u32[]{:S(2)}, u32[]{:S(2)}) async-start(bf16[128,32,128]{2,1,0:T(8,128)(2,1)} %copies.2), calls=%async_computation | async-start | bytes 2097152 | tf_op jit(solution)/shard_map/all_to_all | solution.py:255
  32.7 2.4 %collective-permute-start.2 = (bf16[104,4096]{1,0:T(8,128)(2,1)}, bf16[104,4096]{1,0:T(8,128)(2,1)}, u32[]{:S(2)}, u32[]{:S(2)}) collective-permute-start(bf16[104,4096]{1,0:T(8,128)(2,1)} %param.9), channel_id=1, source_target_pairs={{0,1},{1,0},{2,3},{3,2},{4,5},{5,4},{6,7},{7,6},{8,9},{9,8},{10,11... | collective-permute-start | bytes 2555912 | tf_op jit(solution)/shard_map/ppermute | solution.py:253
  35.1 2.3 %copy.11 = bf16[104,4096]{0,1:T(8,128)(2,1)} copy(bf16[104,4096]{1,0:T(8,128)(2,1)} %param.9) | data formatting | bytes 1703936 | tf_op args[3]
  37.4 1.2 copy-done.3
  38.5 0.4 pack.1.weight_ref
  39.5 1.0 copy-done.1
  40.5 24.2 %collective-permute-done.2 = bf16[104,4096]{1,0:T(8,128)(2,1)} collective-permute-done((bf16[104,4096]{1,0:T(8,128)(2,1)}, bf16[104,4096]{1,0:T(8,128)(2,1)}, u32[]{:S(2)}, u32[]{:S(2)}) %collective-permute-start.2) | collective-permute-done | bytes 852000 | tf_op jit(solution)/shard_map/ppermute | solution.py:253
  64.7 1.9 %collective-permute-start.3 = (bf16[128,32,128]{2,1,0:T(8,128)(2,1)}, bf16[128,32,128]{2,1,0:T(8,128)(2,1)}, u32[]{:S(2)}, u32[]{:S(2)}) collective-permute-start(bf16[128,32,128]{2,1,0:T(8,128)(2,1)} %all-to-all-done), channel_id=1, source_target_pairs={{0,2},{2,0},{1,3},{3,1},{4,6},{6,4},{5,7},{7,5},{8,10},{10,8},{9,1... | collective-permute-start | bytes 3145736 | tf_op jit(solution)/shard_map/ppermute | solution.py:265
  66.6 11.6 %all-to-all-start.2 = ((bf16[64,64,128]{2,1,0:T(8,128)(2,1)}), bf16[64,64,128]{2,1,0:T(8,128)(2,1)S(1)}, u32[]{:S(2)}, u32[]{:S(2)}) async-start(bf16[64,64,128]{2,1,0:T(8,128)(2,1)} %copy-done.1), calls=%async_computation.2 | async-start | bytes 2097152 | tf_op jit(solution)/shard_map/all_to_all | solution.py:266
  78.3 2.3 %gate_up.1 = (f32[2,104,128]{2,1,0:T(8,128)S(1)}, bf16[2,104,128]{2,1,0:T(8,128)(2,1)S(1)}) custom-call(s32[2]{0:T(128)S(1)} %pad_add_fusion.place_ref, bf16[2,64,32,128]{3,2,1,0:T(8,128)(2,1)} %bitcast.3.own_ref, bf16[2,64,32,128]{3,2,1,0:T(8,128)(2,1)} %bitcast.4.other_ref, bf16[2,104,4096]{2,1,0:T(8,128)(2,1)S(1)} %pack.1.weight_ref), custom_call_target="tpu_custom_call" | custom-call | flops 436207616 | bytes 3801088 | tf_op jit(solution)/shard_map/gate_up/pallas_call | solution.py:90
  80.6 3.7 %collective-permute-start.4 = (bf16[2,104,128]{2,1,0:T(8,128)(2,1)S(1)}, bf16[2,104,128]{2,1,0:T(8,128)(2,1)S(1)}, u32[]{:S(2)}, u32[]{:S(2)}) collective-permute-start(bf16[2,104,128]{2,1,0:T(8,128)(2,1)S(1)} %get-tuple-element.26), channel_id=1, source_target_pairs={{0,1},{1,0},{2,3},{3,2},{4,5},{5,4},{6,7},{7,6},{8,9},{9,8},{10,11... | collective-permute-start | bytes 159752 | tf_op jit(solution)/shard_map/ppermute | solution.py:270
  84.3 1.6 copy.12
  85.9 2.4 %collective-permute-done.4.got_ref = bf16[2,104,128]{2,1,0:T(8,128)(2,1)S(1)} collective-permute-done((bf16[2,104,128]{2,1,0:T(8,128)(2,1)S(1)}, bf16[2,104,128]{2,1,0:T(8,128)(2,1)S(1)}, u32[]{:S(2)}, u32[]{:S(2)}) %collective-permute-start.4) | collective-permute-done | bytes 53280 | tf_op jit(solution)/shard_map/ppermute | solution.py:270
  88.3 2.4 %down.1 = (bf16[104,128]{1,0:T(8,128)(2,1)}, bf16[2,64,32,128]{3,2,1,0:T(8,128)(2,1)S(1)}, bf16[2,64,32,128]{3,2,1,0:T(8,128)(2,1)S(1)}) custom-call(s32[2]{0:T(128)S(1)} %pad_add_fusion.place_ref, f32[2,104,128]{2,1,0:T(8,128)S(1)} %get-tuple-element.23.keep_ref, bf16[2,104,128]{2,1,0:T(8,128)(2,1)S(1)} %collective-permute-done.4.got_ref, ...), custom_call_target="tpu_custom_call" | custom-call | tf_op jit(solution)/shard_map/down/pallas_call | solution.py:135
  90.7 1.9 %collective-permute-start.5 = (bf16[128,32,128]{2,1,0:T(8,128)(2,1)S(1)}, bf16[128,32,128]{2,1,0:T(8,128)(2,1)S(1)}, u32[]{:S(2)}, u32[]{:S(2)}) collective-permute-start(bf16[128,32,128]{2,1,0:T(8,128)(2,1)S(1)} %bitcast.18), channel_id=1, source_target_pairs={{0,2},{2,0},{1,3},{3,1},{4,6},{6,4},{5,7},{7,5},{8,10},{10,8},{9,1... | collective-permute-start | bytes 3145736 | tf_op jit(solution)/shard_map/ppermute | solution.py:273
  92.6 2.6 %collective-permute-done.5 = bf16[128,32,128]{2,1,0:T(8,128)(2,1)S(1)} collective-permute-done((bf16[128,32,128]{2,1,0:T(8,128)(2,1)S(1)}, bf16[128,32,128]{2,1,0:T(8,128)(2,1)S(1)}, u32[]{:S(2)}, u32[]{:S(2)}) %collective-permute-start.5) | collective-permute-done | bytes 1048608 | tf_op jit(solution)/shard_map/ppermute | solution.py:273
  95.3 1.3 fusion
  96.6 11.5 %all-to-all-done.2 = bf16[64,64,128]{2,1,0:T(8,128)(2,1)S(1)} async-done(((bf16[64,64,128]{2,1,0:T(8,128)(2,1)}), bf16[64,64,128]{2,1,0:T(8,128)(2,1)S(1)}, u32[]{:S(2)}, u32[]{:S(2)}) %all-to-all-start.2) | async-done | bytes 1048608 | tf_op jit(solution)/shard_map/all_to_all | solution.py:266
  108.0 8.6 %all-to-all-start.1 = ((bf16[128,32,128]{2,1,0:T(8,128)(2,1)}), bf16[128,32,128]{2,1,0:T(8,128)(2,1)S(1)}, u32[]{:S(2)}, u32[]{:S(2)}) async-start(bf16[128,32,128]{2,1,0:T(8,128)(2,1)} %fusion), calls=%async_computation.1 | async-start | bytes 2097152 | tf_op jit(solution)/shard_map/all_to_all | solution.py:275
  116.6 1.9 %collective-permute-start.6 = (bf16[64,64,128]{2,1,0:T(8,128)(2,1)S(1)}, bf16[64,64,128]{2,1,0:T(8,128)(2,1)S(1)}, u32[]{:S(2)}, u32[]{:S(2)}) collective-permute-start(bf16[64,64,128]{2,1,0:T(8,128)(2,1)S(1)} %all-to-all-done.2), channel_id=1, source_target_pairs={{0,2},{2,0},{1,3},{3,1},{4,6},{6,4},{5,7},{7,5},{8,10},{10,8},{9,1... | collective-permute-start | bytes 3145736 | tf_op jit(solution)/shard_map/ppermute | solution.py:277
  118.5 2.6 %collective-permute-done.6 = bf16[64,64,128]{2,1,0:T(8,128)(2,1)S(1)} collective-permute-done((bf16[64,64,128]{2,1,0:T(8,128)(2,1)S(1)}, bf16[64,64,128]{2,1,0:T(8,128)(2,1)S(1)}, u32[]{:S(2)}, u32[]{:S(2)}) %collective-permute-start.6) | collective-permute-done | bytes 1048608 | tf_op jit(solution)/shard_map/ppermute | solution.py:277
  121.2 1.0 copy-done.4
  122.2 1.5 student.1.student_out_ref
  123.7 23.6 %all-to-all-done.1.terms_ref = bf16[128,32,128]{2,1,0:T(8,128)(2,1)S(1)} async-done(((bf16[128,32,128]{2,1,0:T(8,128)(2,1)}), bf16[128,32,128]{2,1,0:T(8,128)(2,1)S(1)}, u32[]{:S(2)}, u32[]{:S(2)}) %all-to-all-start.1) | async-done | bytes 1048608 | tf_op jit(solution)/shard_map/all_to_all | solution.py:275
  147.3 2.4 %gradient.1 = (bf16[32,128]{1,0:T(8,128)(2,1)}, bf16[32,8192]{1,0:T(8,128)(2,1)S(1)}) custom-call(s32[2]{0:T(128)S(1)} %pad_add_fusion.place_ref, bf16[128,32,128]{2,1,0:T(8,128)(2,1)S(1)} %all-to-all-done.1.terms_ref, f32[32,128]{1,0:T(8,128)S(1)} %student.1.student_out_ref, bf16[8,8,64,128]{3,2,1,0:T(8,128)(2,1)S(1)} %bitcast.13, ...), custom_call_target="tpu_custom_call" | custom-call | flops 67108864 | bytes 3670016 | tf_op jit(solution)/shard_map/gradient/pallas_call | solution.py:217
  149.7 4.0 %collective-permute-start.7 = (bf16[32,8192]{1,0:T(8,128)(2,1)S(1)}, bf16[32,8192]{1,0:T(8,128)(2,1)S(1)}, u32[]{:S(2)}, u32[]{:S(2)}) collective-permute-start(bf16[32,8192]{1,0:T(8,128)(2,1)S(1)} %get-tuple-element.34), channel_id=1, source_target_pairs={{0,1},{1,0},{2,3},{3,2},{4,5},{5,4},{6,7},{7,6},{8,9},{9,8},{10,11... | collective-permute-start | bytes 1572872 | tf_op jit(solution)/shard_map/ppermute | solution.py:283
  153.8 11.6 %collective-permute-done.7 = bf16[32,8192]{1,0:T(8,128)(2,1)S(1)} collective-permute-done((bf16[32,8192]{1,0:T(8,128)(2,1)S(1)}, bf16[32,8192]{1,0:T(8,128)(2,1)S(1)}, u32[]{:S(2)}, u32[]{:S(2)}) %collective-permute-start.7) | collective-permute-done | bytes 524320 | tf_op jit(solution)/shard_map/ppermute | solution.py:283
  165.3 0.9 add.7
  (16 shorter events, 0.6 us)
Async XLA Ops:
  0.6 4.8 %collective-permute-start = (bf16[32,128]{1,0:T(8,128)(2,1)}, bf16[32,128]{1,0:T(8,128)(2,1)S(1)}, u32[]{:S(2)}, u32[]{:S(2)}) collective-permute-start(bf16[32,128]{1,0:T(8,128)(2,1)} %param.6), channel_id=1, source_target_pairs={{0,0},{1,256},{256,1},{257,257},{64,64},{65,320},{320,65},{321,321... | collective-permute-start | bytes 24584 | tf_op jit(solution)/shard_map/ppermute | solution.py:246
  2.0 5.7 %collective-permute-start.1 = (bf16[32,128]{1,0:T(8,128)(2,1)}, bf16[32,128]{1,0:T(8,128)(2,1)S(1)}, u32[]{:S(2)}, u32[]{:S(2)}) collective-permute-start(bf16[32,128]{1,0:T(8,128)(2,1)} %param.10), channel_id=1, source_target_pairs={{0,32},{32,0},{1,33},{33,1},{2,34},{34,2},{3,35},{35,3},{4,36},{36... | collective-permute-start | bytes 24584 | tf_op jit(solution)/shard_map/ppermute | solution.py:247
  8.8 28.6 %copy-start.2 = (bf16[104,4096]{1,0:T(8,128)(2,1)S(1)}, bf16[104,4096]{1,0:T(8,128)(2,1)}, u32[]{:S(2)}) copy-start(bf16[104,4096]{1,0:T(8,128)(2,1)} %gate_ref.1) | copy-start | bytes 2555908
  8.8 55.9 %all-to-all-start = ((bf16[128,32,128]{2,1,0:T(8,128)(2,1)}), bf16[128,32,128]{2,1,0:T(8,128)(2,1)}, u32[]{:S(2)}, u32[]{:S(2)}) async-start(bf16[128,32,128]{2,1,0:T(8,128)(2,1)} %copies.2), calls=%async_computation | async-start | bytes 2097152 | tf_op jit(solution)/shard_map/all_to_all | solution.py:255
  32.7 32.0 %collective-permute-start.2 = (bf16[104,4096]{1,0:T(8,128)(2,1)}, bf16[104,4096]{1,0:T(8,128)(2,1)}, u32[]{:S(2)}, u32[]{:S(2)}) collective-permute-start(bf16[104,4096]{1,0:T(8,128)(2,1)} %param.9), channel_id=1, source_target_pairs={{0,1},{1,0},{2,3},{3,2},{4,5},{5,4},{6,7},{7,6},{8,9},{9,8},{10,11... | collective-permute-start | bytes 2555912 | tf_op jit(solution)/shard_map/ppermute | solution.py:253
  37.4 1.2 copy-start.3
  38.5 0.7 copy-start.5
  39.5 1.0 copy-start.1
  64.7 13.6 %collective-permute-start.3 = (bf16[128,32,128]{2,1,0:T(8,128)(2,1)}, bf16[128,32,128]{2,1,0:T(8,128)(2,1)}, u32[]{:S(2)}, u32[]{:S(2)}) collective-permute-start(bf16[128,32,128]{2,1,0:T(8,128)(2,1)} %all-to-all-done), channel_id=1, source_target_pairs={{0,2},{2,0},{1,3},{3,1},{4,6},{6,4},{5,7},{7,5},{8,10},{10,8},{9,1... | collective-permute-start | bytes 3145736 | tf_op jit(solution)/shard_map/ppermute | solution.py:265
  66.6 41.4 %all-to-all-start.2 = ((bf16[64,64,128]{2,1,0:T(8,128)(2,1)}), bf16[64,64,128]{2,1,0:T(8,128)(2,1)S(1)}, u32[]{:S(2)}, u32[]{:S(2)}) async-start(bf16[64,64,128]{2,1,0:T(8,128)(2,1)} %copy-done.1), calls=%async_computation.2 | async-start | bytes 2097152 | tf_op jit(solution)/shard_map/all_to_all | solution.py:266
  80.6 7.7 %copy-start = (bf16[104,4096]{0,1:T(8,128)(2,1)S(1)}, bf16[104,4096]{0,1:T(8,128)(2,1)}, u32[]{:S(2)}) copy-start(bf16[104,4096]{0,1:T(8,128)(2,1)} %copy.11) | copy-start | bytes 2555908
  80.6 7.7 %collective-permute-start.4 = (bf16[2,104,128]{2,1,0:T(8,128)(2,1)S(1)}, bf16[2,104,128]{2,1,0:T(8,128)(2,1)S(1)}, u32[]{:S(2)}, u32[]{:S(2)}) collective-permute-start(bf16[2,104,128]{2,1,0:T(8,128)(2,1)S(1)} %get-tuple-element.26), channel_id=1, source_target_pairs={{0,1},{1,0},{2,3},{3,2},{4,5},{5,4},{6,7},{7,6},{8,9},{9,8},{10,11... | collective-permute-start | bytes 159752 | tf_op jit(solution)/shard_map/ppermute | solution.py:270
  90.7 4.5 %collective-permute-start.5 = (bf16[128,32,128]{2,1,0:T(8,128)(2,1)S(1)}, bf16[128,32,128]{2,1,0:T(8,128)(2,1)S(1)}, u32[]{:S(2)}, u32[]{:S(2)}) collective-permute-start(bf16[128,32,128]{2,1,0:T(8,128)(2,1)S(1)} %bitcast.18), channel_id=1, source_target_pairs={{0,2},{2,0},{1,3},{3,1},{4,6},{6,4},{5,7},{7,5},{8,10},{10,8},{9,1... | collective-permute-start | bytes 3145736 | tf_op jit(solution)/shard_map/ppermute | solution.py:273
  108.0 39.3 %all-to-all-start.1 = ((bf16[128,32,128]{2,1,0:T(8,128)(2,1)}), bf16[128,32,128]{2,1,0:T(8,128)(2,1)S(1)}, u32[]{:S(2)}, u32[]{:S(2)}) async-start(bf16[128,32,128]{2,1,0:T(8,128)(2,1)} %fusion), calls=%async_computation.1 | async-start | bytes 2097152 | tf_op jit(solution)/shard_map/all_to_all | solution.py:275
  116.6 4.6 %collective-permute-start.6 = (bf16[64,64,128]{2,1,0:T(8,128)(2,1)S(1)}, bf16[64,64,128]{2,1,0:T(8,128)(2,1)S(1)}, u32[]{:S(2)}, u32[]{:S(2)}) collective-permute-start(bf16[64,64,128]{2,1,0:T(8,128)(2,1)S(1)} %all-to-all-done.2), channel_id=1, source_target_pairs={{0,2},{2,0},{1,3},{3,1},{4,6},{6,4},{5,7},{7,5},{8,10},{10,8},{9,1... | collective-permute-start | bytes 3145736 | tf_op jit(solution)/shard_map/ppermute | solution.py:277
  121.2 1.0 copy-start.4
  149.7 15.6 %collective-permute-start.7 = (bf16[32,8192]{1,0:T(8,128)(2,1)S(1)}, bf16[32,8192]{1,0:T(8,128)(2,1)S(1)}, u32[]{:S(2)}, u32[]{:S(2)}) collective-permute-start(bf16[32,8192]{1,0:T(8,128)(2,1)S(1)} %get-tuple-element.34), channel_id=1, source_target_pairs={{0,1},{1,0},{2,3},{3,2},{4,5},{5,4},{6,7},{7,6},{8,9},{9,8},{10,11... | collective-permute-start | bytes 1572872 | tf_op jit(solution)/shard_map/ppermute | solution.py:283

commit v8 on v7

--- a/solution.py
+++ b/solution.py
@@ -24,19 +24,27 @@
     return jnp.stack([even, odd], axis=1).reshape(count * 2 * rows, tokens)
 
 
-def copies_kernel(rows_ref, _, out_ref):
-    out_ref[...] = jnp.broadcast_to(rows_ref[...][None], out_ref.shape)
-
-
-def copies(rows, after, count):
+def copies_kernel(place_ref, mine_ref, next_ref, out_ref):
+    rows = mine_ref.shape[0]
+    shape = (out_ref.shape[0], *mine_ref.shape)
+    even = place_ref[2] == 0
+    mine, other = mine_ref[...], next_ref[...]
+    out_ref[:, :rows] = jnp.broadcast_to(jnp.where(even, mine, other)[None], shape)
+    out_ref[:, rows:] = jnp.broadcast_to(jnp.where(even, other, mine)[None], shape)
+
+
+def copies(place, mine, next_x, count):
+    rows, tokens = mine.shape
+    vmem = pl.BlockSpec(memory_space=pltpu.VMEM)
     return pl.pallas_call(
         copies_kernel,
-        in_specs=[pl.BlockSpec(memory_space=pltpu.VMEM), pl.BlockSpec(memory_space=pl.ANY)],
-        out_shape=jax.ShapeDtypeStruct((count, *rows.shape), rows.dtype),
-        compiler_params=PARAMS,
-        cost_estimate=cost(0, count * rows.size * 2),
+        in_specs=[pl.BlockSpec(memory_space=pltpu.SMEM), vmem, vmem],
+        out_specs=vmem,
+        out_shape=jax.ShapeDtypeStruct((count, 2 * rows, tokens), BF16),
+        compiler_params=PARAMS,
+        cost_estimate=cost(0, 4 * count * rows * tokens),
         name="copies",
-    )(rows, after)
+    )(place, mine, next_x)
 
 
 def pack_kernel(gate_ref, up_ref, out_ref):
@@ -59,18 +67,28 @@
     )(gate, up)
 
 
-def up_kernel(steps, place_ref, own_ref, other_ref, weight_ref, keep_ref, send_ref, acc_ref):
+def in_order(core, own_ref, other_ref):
+    rows = own_ref.shape[2] // 2
+    return jnp.concatenate(
+        [
+            zip_cores(core, own_ref[y, :, part], other_ref[y, :, part])
+            for y in range(own_ref.shape[0])
+            for part in (slice(0, rows), slice(rows, 2 * rows))
+        ]
+    )
+
+
+def up_kernel(place_ref, own_ref, other_ref, weight_ref, keep_ref, send_ref, acc_ref):
     core, half = place_ref[0], place_ref[1]
-    count, tokens = own_ref.shape[1], own_ref.shape[3]
-    width = weight_ref.shape[2]
+    steps, tokens = own_ref.shape[1], own_ref.shape[4]
+    width = weight_ref.shape[2] // steps
     for k in range(steps):
-        part = slice(k * count // steps, (k + 1) * count // steps)
-        columns = slice(k * width // steps, (k + 1) * width // steps)
+        part = pl.ds(k, 1)
         block = jnp.concatenate(
-            [zip_cores(core, own_ref[t, part], other_ref[t, part]) for t in range(2)],
-            axis=1,
+            [in_order(core, own_ref.at[t, part], other_ref.at[t, part]) for t in range(2)], axis=1
         )
         for i in range(2):
+            columns = slice(k * width, (k + 1) * width)
             term = jnp.dot(weight_ref[i, :, columns], block, preferred_element_type=F32)
             if k == 0:
                 acc_ref[i] = term
@@ -82,13 +100,13 @@
         send_ref[i] = jnp.where(half == 0, high, low).astype(BF16)
 
 
-def up_part(place, own, other, weights, steps=4):
+def up_part(place, own, other, weights):
     hidden, width = weights.shape[1:]
     tokens = own.shape[-1]
     own, other = (a.reshape(2, -1, *a.shape[1:]) for a in (own, other))
     vmem = pl.BlockSpec(memory_space=pltpu.VMEM)
     return pl.pallas_call(
-        functools.partial(up_kernel, steps),
+        up_kernel,
         in_specs=[pl.BlockSpec(memory_space=pltpu.SMEM), vmem, vmem, vmem],
         out_specs=[vmem, vmem],
         out_shape=[
@@ -102,7 +120,7 @@
     )(place, own, other, weights)
 
 
-def down_kernel(place_ref, keep_ref, got_ref, near_ref, far_ref, hidden_ref, mine_ref, theirs_ref):
+def down_kernel(place_ref, keep_ref, got_ref, near_ref, far_low_ref, far_high_ref, hidden_ref, mine_ref, theirs_ref):
     side, step = pl.program_id(0), pl.program_id(1)
     core = place_ref[0]
 
@@ -111,8 +129,13 @@
         preact, uppre = (keep_ref[i] + got_ref[i].astype(F32) for i in range(2))
         hidden_ref[...] = (preact / (1 + jnp.exp(-preact)) * uppre).astype(BF16)
 
-    def part(ref):
-        out = jnp.dot(ref[...], hidden_ref[...], preferred_element_type=F32).astype(BF16)
+    def part(*refs):
+        out, row = 0, 0
+        for ref in refs:
+            units = hidden_ref[row : row + ref.shape[1]]
+            out += jnp.dot(ref[...], units, preferred_element_type=F32)
+            row += ref.shape[1]
+        out = out.astype(BF16)
         count, rows, tokens = mine_ref.shape[1:]
         out = out.reshape(count, 2, rows, tokens)
         even, odd = out[:, 0], out[:, 1]
@@ -120,10 +143,10 @@
         theirs_ref[0] = jnp.where(core == 0, odd, even)
 
     pl.when(side == 0)(lambda: part(near_ref))
-    pl.when(side == 1)(lambda: part(far_ref))
-
-
-def down_part(place, keep, got, near, far, rows, steps=2):
+    pl.when(side == 1)(lambda: part(far_low_ref, far_high_ref))
+
+
+def down_part(place, keep, got, near, far_low, far_high, rows, steps=2):
     width, hidden = near.shape
     tokens = keep.shape[-1]
     count = width // (2 * rows)
@@ -141,7 +164,12 @@
                 whole,
                 whole,
                 pl.BlockSpec((width // steps, hidden), lambda s, k, _: (jnp.where(s == 0, k, steps - 1), 0)),
-                pl.BlockSpec((width // steps, hidden), lambda s, k, _: (jnp.where(s == 1, k, 0), 0)),
+                *(
+                    pl.BlockSpec(
+                        (width // steps, far.shape[1]), lambda s, k, _: (jnp.where(s == 1, k, 0), 0)
+                    )
+                    for far in (far_low, far_high)
+                ),
             ],
             out_specs=[pl.BlockSpec((hidden, tokens), lambda s, k, _: (0, 0)), block, block],
         ),
@@ -149,19 +177,8 @@
         compiler_params=PARAMS,
         cost_estimate=cost(0, 0),
         name="down",
-    )(place, keep, got, near, far)
+    )(place, keep, got, near, far_low, far_high)
     return hidden_units, *(a.reshape(2 * count, rows, tokens) for a in (mine, theirs))
-
-
-def in_order(core, own_ref, other_ref):
-    rows = own_ref.shape[2] // 2
-    return jnp.concatenate(
-        [
-            zip_cores(core, own_ref[y, :, part], other_ref[y, :, part])
-            for y in range(own_ref.shape[0])
-            for part in (slice(0, rows), slice(rows, 2 * rows))
-        ]
-    )
 
 
 def student_kernel(place_ref, own_ref, other_ref, projector_ref, out_ref):
@@ -233,42 +250,45 @@
 
 
 def shards(teacher_rows, teacher_gate, teacher_up, teacher_down, student_rows, projector):
-    place = jnp.stack([lax.axis_index(name) for name in ("core", "dp")]).astype(jnp.int32)
+    place = jnp.stack([lax.axis_index(name) for name in ("core", "dp", "x")]).astype(jnp.int32)
     rows = teacher_rows.shape[0]
-    chips = lax.axis_size(CHIPS)
+    plane = ("y", "z")
+    peers = lax.axis_size(plane)
     across = lax.axis_size("y") // 2
     spread = functools.partial(lax.all_to_all, split_axis=0, concat_axis=0, tiled=True)
 
-    trade = []
-    for y in range(across):
-        low, high = 2 * y, 2 * (y + across)
-        trade += [(low, low), (low + 1, high), (high, low + 1), (high + 1, high + 1)]
-    held = lax.ppermute(teacher_rows, ("y", "dp"), trade)
+    trade, trade_x = [], []
+    for y in range(2 * across):
+        for d in range(2):
+            low = y < across
+            to = (y, d) if low == (d == 0) else (y + across if low else y - across, 1 - d)
+            for x in range(2):
+                trade.append(((y * 2 + x) * 2 + d, (to[0] * 2 + x) * 2 + to[1]))
+                trade_x.append(((y * 2 + x) * 2 + d, (to[0] * 2 + 1 - x) * 2 + to[1]))
+    held, held_x = (lax.ppermute(teacher_rows, ("y", "x", "dp"), t) for t in (trade, trade_x))
     near_x = lax.ppermute(student_rows, "x", SWAP)
-    held, near_x = lax.optimization_barrier((held, near_x))
-    first = lax.axis_index("x") == 0
-    pair = jnp.concatenate(
-        [jnp.where(first, student_rows, near_x), jnp.where(first, near_x, student_rows)]
-    )
-    down_far = lax.ppermute(teacher_down, "dp", SWAP)
-    plane = ("y", "z")
-    teacher_own = spread(copies(held, held, chips), CHIPS)
-    teacher_own, down_far, down_near, student_copies, gate_and_up = lax.optimization_barrier(
+    held, held_x, near_x = lax.optimization_barrier((held, held_x, near_x))
+    units = 48
+    far_low = lax.ppermute(teacher_down[:units], "dp", SWAP)
+    teacher_own = spread(copies(place, held, held_x, peers), plane)
+    teacher_own, far_low, down_near, student_copies, gate_and_up = lax.optimization_barrier(
         (
             teacher_own,
-            down_far,
+            far_low,
             teacher_down.T,
-            copies(pair, held, lax.axis_size(plane)),
+            copies(place, student_rows, near_x, peers),
             pack(teacher_gate, teacher_up),
         )
     )
+    by_y = lambda a: a.reshape(2 * across, -1, *a.shape[1:])
     teacher_other = lax.ppermute(teacher_own, "core", SWAP)
+    far_high = lax.ppermute(teacher_down[units:], "dp", SWAP)
     student_own = spread(student_copies, plane)
 
-    keep, send = up_part(place, teacher_own, teacher_other, gate_and_up)
-    send, down_far = lax.optimization_barrier((send, down_far))
+    keep, send = up_part(place, by_y(teacher_own), by_y(teacher_other), gate_and_up)
+    send, far_low = lax.optimization_barrier((send, far_low))
     got = lax.ppermute(send, "dp", SWAP)
-    teacher_hidden, mine, theirs = down_part(place, keep, got, down_near, down_far.T, rows)
+    teacher_hidden, mine, theirs = down_part(place, keep, got, down_near, far_low.T, far_high.T, rows)
     chip_sum = (
         mine.astype(F32) + lax.ppermute(theirs, "core", SWAP).astype(F32)
     ).astype(BF16)

time: 167 us -> 170 us (1.018)
  waiting for transfers between devices: 80.8 us -> 72.7 us
  starting transfers between devices: 64.6 us -> 70.8 us
  local copies, waits for them, and re-layouts: 7.3 us -> 10.9 us
    all_to_all x1, waiting for transfers between devices: 0.01 us -> 15.3 us  [shards(): teacher_own = spread(copies(place, held, held_x, peers), plane)]
    ppermute x2 -> x4, waiting for transfers between devices: 24.2 us -> 11.8 us  [the longest x1 6.61 us: shards(): far_high = lax.ppermute(teacher_down[units:], 'dp', SWAP)]
    all_to_all x1, waiting for transfers between devices: 11.5 us -> 0.01 us  [shards(): student_own = spread(student_copies, plane)]
    ppermute x2 -> x4, starting transfers between devices: 3.77 us -> 8.93 us  [the longest x2 4.87 us: shards(): lax.ppermute(teacher_rows, ('y', 'x', 'dp'), t)]
    all_to_all x1, starting transfers between devices: 8.57 us -> 13.5 us  [shards(): terms = spread(chip_sum, CHIPS)]
    all_to_all x1, starting transfers between devices: 11.6 us -> 6.72 us  [shards(): student_own = spread(student_copies, plane)]
    ppermute x1, waiting for transfers between devices: 2.37 us -> 0.01 us  [shards(): got = lax.ppermute(send, 'dp', SWAP)]
    ppermute x1, starting transfers between devices: 3.69 us -> 5.47 us  [shards(): got = lax.ppermute(send, 'dp', SWAP)]
  transfers between devices with their start and end apart: 11 -> 13, of which waited for: 8 -> 8; matrix products, arithmetic and copies ran while one was open for 3% -> 4% of each run, Pallas kernels for 4% -> 5%
where the time goes in v8:
time: 170 us; the launch traced here: 169 us
  waiting for transfers between devices  72.7 us (43%)
  starting transfers between devices  70.8 us (42%)
  Pallas kernels  11.9 us (7%)
  local copies, waits for them, and re-layouts  10.9 us (6%)
  other arithmetic  2.3 us (1%)
    all_to_all x1, starting transfers between devices, shards(): teacher_own = spread(copies(place, held, held_x, peers), plane)  24.8 us
    all_to_all x1, waiting for transfers between devices, shards(): terms = spread(chip_sum, CHIPS)  24.1 us
    all_to_all x1, waiting for transfers between devices, shards(): teacher_own = spread(copies(place, held, held_x, peers), plane)  15.3 us
    all_to_all x1, starting transfers between devices, shards(): terms = spread(chip_sum, CHIPS)  13.5 us
    ppermute x1, waiting for transfers between devices, shards(): grad_projector = grad_local + lax.ppermute(grad_local, 'dp', SWAP)  13.1 us
    all_to_all x1, starting transfers between devices, shards(): student_own = spread(student_copies, plane)  6.72 us
    ppermute x1, waiting for transfers between devices, shards(): far_high = lax.ppermute(teacher_down[units:], 'dp', SWAP)  6.61 us
    unnamed x17, local copies, waits for them, and re-layouts  6.01 us
  transfers between devices with their start and end apart: 13, of which 8 were waited for; matrix products, arithmetic and copies ran while one was open for 4% of the time, Pallas kernels for 5%

profile of v8, /device:TPU:8, one launch (start us, length us, event | category | flops | bytes accessed | tf_op | source)
XLA Modules:
  0.0 169.5 jit_solution(3204507802354677534)
XLA Ops:
  0.6 1.5 collective-permute-start
  2.1 3.4 %collective-permute-start.1 = (bf16[32,128]{1,0:T(8,128)(2,1)}, bf16[32,128]{1,0:T(8,128)(2,1)S(1)}, u32[]{:S(2)}, u32[]{:S(2)}) collective-permute-start(bf16[32,128]{1,0:T(8,128)(2,1)} %param.6), channel_id=1, source_target_pairs={{0,32},{32,0},{1,288},{33,256},{64,96},{96,64},{65,352},{97,320},{... | collective-permute-start | bytes 24584 | tf_op jit(solution)/shard_map/ppermute | solution.py:268
  5.5 2.4 %collective-permute-start.2 = (bf16[32,128]{1,0:T(8,128)(2,1)}, bf16[32,128]{1,0:T(8,128)(2,1)S(1)}, u32[]{:S(2)}, u32[]{:S(2)}) collective-permute-start(bf16[32,128]{1,0:T(8,128)(2,1)} %mine_ref.1), channel_id=1, source_target_pairs={{0,32},{32,0},{1,33},{33,1},{2,34},{34,2},{3,35},{35,3},{4,36},{36... | collective-permute-start | bytes 24584 | tf_op jit(solution)/shard_map/ppermute | solution.py:269
  8.1 3.2 %collective-permute-done.2.next_ref = bf16[32,128]{1,0:T(8,128)(2,1)S(1)} collective-permute-done((bf16[32,128]{1,0:T(8,128)(2,1)}, bf16[32,128]{1,0:T(8,128)(2,1)S(1)}, u32[]{:S(2)}, u32[]{:S(2)}) %collective-permute-start.2) | collective-permute-done | bytes 8224 | tf_op jit(solution)/shard_map/ppermute | solution.py:269
  11.3 1.8 %copies.2 = bf16[64,64,128]{2,1,0:T(8,128)(2,1)} custom-call(s32[3]{0:T(128)S(1)} %pad_add_fusion.place_ref, bf16[32,128]{1,0:T(8,128)(2,1)S(1)} %collective-permute-done.mine_ref, bf16[32,128]{1,0:T(8,128)(2,1)S(1)} %collective-permute-done.1.next_ref), custom_call_target="tpu_custom_call" | custom-call | bytes 1048576 | tf_op jit(solution)/shard_map/copies/pallas_call | solution.py:39
  13.0 24.8 %all-to-all-start = ((bf16[64,64,128]{2,1,0:T(8,128)(2,1)}), bf16[64,64,128]{2,1,0:T(8,128)(2,1)}, u32[]{:S(2)}, u32[]{:S(2)}) async-start(bf16[64,64,128]{2,1,0:T(8,128)(2,1)} %copies.2), calls=%async_computation | async-start | bytes 2097152 | tf_op jit(solution)/shard_map/all_to_all | solution.py:273
  37.9 2.1 %collective-permute-start.3 = (bf16[48,4096]{1,0:T(8,128)(2,1)S(1)}, bf16[48,4096]{1,0:T(8,128)(2,1)}, u32[]{:S(2)}, u32[]{:S(2)}) collective-permute-start(bf16[48,4096]{1,0:T(8,128)(2,1)S(1)} %slice.6), channel_id=1, source_target_pairs={{0,1},{1,0},{2,3},{3,2},{4,5},{5,4},{6,7},{7,6},{8,9},{9,8},{10,11... | collective-permute-start | bytes 1179656 | tf_op jit(solution)/shard_map/ppermute | solution.py:272
  40.0 1.3 copy.12
  41.3 1.2 copy-done.4
  45.0 5.2 %collective-permute-done.3 = bf16[48,4096]{1,0:T(8,128)(2,1)} collective-permute-done((bf16[48,4096]{1,0:T(8,128)(2,1)S(1)}, bf16[48,4096]{1,0:T(8,128)(2,1)}, u32[]{:S(2)}, u32[]{:S(2)}) %collective-permute-start.3) | collective-permute-done | bytes 393248 | tf_op jit(solution)/shard_map/ppermute | solution.py:272
  50.2 15.3 %all-to-all-done = bf16[64,64,128]{2,1,0:T(8,128)(2,1)} async-done(((bf16[64,64,128]{2,1,0:T(8,128)(2,1)}), bf16[64,64,128]{2,1,0:T(8,128)(2,1)}, u32[]{:S(2)}, u32[]{:S(2)}) %all-to-all-start) | async-done | bytes 1048608 | tf_op jit(solution)/shard_map/all_to_all | solution.py:273
  65.5 1.9 %collective-permute-start.4 = (bf16[64,64,128]{2,1,0:T(8,128)(2,1)}, bf16[64,64,128]{2,1,0:T(8,128)(2,1)}, u32[]{:S(2)}, u32[]{:S(2)}) collective-permute-start(bf16[64,64,128]{2,1,0:T(8,128)(2,1)} %all-to-all-done), channel_id=1, source_target_pairs={{0,2},{2,0},{1,3},{3,1},{4,6},{6,4},{5,7},{7,5},{8,10},{10,8},{9,1... | collective-permute-start | bytes 3145736 | tf_op jit(solution)/shard_map/ppermute | solution.py:284
  67.4 6.7 %all-to-all-start.2 = ((bf16[64,64,128]{2,1,0:T(8,128)(2,1)}), bf16[64,64,128]{2,1,0:T(8,128)(2,1)S(1)}, u32[]{:S(2)}, u32[]{:S(2)}) async-start(bf16[64,64,128]{2,1,0:T(8,128)(2,1)} %copy-done), calls=%async_computation.2 | async-start | bytes 2097152 | tf_op jit(solution)/shard_map/all_to_all | solution.py:286
  75.2 2.0 %collective-permute-start.6 = (bf16[56,4096]{1,0:T(8,128)(2,1)S(1)}, bf16[56,4096]{1,0:T(8,128)(2,1)}, u32[]{:S(2)}, u32[]{:S(2)}) collective-permute-start(bf16[56,4096]{1,0:T(8,128)(2,1)S(1)} %slice.7), channel_id=1, source_target_pairs={{0,1},{1,0},{2,3},{3,2},{4,5},{5,4},{6,7},{7,6},{8,9},{9,8},{10,11... | collective-permute-start | bytes 1376264 | tf_op jit(solution)/shard_map/ppermute | solution.py:285
  77.2 2.3 %gate_up.1 = (f32[2,104,128]{2,1,0:T(8,128)S(1)}, bf16[2,104,128]{2,1,0:T(8,128)(2,1)S(1)}) custom-call(s32[3]{0:T(128)S(1)} %pad_add_fusion.place_ref, bf16[2,4,8,64,128]{4,3,2,1,0:T(8,128)(2,1)} %bitcast.4.own_ref, bf16[2,4,8,64,128]{4,3,2,1,0:T(8,128)(2,1)} %bitcast.5.other_ref, bf16[2,104,4096]{2,1,0:T(8,128)(2,1)S(1)} %pack.1.weight_ref), custom_call_target="tpu_custom_call" | custom-call | flops 436207616 | bytes 3801088 | tf_op jit(solution)/shard_map/gate_up/pallas_call | solution.py:108
  79.5 5.5 %collective-permute-start.5 = (bf16[2,104,128]{2,1,0:T(8,128)(2,1)S(1)}, bf16[2,104,128]{2,1,0:T(8,128)(2,1)S(1)}, u32[]{:S(2)}, u32[]{:S(2)}) collective-permute-start(bf16[2,104,128]{2,1,0:T(8,128)(2,1)S(1)} %get-tuple-element.28), channel_id=1, source_target_pairs={{0,1},{1,0},{2,3},{3,2},{4,5},{5,4},{6,7},{7,6},{8,9},{9,8},{10,11... | collective-permute-start | bytes 159752 | tf_op jit(solution)/shard_map/ppermute | solution.py:290
  85.0 6.6 %collective-permute-done.6 = bf16[56,4096]{1,0:T(8,128)(2,1)} collective-permute-done((bf16[56,4096]{1,0:T(8,128)(2,1)S(1)}, bf16[56,4096]{1,0:T(8,128)(2,1)}, u32[]{:S(2)}, u32[]{:S(2)}) %collective-permute-start.6) | collective-permute-done | bytes 458784 | tf_op jit(solution)/shard_map/ppermute | solution.py:285
  91.6 1.5 copy.14
  93.1 2.3 %copy.13 = bf16[48,4096]{0,1:T(8,128)(2,1)} copy(bf16[48,4096]{1,0:T(8,128)(2,1)} %collective-permute-done.3) | data formatting | bytes 786432 | tf_op jit(solution)/shard_map/optimization_barrier | solution.py:289
  95.4 1.2 copy-done.2
  96.7 2.7 %down.1 = (bf16[104,128]{1,0:T(8,128)(2,1)}, bf16[2,64,32,128]{3,2,1,0:T(8,128)(2,1)S(1)}, bf16[2,64,32,128]{3,2,1,0:T(8,128)(2,1)S(1)}) custom-call(s32[3]{0:T(128)S(1)} %pad_add_fusion.place_ref, f32[2,104,128]{2,1,0:T(8,128)S(1)} %get-tuple-element.25.keep_ref, bf16[2,104,128]{2,1,0:T(8,128)(2,1)S(1)} %collective-permute-done.5.got_ref, ...), custom_call_target="tpu_custom_call" | custom-call | tf_op jit(solution)/shard_map/down/pallas_call | solution.py:158
  99.3 1.9 %collective-permute-start.7 = (bf16[128,32,128]{2,1,0:T(8,128)(2,1)S(1)}, bf16[128,32,128]{2,1,0:T(8,128)(2,1)S(1)}, u32[]{:S(2)}, u32[]{:S(2)}) collective-permute-start(bf16[128,32,128]{2,1,0:T(8,128)(2,1)S(1)} %bitcast.21), channel_id=1, source_target_pairs={{0,2},{2,0},{1,3},{3,1},{4,6},{6,4},{5,7},{7,5},{8,10},{10,8},{9,1... | collective-permute-start | bytes 3145736 | tf_op jit(solution)/shard_map/ppermute | solution.py:293
  101.3 2.6 %collective-permute-done.7 = bf16[128,32,128]{2,1,0:T(8,128)(2,1)S(1)} collective-permute-done((bf16[128,32,128]{2,1,0:T(8,128)(2,1)S(1)}, bf16[128,32,128]{2,1,0:T(8,128)(2,1)S(1)}, u32[]{:S(2)}, u32[]{:S(2)}) %collective-permute-start.7) | collective-permute-done | bytes 1048608 | tf_op jit(solution)/shard_map/ppermute | solution.py:293
  103.9 1.3 fusion
  105.2 13.5 %all-to-all-start.1 = ((bf16[128,32,128]{2,1,0:T(8,128)(2,1)}), bf16[128,32,128]{2,1,0:T(8,128)(2,1)S(1)}, u32[]{:S(2)}, u32[]{:S(2)}) async-start(bf16[128,32,128]{2,1,0:T(8,128)(2,1)} %fusion), calls=%async_computation.1 | async-start | bytes 2097152 | tf_op jit(solution)/shard_map/all_to_all | solution.py:295
  118.7 1.9 %collective-permute-start.8 = (bf16[64,64,128]{2,1,0:T(8,128)(2,1)S(1)}, bf16[64,64,128]{2,1,0:T(8,128)(2,1)S(1)}, u32[]{:S(2)}, u32[]{:S(2)}) collective-permute-start(bf16[64,64,128]{2,1,0:T(8,128)(2,1)S(1)} %all-to-all-done.2), channel_id=1, source_target_pairs={{0,2},{2,0},{1,3},{3,1},{4,6},{6,4},{5,7},{7,5},{8,10},{10,8},{9,1... | collective-permute-start | bytes 3145736 | tf_op jit(solution)/shard_map/ppermute | solution.py:297
  120.6 2.6 %collective-permute-done.8 = bf16[64,64,128]{2,1,0:T(8,128)(2,1)S(1)} collective-permute-done((bf16[64,64,128]{2,1,0:T(8,128)(2,1)S(1)}, bf16[64,64,128]{2,1,0:T(8,128)(2,1)S(1)}, u32[]{:S(2)}, u32[]{:S(2)}) %collective-permute-start.8) | collective-permute-done | bytes 1048608 | tf_op jit(solution)/shard_map/ppermute | solution.py:297
  124.3 1.5 student.1.student_out_ref
  125.8 24.1 %all-to-all-done.1.terms_ref = bf16[128,32,128]{2,1,0:T(8,128)(2,1)S(1)} async-done(((bf16[128,32,128]{2,1,0:T(8,128)(2,1)}), bf16[128,32,128]{2,1,0:T(8,128)(2,1)S(1)}, u32[]{:S(2)}, u32[]{:S(2)}) %all-to-all-start.1) | async-done | bytes 1048608 | tf_op jit(solution)/shard_map/all_to_all | solution.py:295
  149.9 2.4 %gradient.1 = (bf16[32,128]{1,0:T(8,128)(2,1)}, bf16[32,8192]{1,0:T(8,128)(2,1)S(1)}) custom-call(s32[3]{0:T(128)S(1)} %pad_add_fusion.place_ref, bf16[128,32,128]{2,1,0:T(8,128)(2,1)S(1)} %all-to-all-done.1.terms_ref, f32[32,128]{1,0:T(8,128)S(1)} %student.1.student_out_ref, bf16[8,8,64,128]{3,2,1,0:T(8,128)(2,1)S(1)} %bitcast.15, ...), custom_call_target="tpu_custom_call" | custom-call | flops 67108864 | bytes 3670016 | tf_op jit(solution)/shard_map/gradient/pallas_call | solution.py:234
  152.3 3.2 %collective-permute-start.9 = (bf16[32,8192]{1,0:T(8,128)(2,1)S(1)}, bf16[32,8192]{1,0:T(8,128)(2,1)S(1)}, u32[]{:S(2)}, u32[]{:S(2)}) collective-permute-start(bf16[32,8192]{1,0:T(8,128)(2,1)S(1)} %get-tuple-element.36), channel_id=1, source_target_pairs={{0,1},{1,0},{2,3},{3,2},{4,5},{5,4},{6,7},{7,6},{8,9},{9,8},{10,11... | collective-permute-start | bytes 1572872 | tf_op jit(solution)/shard_map/ppermute | solution.py:303
  155.5 13.1 %collective-permute-done.9 = bf16[32,8192]{1,0:T(8,128)(2,1)S(1)} collective-permute-done((bf16[32,8192]{1,0:T(8,128)(2,1)S(1)}, bf16[32,8192]{1,0:T(8,128)(2,1)S(1)}, u32[]{:S(2)}, u32[]{:S(2)}) %collective-permute-start.9) | collective-permute-done | bytes 524320 | tf_op jit(solution)/shard_map/ppermute | solution.py:303
  (25 shorter events, 5.6 us)
Async XLA Ops:
  0.6 37.2 %copy-start.7 = (bf16[104,4096]{1,0:T(8,128)(2,1)S(1)}, bf16[104,4096]{1,0:T(8,128)(2,1)}, u32[]{:S(2)}) copy-start(bf16[104,4096]{1,0:T(8,128)(2,1)} %param.9) | copy-start | bytes 2555908
  0.6 7.4 %collective-permute-start = (bf16[32,128]{1,0:T(8,128)(2,1)}, bf16[32,128]{1,0:T(8,128)(2,1)S(1)}, u32[]{:S(2)}, u32[]{:S(2)}) collective-permute-start(bf16[32,128]{1,0:T(8,128)(2,1)} %param.6), channel_id=1, source_target_pairs={{0,0},{32,32},{1,256},{33,288},{64,64},{96,96},{65,320},{97,352},{... | collective-permute-start | bytes 24584 | tf_op jit(solution)/shard_map/ppermute | solution.py:268
  2.1 5.9 %collective-permute-start.1 = (bf16[32,128]{1,0:T(8,128)(2,1)}, bf16[32,128]{1,0:T(8,128)(2,1)S(1)}, u32[]{:S(2)}, u32[]{:S(2)}) collective-permute-start(bf16[32,128]{1,0:T(8,128)(2,1)} %param.6), channel_id=1, source_target_pairs={{0,32},{32,0},{1,288},{33,256},{64,96},{96,64},{65,352},{97,320},{... | collective-permute-start | bytes 24584 | tf_op jit(solution)/shard_map/ppermute | solution.py:268
  5.5 5.8 %collective-permute-start.2 = (bf16[32,128]{1,0:T(8,128)(2,1)}, bf16[32,128]{1,0:T(8,128)(2,1)S(1)}, u32[]{:S(2)}, u32[]{:S(2)}) collective-permute-start(bf16[32,128]{1,0:T(8,128)(2,1)} %mine_ref.1), channel_id=1, source_target_pairs={{0,32},{32,0},{1,33},{33,1},{2,34},{34,2},{3,35},{35,3},{4,36},{36... | collective-permute-start | bytes 24584 | tf_op jit(solution)/shard_map/ppermute | solution.py:269
  13.0 52.4 %all-to-all-start = ((bf16[64,64,128]{2,1,0:T(8,128)(2,1)}), bf16[64,64,128]{2,1,0:T(8,128)(2,1)}, u32[]{:S(2)}, u32[]{:S(2)}) async-start(bf16[64,64,128]{2,1,0:T(8,128)(2,1)} %copies.2), calls=%async_computation | async-start | bytes 2097152 | tf_op jit(solution)/shard_map/all_to_all | solution.py:273
  37.9 3.4 %copy-start.3 = (bf16[104,4096]{1,0:T(8,128)(2,1)S(1)}, bf16[104,4096]{1,0:T(8,128)(2,1)}, u32[]{:S(2)}) copy-start(bf16[104,4096]{1,0:T(8,128)(2,1)} %gate_ref.1) | copy-start | bytes 2555908
  37.9 12.2 %collective-permute-start.3 = (bf16[48,4096]{1,0:T(8,128)(2,1)S(1)}, bf16[48,4096]{1,0:T(8,128)(2,1)}, u32[]{:S(2)}, u32[]{:S(2)}) collective-permute-start(bf16[48,4096]{1,0:T(8,128)(2,1)S(1)} %slice.6), channel_id=1, source_target_pairs={{0,1},{1,0},{2,3},{3,2},{4,5},{5,4},{6,7},{7,6},{8,9},{9,8},{10,11... | collective-permute-start | bytes 1179656 | tf_op jit(solution)/shard_map/ppermute | solution.py:272
  41.3 1.2 copy-start.4
  42.5 0.7 copy-start.6
  44.0 1.0 copy-start
  65.5 11.7 %collective-permute-start.4 = (bf16[64,64,128]{2,1,0:T(8,128)(2,1)}, bf16[64,64,128]{2,1,0:T(8,128)(2,1)}, u32[]{:S(2)}, u32[]{:S(2)}) collective-permute-start(bf16[64,64,128]{2,1,0:T(8,128)(2,1)} %all-to-all-done), channel_id=1, source_target_pairs={{0,2},{2,0},{1,3},{3,1},{4,6},{6,4},{5,7},{7,5},{8,10},{10,8},{9,1... | collective-permute-start | bytes 3145736 | tf_op jit(solution)/shard_map/ppermute | solution.py:284
  67.4 37.8 %all-to-all-start.2 = ((bf16[64,64,128]{2,1,0:T(8,128)(2,1)}), bf16[64,64,128]{2,1,0:T(8,128)(2,1)S(1)}, u32[]{:S(2)}, u32[]{:S(2)}) async-start(bf16[64,64,128]{2,1,0:T(8,128)(2,1)} %copy-done), calls=%async_computation.2 | async-start | bytes 2097152 | tf_op jit(solution)/shard_map/all_to_all | solution.py:286
  75.2 16.4 %collective-permute-start.6 = (bf16[56,4096]{1,0:T(8,128)(2,1)S(1)}, bf16[56,4096]{1,0:T(8,128)(2,1)}, u32[]{:S(2)}, u32[]{:S(2)}) collective-permute-start(bf16[56,4096]{1,0:T(8,128)(2,1)S(1)} %slice.7), channel_id=1, source_target_pairs={{0,1},{1,0},{2,3},{3,2},{4,5},{5,4},{6,7},{7,6},{8,9},{9,8},{10,11... | collective-permute-start | bytes 1376264 | tf_op jit(solution)/shard_map/ppermute | solution.py:285
  79.5 15.9 %copy-start.1 = (bf16[104,4096]{0,1:T(8,128)(2,1)S(1)}, bf16[104,4096]{0,1:T(8,128)(2,1)}, u32[]{:S(2)}) copy-start(bf16[104,4096]{0,1:T(8,128)(2,1)} %copy.12) | copy-start | bytes 2555908
  79.5 15.9 %collective-permute-start.5 = (bf16[2,104,128]{2,1,0:T(8,128)(2,1)S(1)}, bf16[2,104,128]{2,1,0:T(8,128)(2,1)S(1)}, u32[]{:S(2)}, u32[]{:S(2)}) collective-permute-start(bf16[2,104,128]{2,1,0:T(8,128)(2,1)S(1)} %get-tuple-element.28), channel_id=1, source_target_pairs={{0,1},{1,0},{2,3},{3,2},{4,5},{5,4},{6,7},{7,6},{8,9},{9,8},{10,11... | collective-permute-start | bytes 159752 | tf_op jit(solution)/shard_map/ppermute | solution.py:290
  95.4 1.2 copy-start.2
  99.3 4.5 %collective-permute-start.7 = (bf16[128,32,128]{2,1,0:T(8,128)(2,1)S(1)}, bf16[128,32,128]{2,1,0:T(8,128)(2,1)S(1)}, u32[]{:S(2)}, u32[]{:S(2)}) collective-permute-start(bf16[128,32,128]{2,1,0:T(8,128)(2,1)S(1)} %bitcast.21), channel_id=1, source_target_pairs={{0,2},{2,0},{1,3},{3,1},{4,6},{6,4},{5,7},{7,5},{8,10},{10,8},{9,1... | collective-permute-start | bytes 3145736 | tf_op jit(solution)/shard_map/ppermute | solution.py:293
  105.2 44.7 %all-to-all-start.1 = ((bf16[128,32,128]{2,1,0:T(8,128)(2,1)}), bf16[128,32,128]{2,1,0:T(8,128)(2,1)S(1)}, u32[]{:S(2)}, u32[]{:S(2)}) async-start(bf16[128,32,128]{2,1,0:T(8,128)(2,1)} %fusion), calls=%async_computation.1 | async-start | bytes 2097152 | tf_op jit(solution)/shard_map/all_to_all | solution.py:295
  118.7 4.6 %collective-permute-start.8 = (bf16[64,64,128]{2,1,0:T(8,128)(2,1)S(1)}, bf16[64,64,128]{2,1,0:T(8,128)(2,1)S(1)}, u32[]{:S(2)}, u32[]{:S(2)}) collective-permute-start(bf16[64,64,128]{2,1,0:T(8,128)(2,1)S(1)} %all-to-all-done.2), channel_id=1, source_target_pairs={{0,2},{2,0},{1,3},{3,1},{4,6},{6,4},{5,7},{7,5},{8,10},{10,8},{9,1... | collective-permute-start | bytes 3145736 | tf_op jit(solution)/shard_map/ppermute | solution.py:297
  123.3 1.0 copy-start.5
  152.3 16.3 %collective-permute-start.9 = (bf16[32,8192]{1,0:T(8,128)(2,1)S(1)}, bf16[32,8192]{1,0:T(8,128)(2,1)S(1)}, u32[]{:S(2)}, u32[]{:S(2)}) collective-permute-start(bf16[32,8192]{1,0:T(8,128)(2,1)S(1)} %get-tuple-element.36), channel_id=1, source_target_pairs={{0,1},{1,0},{2,3},{3,2},{4,5},{5,4},{6,7},{7,6},{8,9},{9,8},{10,11... | collective-permute-start | bytes 1572872 | tf_op jit(solution)/shard_map/ppermute | solution.py:303

commit v9 on v8

--- a/solution.py
+++ b/solution.py
@@ -268,7 +268,7 @@
     held, held_x = (lax.ppermute(teacher_rows, ("y", "x", "dp"), t) for t in (trade, trade_x))
     near_x = lax.ppermute(student_rows, "x", SWAP)
     held, held_x, near_x = lax.optimization_barrier((held, held_x, near_x))
-    units = 48
+    units = 80
     far_low = lax.ppermute(teacher_down[:units], "dp", SWAP)
     teacher_own = spread(copies(place, held, held_x, peers), plane)
     teacher_own, far_low, down_near, student_copies, gate_and_up = lax.optimization_barrier(

time: 170 us -> 164 us (0.965)
  starting transfers between devices: 70.8 us -> 66.3 us
  waiting for transfers between devices: 72.7 us -> 70.2 us
    all_to_all x1, waiting for transfers between devices: 15.3 us -> 8.74 us  [shards(): teacher_own = spread(copies(place, held, held_x, peers), plane)]
    ppermute x1, waiting for transfers between devices: 6.61 us -> 0.42 us  [shards(): far_high = lax.ppermute(teacher_down[units:], 'dp', SWAP)]
    ppermute x1, waiting for transfers between devices: 5.18 us -> 11 us  [shards(): far_low = lax.ppermute(teacher_down[:units], 'dp', SWAP)]
    all_to_all x1, waiting for transfers between devices: 0.01 us -> 5.24 us  [shards(): student_own = spread(student_copies, plane)]
    all_to_all x1, starting transfers between devices: 13.5 us -> 8.25 us  [shards(): terms = spread(chip_sum, CHIPS)]
  transfers between devices with their start and end apart: 13 -> 13, of which waited for: 8 -> 9; matrix products, arithmetic and copies ran while one was open for 4% -> 5% of each run, Pallas kernels for 5% -> 5%
where the time goes in v9:
time: 164 us; the launch traced here: 163 us
  waiting for transfers between devices  70.2 us (43%)
  starting transfers between devices  66.3 us (40%)
  Pallas kernels  11.9 us (7%)
  local copies, waits for them, and re-layouts  11.5 us (7%)
  other arithmetic  2.3 us (1%)
    all_to_all x1, starting transfers between devices, shards(): teacher_own = spread(copies(place, held, held_x, peers), plane)  24.8 us
    all_to_all x1, waiting for transfers between devices, shards(): terms = spread(chip_sum, CHIPS)  24.1 us
    ppermute x1, waiting for transfers between devices, shards(): grad_projector = grad_local + lax.ppermute(grad_local, 'dp', SWAP)  12.3 us
    ppermute x1, waiting for transfers between devices, shards(): far_low = lax.ppermute(teacher_down[:units], 'dp', SWAP)  11 us
    all_to_all x1, waiting for transfers between devices, shards(): teacher_own = spread(copies(place, held, held_x, peers), plane)  8.74 us
    all_to_all x1, starting transfers between devices, shards(): terms = spread(chip_sum, CHIPS)  8.25 us
    all_to_all x1, starting transfers between devices, shards(): student_own = spread(student_copies, plane)  6.72 us
    unnamed x17, local copies, waits for them, and re-layouts  6.01 us
  transfers between devices with their start and end apart: 13, of which 9 were waited for; matrix products, arithmetic and copies ran while one was open for 5% of the time, Pallas kernels for 5%

profile of v9, /device:TPU:8, one launch (start us, length us, event | category | flops | bytes accessed | tf_op | source)
XLA Modules:
  0.0 163.0 jit_solution(14272179768863355036)
XLA Ops:
  0.6 1.5 collective-permute-start
  2.1 3.4 %collective-permute-start.1 = (bf16[32,128]{1,0:T(8,128)(2,1)}, bf16[32,128]{1,0:T(8,128)(2,1)S(1)}, u32[]{:S(2)}, u32[]{:S(2)}) collective-permute-start(bf16[32,128]{1,0:T(8,128)(2,1)} %param.6), channel_id=1, source_target_pairs={{0,32},{32,0},{1,288},{33,256},{64,96},{96,64},{65,352},{97,320},{... | collective-permute-start | bytes 24584 | tf_op jit(solution)/shard_map/ppermute | solution.py:268
  5.5 2.4 %collective-permute-start.2 = (bf16[32,128]{1,0:T(8,128)(2,1)}, bf16[32,128]{1,0:T(8,128)(2,1)S(1)}, u32[]{:S(2)}, u32[]{:S(2)}) collective-permute-start(bf16[32,128]{1,0:T(8,128)(2,1)} %mine_ref.1), channel_id=1, source_target_pairs={{0,32},{32,0},{1,33},{33,1},{2,34},{34,2},{3,35},{35,3},{4,36},{36... | collective-permute-start | bytes 24584 | tf_op jit(solution)/shard_map/ppermute | solution.py:269
  8.1 3.2 %collective-permute-done.2.next_ref = bf16[32,128]{1,0:T(8,128)(2,1)S(1)} collective-permute-done((bf16[32,128]{1,0:T(8,128)(2,1)}, bf16[32,128]{1,0:T(8,128)(2,1)S(1)}, u32[]{:S(2)}, u32[]{:S(2)}) %collective-permute-start.2) | collective-permute-done | bytes 8224 | tf_op jit(solution)/shard_map/ppermute | solution.py:269
  11.3 1.8 %copies.2 = bf16[64,64,128]{2,1,0:T(8,128)(2,1)} custom-call(s32[3]{0:T(128)S(1)} %pad_add_fusion.place_ref, bf16[32,128]{1,0:T(8,128)(2,1)S(1)} %collective-permute-done.mine_ref, bf16[32,128]{1,0:T(8,128)(2,1)S(1)} %collective-permute-done.1.next_ref), custom_call_target="tpu_custom_call" | custom-call | bytes 1048576 | tf_op jit(solution)/shard_map/copies/pallas_call | solution.py:39
  13.0 24.8 %all-to-all-start = ((bf16[64,64,128]{2,1,0:T(8,128)(2,1)}), bf16[64,64,128]{2,1,0:T(8,128)(2,1)}, u32[]{:S(2)}, u32[]{:S(2)}) async-start(bf16[64,64,128]{2,1,0:T(8,128)(2,1)} %copies.2), calls=%async_computation | async-start | bytes 2097152 | tf_op jit(solution)/shard_map/all_to_all | solution.py:273
  38.8 1.9 %collective-permute-start.3 = (bf16[80,4096]{1,0:T(8,128)(2,1)}, bf16[80,4096]{1,0:T(8,128)(2,1)}, u32[]{:S(2)}, u32[]{:S(2)}) collective-permute-start(bf16[80,4096]{1,0:T(8,128)(2,1)} %slice.6), channel_id=1, source_target_pairs={{0,1},{1,0},{2,3},{3,2},{4,5},{5,4},{6,7},{7,6},{8,9},{9,8},{10,11... | collective-permute-start | bytes 1966088 | tf_op jit(solution)/shard_map/ppermute | solution.py:272
  40.7 1.3 copy.12
  42.0 1.2 copy-done.4
  45.7 11.0 %collective-permute-done.3 = bf16[80,4096]{1,0:T(8,128)(2,1)} collective-permute-done((bf16[80,4096]{1,0:T(8,128)(2,1)}, bf16[80,4096]{1,0:T(8,128)(2,1)}, u32[]{:S(2)}, u32[]{:S(2)}) %collective-permute-start.3) | collective-permute-done | bytes 655392 | tf_op jit(solution)/shard_map/ppermute | solution.py:272
  56.7 8.7 %all-to-all-done = bf16[64,64,128]{2,1,0:T(8,128)(2,1)} async-done(((bf16[64,64,128]{2,1,0:T(8,128)(2,1)}), bf16[64,64,128]{2,1,0:T(8,128)(2,1)}, u32[]{:S(2)}, u32[]{:S(2)}) %all-to-all-start) | async-done | bytes 1048608 | tf_op jit(solution)/shard_map/all_to_all | solution.py:273
  65.5 1.9 %collective-permute-start.4 = (bf16[64,64,128]{2,1,0:T(8,128)(2,1)}, bf16[64,64,128]{2,1,0:T(8,128)(2,1)}, u32[]{:S(2)}, u32[]{:S(2)}) collective-permute-start(bf16[64,64,128]{2,1,0:T(8,128)(2,1)} %all-to-all-done), channel_id=1, source_target_pairs={{0,2},{2,0},{1,3},{3,1},{4,6},{6,4},{5,7},{7,5},{8,10},{10,8},{9,1... | collective-permute-start | bytes 3145736 | tf_op jit(solution)/shard_map/ppermute | solution.py:284
  67.4 6.7 %all-to-all-start.2 = ((bf16[64,64,128]{2,1,0:T(8,128)(2,1)}), bf16[64,64,128]{2,1,0:T(8,128)(2,1)S(1)}, u32[]{:S(2)}, u32[]{:S(2)}) async-start(bf16[64,64,128]{2,1,0:T(8,128)(2,1)} %copy-done), calls=%async_computation.2 | async-start | bytes 2097152 | tf_op jit(solution)/shard_map/all_to_all | solution.py:286
  75.0 2.0 %collective-permute-start.6 = (bf16[24,4096]{1,0:T(8,128)(2,1)S(1)}, bf16[24,4096]{1,0:T(8,128)(2,1)}, u32[]{:S(2)}, u32[]{:S(2)}) collective-permute-start(bf16[24,4096]{1,0:T(8,128)(2,1)S(1)} %slice.7), channel_id=1, source_target_pairs={{0,1},{1,0},{2,3},{3,2},{4,5},{5,4},{6,7},{7,6},{8,9},{9,8},{10,11... | collective-permute-start | bytes 589832 | tf_op jit(solution)/shard_map/ppermute | solution.py:285
  77.1 2.3 %gate_up.1 = (f32[2,104,128]{2,1,0:T(8,128)S(1)}, bf16[2,104,128]{2,1,0:T(8,128)(2,1)S(1)}) custom-call(s32[3]{0:T(128)S(1)} %pad_add_fusion.place_ref, bf16[2,4,8,64,128]{4,3,2,1,0:T(8,128)(2,1)} %bitcast.4.own_ref, bf16[2,4,8,64,128]{4,3,2,1,0:T(8,128)(2,1)} %bitcast.5.other_ref, bf16[2,104,4096]{2,1,0:T(8,128)(2,1)S(1)} %pack.1.weight_ref), custom_call_target="tpu_custom_call" | custom-call | flops 436207616 | bytes 3801088 | tf_op jit(solution)/shard_map/gate_up/pallas_call | solution.py:108
  79.4 5.5 %collective-permute-start.5 = (bf16[2,104,128]{2,1,0:T(8,128)(2,1)S(1)}, bf16[2,104,128]{2,1,0:T(8,128)(2,1)S(1)}, u32[]{:S(2)}, u32[]{:S(2)}) collective-permute-start(bf16[2,104,128]{2,1,0:T(8,128)(2,1)S(1)} %get-tuple-element.28), channel_id=1, source_target_pairs={{0,1},{1,0},{2,3},{3,2},{4,5},{5,4},{6,7},{7,6},{8,9},{9,8},{10,11... | collective-permute-start | bytes 159752 | tf_op jit(solution)/shard_map/ppermute | solution.py:290
  85.3 1.4 copy.14
  86.7 2.2 %copy.13 = bf16[80,4096]{0,1:T(8,128)(2,1)} copy(bf16[80,4096]{1,0:T(8,128)(2,1)} %collective-permute-done.3) | data formatting | bytes 1310720 | tf_op jit(solution)/shard_map/optimization_barrier | solution.py:289
  88.9 1.2 copy-done.2
  90.1 2.7 %down.1 = (bf16[104,128]{1,0:T(8,128)(2,1)}, bf16[2,64,32,128]{3,2,1,0:T(8,128)(2,1)S(1)}, bf16[2,64,32,128]{3,2,1,0:T(8,128)(2,1)S(1)}) custom-call(s32[3]{0:T(128)S(1)} %pad_add_fusion.place_ref, f32[2,104,128]{2,1,0:T(8,128)S(1)} %get-tuple-element.25.keep_ref, bf16[2,104,128]{2,1,0:T(8,128)(2,1)S(1)} %collective-permute-done.5.got_ref, ...), custom_call_target="tpu_custom_call" | custom-call | tf_op jit(solution)/shard_map/down/pallas_call | solution.py:158
  92.8 1.9 %collective-permute-start.7 = (bf16[128,32,128]{2,1,0:T(8,128)(2,1)S(1)}, bf16[128,32,128]{2,1,0:T(8,128)(2,1)S(1)}, u32[]{:S(2)}, u32[]{:S(2)}) collective-permute-start(bf16[128,32,128]{2,1,0:T(8,128)(2,1)S(1)} %bitcast.21), channel_id=1, source_target_pairs={{0,2},{2,0},{1,3},{3,1},{4,6},{6,4},{5,7},{7,5},{8,10},{10,8},{9,1... | collective-permute-start | bytes 3145736 | tf_op jit(solution)/shard_map/ppermute | solution.py:293
  94.8 2.6 %collective-permute-done.7 = bf16[128,32,128]{2,1,0:T(8,128)(2,1)S(1)} collective-permute-done((bf16[128,32,128]{2,1,0:T(8,128)(2,1)S(1)}, bf16[128,32,128]{2,1,0:T(8,128)(2,1)S(1)}, u32[]{:S(2)}, u32[]{:S(2)}) %collective-permute-start.7) | collective-permute-done | bytes 1048608 | tf_op jit(solution)/shard_map/ppermute | solution.py:293
  97.4 1.3 fusion
  98.7 5.2 %all-to-all-done.2 = bf16[64,64,128]{2,1,0:T(8,128)(2,1)S(1)} async-done(((bf16[64,64,128]{2,1,0:T(8,128)(2,1)}), bf16[64,64,128]{2,1,0:T(8,128)(2,1)S(1)}, u32[]{:S(2)}, u32[]{:S(2)}) %all-to-all-start.2) | async-done | bytes 1048608 | tf_op jit(solution)/shard_map/all_to_all | solution.py:286
  103.9 8.3 %all-to-all-start.1 = ((bf16[128,32,128]{2,1,0:T(8,128)(2,1)}), bf16[128,32,128]{2,1,0:T(8,128)(2,1)S(1)}, u32[]{:S(2)}, u32[]{:S(2)}) async-start(bf16[128,32,128]{2,1,0:T(8,128)(2,1)} %fusion), calls=%async_computation.1 | async-start | bytes 2097152 | tf_op jit(solution)/shard_map/all_to_all | solution.py:295
  112.2 1.9 %collective-permute-start.8 = (bf16[64,64,128]{2,1,0:T(8,128)(2,1)S(1)}, bf16[64,64,128]{2,1,0:T(8,128)(2,1)S(1)}, u32[]{:S(2)}, u32[]{:S(2)}) collective-permute-start(bf16[64,64,128]{2,1,0:T(8,128)(2,1)S(1)} %all-to-all-done.2), channel_id=1, source_target_pairs={{0,2},{2,0},{1,3},{3,1},{4,6},{6,4},{5,7},{7,5},{8,10},{10,8},{9,1... | collective-permute-start | bytes 3145736 | tf_op jit(solution)/shard_map/ppermute | solution.py:297
  114.1 2.6 %collective-permute-done.8 = bf16[64,64,128]{2,1,0:T(8,128)(2,1)S(1)} collective-permute-done((bf16[64,64,128]{2,1,0:T(8,128)(2,1)S(1)}, bf16[64,64,128]{2,1,0:T(8,128)(2,1)S(1)}, u32[]{:S(2)}, u32[]{:S(2)}) %collective-permute-start.8) | collective-permute-done | bytes 1048608 | tf_op jit(solution)/shard_map/ppermute | solution.py:297
  117.8 1.5 student.1.student_out_ref
  119.3 24.1 %all-to-all-done.1.terms_ref = bf16[128,32,128]{2,1,0:T(8,128)(2,1)S(1)} async-done(((bf16[128,32,128]{2,1,0:T(8,128)(2,1)}), bf16[128,32,128]{2,1,0:T(8,128)(2,1)S(1)}, u32[]{:S(2)}, u32[]{:S(2)}) %all-to-all-start.1) | async-done | bytes 1048608 | tf_op jit(solution)/shard_map/all_to_all | solution.py:295
  143.4 2.4 %gradient.1 = (bf16[32,128]{1,0:T(8,128)(2,1)}, bf16[32,8192]{1,0:T(8,128)(2,1)S(1)}) custom-call(s32[3]{0:T(128)S(1)} %pad_add_fusion.place_ref, bf16[128,32,128]{2,1,0:T(8,128)(2,1)S(1)} %all-to-all-done.1.terms_ref, f32[32,128]{1,0:T(8,128)S(1)} %student.1.student_out_ref, bf16[8,8,64,128]{3,2,1,0:T(8,128)(2,1)S(1)} %bitcast.15, ...), custom_call_target="tpu_custom_call" | custom-call | flops 67108864 | bytes 3670016 | tf_op jit(solution)/shard_map/gradient/pallas_call | solution.py:234
  145.8 4.0 %collective-permute-start.9 = (bf16[32,8192]{1,0:T(8,128)(2,1)S(1)}, bf16[32,8192]{1,0:T(8,128)(2,1)S(1)}, u32[]{:S(2)}, u32[]{:S(2)}) collective-permute-start(bf16[32,8192]{1,0:T(8,128)(2,1)S(1)} %get-tuple-element.36), channel_id=1, source_target_pairs={{0,1},{1,0},{2,3},{3,2},{4,5},{5,4},{6,7},{7,6},{8,9},{9,8},{10,11... | collective-permute-start | bytes 1572872 | tf_op jit(solution)/shard_map/ppermute | solution.py:303
  149.8 12.3 %collective-permute-done.9 = bf16[32,8192]{1,0:T(8,128)(2,1)S(1)} collective-permute-done((bf16[32,8192]{1,0:T(8,128)(2,1)S(1)}, bf16[32,8192]{1,0:T(8,128)(2,1)S(1)}, u32[]{:S(2)}, u32[]{:S(2)}) %collective-permute-start.9) | collective-permute-done | bytes 524320 | tf_op jit(solution)/shard_map/ppermute | solution.py:303
  (25 shorter events, 6.8 us)
Async XLA Ops:
  0.6 37.2 %copy-start.7 = (bf16[104,4096]{1,0:T(8,128)(2,1)S(1)}, bf16[104,4096]{1,0:T(8,128)(2,1)}, u32[]{:S(2)}) copy-start(bf16[104,4096]{1,0:T(8,128)(2,1)} %param.9) | copy-start | bytes 2555908
  0.6 7.4 %collective-permute-start = (bf16[32,128]{1,0:T(8,128)(2,1)}, bf16[32,128]{1,0:T(8,128)(2,1)S(1)}, u32[]{:S(2)}, u32[]{:S(2)}) collective-permute-start(bf16[32,128]{1,0:T(8,128)(2,1)} %param.6), channel_id=1, source_target_pairs={{0,0},{32,32},{1,256},{33,288},{64,64},{96,96},{65,320},{97,352},{... | collective-permute-start | bytes 24584 | tf_op jit(solution)/shard_map/ppermute | solution.py:268
  2.1 5.9 %collective-permute-start.1 = (bf16[32,128]{1,0:T(8,128)(2,1)}, bf16[32,128]{1,0:T(8,128)(2,1)S(1)}, u32[]{:S(2)}, u32[]{:S(2)}) collective-permute-start(bf16[32,128]{1,0:T(8,128)(2,1)} %param.6), channel_id=1, source_target_pairs={{0,32},{32,0},{1,288},{33,256},{64,96},{96,64},{65,352},{97,320},{... | collective-permute-start | bytes 24584 | tf_op jit(solution)/shard_map/ppermute | solution.py:268
  5.5 5.8 %collective-permute-start.2 = (bf16[32,128]{1,0:T(8,128)(2,1)}, bf16[32,128]{1,0:T(8,128)(2,1)S(1)}, u32[]{:S(2)}, u32[]{:S(2)}) collective-permute-start(bf16[32,128]{1,0:T(8,128)(2,1)} %mine_ref.1), channel_id=1, source_target_pairs={{0,32},{32,0},{1,33},{33,1},{2,34},{34,2},{3,35},{35,3},{4,36},{36... | collective-permute-start | bytes 24584 | tf_op jit(solution)/shard_map/ppermute | solution.py:269
  13.0 52.4 %all-to-all-start = ((bf16[64,64,128]{2,1,0:T(8,128)(2,1)}), bf16[64,64,128]{2,1,0:T(8,128)(2,1)}, u32[]{:S(2)}, u32[]{:S(2)}) async-start(bf16[64,64,128]{2,1,0:T(8,128)(2,1)} %copies.2), calls=%async_computation | async-start | bytes 2097152 | tf_op jit(solution)/shard_map/all_to_all | solution.py:273
  37.9 4.2 %copy-start.3 = (bf16[104,4096]{1,0:T(8,128)(2,1)S(1)}, bf16[104,4096]{1,0:T(8,128)(2,1)}, u32[]{:S(2)}) copy-start(bf16[104,4096]{1,0:T(8,128)(2,1)} %gate_ref.1) | copy-start | bytes 2555908
  38.8 17.9 %collective-permute-start.3 = (bf16[80,4096]{1,0:T(8,128)(2,1)}, bf16[80,4096]{1,0:T(8,128)(2,1)}, u32[]{:S(2)}, u32[]{:S(2)}) collective-permute-start(bf16[80,4096]{1,0:T(8,128)(2,1)} %slice.6), channel_id=1, source_target_pairs={{0,1},{1,0},{2,3},{3,2},{4,5},{5,4},{6,7},{7,6},{8,9},{9,8},{10,11... | collective-permute-start | bytes 1966088 | tf_op jit(solution)/shard_map/ppermute | solution.py:272
  42.0 1.2 copy-start.4
  43.2 0.7 copy-start.6
  44.7 1.0 copy-start
  65.5 11.6 %collective-permute-start.4 = (bf16[64,64,128]{2,1,0:T(8,128)(2,1)}, bf16[64,64,128]{2,1,0:T(8,128)(2,1)}, u32[]{:S(2)}, u32[]{:S(2)}) collective-permute-start(bf16[64,64,128]{2,1,0:T(8,128)(2,1)} %all-to-all-done), channel_id=1, source_target_pairs={{0,2},{2,0},{1,3},{3,1},{4,6},{6,4},{5,7},{7,5},{8,10},{10,8},{9,1... | collective-permute-start | bytes 3145736 | tf_op jit(solution)/shard_map/ppermute | solution.py:284
  67.4 36.6 %all-to-all-start.2 = ((bf16[64,64,128]{2,1,0:T(8,128)(2,1)}), bf16[64,64,128]{2,1,0:T(8,128)(2,1)S(1)}, u32[]{:S(2)}, u32[]{:S(2)}) async-start(bf16[64,64,128]{2,1,0:T(8,128)(2,1)} %copy-done), calls=%async_computation.2 | async-start | bytes 2097152 | tf_op jit(solution)/shard_map/all_to_all | solution.py:286
  75.0 10.2 %collective-permute-start.6 = (bf16[24,4096]{1,0:T(8,128)(2,1)S(1)}, bf16[24,4096]{1,0:T(8,128)(2,1)}, u32[]{:S(2)}, u32[]{:S(2)}) collective-permute-start(bf16[24,4096]{1,0:T(8,128)(2,1)S(1)} %slice.7), channel_id=1, source_target_pairs={{0,1},{1,0},{2,3},{3,2},{4,5},{5,4},{6,7},{7,6},{8,9},{9,8},{10,11... | collective-permute-start | bytes 589832 | tf_op jit(solution)/shard_map/ppermute | solution.py:285
  79.4 9.5 %copy-start.1 = (bf16[104,4096]{0,1:T(8,128)(2,1)S(1)}, bf16[104,4096]{0,1:T(8,128)(2,1)}, u32[]{:S(2)}) copy-start(bf16[104,4096]{0,1:T(8,128)(2,1)} %copy.12) | copy-start | bytes 2555908
  79.4 9.5 %collective-permute-start.5 = (bf16[2,104,128]{2,1,0:T(8,128)(2,1)S(1)}, bf16[2,104,128]{2,1,0:T(8,128)(2,1)S(1)}, u32[]{:S(2)}, u32[]{:S(2)}) collective-permute-start(bf16[2,104,128]{2,1,0:T(8,128)(2,1)S(1)} %get-tuple-element.28), channel_id=1, source_target_pairs={{0,1},{1,0},{2,3},{3,2},{4,5},{5,4},{6,7},{7,6},{8,9},{9,8},{10,11... | collective-permute-start | bytes 159752 | tf_op jit(solution)/shard_map/ppermute | solution.py:290
  88.9 1.2 copy-start.2
  92.8 4.5 %collective-permute-start.7 = (bf16[128,32,128]{2,1,0:T(8,128)(2,1)S(1)}, bf16[128,32,128]{2,1,0:T(8,128)(2,1)S(1)}, u32[]{:S(2)}, u32[]{:S(2)}) collective-permute-start(bf16[128,32,128]{2,1,0:T(8,128)(2,1)S(1)} %bitcast.21), channel_id=1, source_target_pairs={{0,2},{2,0},{1,3},{3,1},{4,6},{6,4},{5,7},{7,5},{8,10},{10,8},{9,1... | collective-permute-start | bytes 3145736 | tf_op jit(solution)/shard_map/ppermute | solution.py:293
  103.9 39.4 %all-to-all-start.1 = ((bf16[128,32,128]{2,1,0:T(8,128)(2,1)}), bf16[128,32,128]{2,1,0:T(8,128)(2,1)S(1)}, u32[]{:S(2)}, u32[]{:S(2)}) async-start(bf16[128,32,128]{2,1,0:T(8,128)(2,1)} %fusion), calls=%async_computation.1 | async-start | bytes 2097152 | tf_op jit(solution)/shard_map/all_to_all | solution.py:295
  112.2 4.6 %collective-permute-start.8 = (bf16[64,64,128]{2,1,0:T(8,128)(2,1)S(1)}, bf16[64,64,128]{2,1,0:T(8,128)(2,1)S(1)}, u32[]{:S(2)}, u32[]{:S(2)}) collective-permute-start(bf16[64,64,128]{2,1,0:T(8,128)(2,1)S(1)} %all-to-all-done.2), channel_id=1, source_target_pairs={{0,2},{2,0},{1,3},{3,1},{4,6},{6,4},{5,7},{7,5},{8,10},{10,8},{9,1... | collective-permute-start | bytes 3145736 | tf_op jit(solution)/shard_map/ppermute | solution.py:297
  116.7 1.0 copy-start.5
  145.8 16.3 %collective-permute-start.9 = (bf16[32,8192]{1,0:T(8,128)(2,1)S(1)}, bf16[32,8192]{1,0:T(8,128)(2,1)S(1)}, u32[]{:S(2)}, u32[]{:S(2)}) collective-permute-start(bf16[32,8192]{1,0:T(8,128)(2,1)S(1)} %get-tuple-element.36), channel_id=1, source_target_pairs={{0,1},{1,0},{2,3},{3,2},{4,5},{5,4},{6,7},{7,6},{8,9},{9,8},{10,11... | collective-permute-start | bytes 1572872 | tf_op jit(solution)/shard_map/ppermute | solution.py:303
